TPU v7x, 32 devices: a whole 2x2x4 slice. The times are simulated.
32 devices in a mesh: fsdp: 4 (over y, x), ctx: 4 (over z), tp: 2 (over core).
Axes of the slice: x: 2, y: 2, z: 4, core: 2. Of those that a mesh axis runs over, the one named last changes fastest.
Arguments:
- tokens: bfloat16 [4, 1024, 1536], P('fsdp', 'ctx'), may hold values from -6 to 6
- attn_norm: float32 [1536], replicated, may hold values from 0.5 to 1.5
- attention_params: bfloat16 [1536, 2, 1792], P('fsdp', 'tp')
- ffn_norm: float32 [1536], replicated, may hold values from 0.5 to 1.5
- expert_weights: bfloat16 [1536, 8, 3, 768], P('fsdp', None, None, 'tp'), may hold values from -0.15625 to 0.15625
- gate_values: float32 [4, 1024, 4], P('fsdp', 'ctx'), may hold values from 0.5 to 1.5
- routes: int32 [4, 1024, 4], P('fsdp', 'ctx'), may hold values from 0 to 7, all different within a row
- slot_order: int32 [4, 1024], P('fsdp', 'ctx'), may hold values from 0 to 255, as said below
- cotangent: bfloat16 [4, 1024, 1536], P('fsdp', 'ctx'), may hold values from -6 to 6
Outputs:
- layer_out: bfloat16 [4, 1024, 1536], P('fsdp', 'ctx')
- tokens_grad: bfloat16 [4, 1024, 1536], P('fsdp', 'ctx')
- attn_weights_grad: float32 [1536, 2, 1792], P('fsdp', 'tp')
- expert_weights_grad: float32 [1536, 8, 3, 768], P('fsdp', None, None, 'tp')
- attn_norm_grad: float32 [1536], replicated
- ffn_norm_grad: float32 [1536], replicated
- gate_grad: float32 [4, 1024, 4], P('fsdp', 'ctx')
Inputs may be any that keep to these rules, and one draw needn't show every extreme that they name: `slot_order`: within each group of 1 sequence and one block of 256 positions the values are a permutation of the group's ranks, read with sequences first and positions second. `routes`: the 4 experts of a token are different.
All inputs are finite; a program needn't handle non-finite values.
Results may differ from a plain program's by a relative error of at most 0.018.
Values may be sent and summed in bfloat16 or wider, within the bound.
A program may use at most 256 MiB of HBM per device.

v0:
```python
import jax
import jax.numpy as jnp
from jax import lax
from jax.sharding import PartitionSpec as P

HEAD_DIM = 128
TOP = 4
EXPERTS = 8
QUERY_PER_GROUP = 6
CAP = 160


eps = 1e-06
theta_base = 1000000.0


def angle_tables(positions):
    frequency = theta_base ** (-(jnp.arange(HEAD_DIM // 2, dtype=jnp.float32) * 2.0) / HEAD_DIM)
    angles = positions.astype(jnp.float32)[:, None] * frequency[None, :]
    return (jnp.cos(angles), jnp.sin(angles))


def rotate(source, cosine_table, sine_table):
    half_size = source.shape[-1] // 2
    front_half = source[..., :half_size]
    back_half = source[..., half_size:]
    return jnp.concatenate(
        [
            front_half * cosine_table - back_half * sine_table,
            back_half * cosine_table + front_half * sine_table,
        ],
        axis=-1,
    )


def norm_back(source, inv_rms, gain_vec, upstream):
    scaled = upstream * gain_vec
    inner_sum = jnp.mean(scaled * source, axis=-1, keepdims=True)
    d_source = inv_rms * scaled - source * inv_rms * inv_rms * inv_rms * inner_sum
    return (d_source, jnp.sum(upstream * source * inv_rms, axis=0))


def slot_tables(route_rows, rank_rows):
    tok_count = route_rows.shape[0]
    inverse = (
        jnp.zeros((tok_count,), jnp.int32).at[rank_rows].set(jnp.arange(tok_count, dtype=jnp.int32))
    )
    ranked = route_rows[inverse].reshape(-1)
    onehot = (ranked[:, None] == jnp.arange(EXPERTS, dtype=jnp.int32)[None, :]).astype(jnp.int32)
    before = jnp.cumsum(onehot, axis=0) - onehot
    slot_ranked = jnp.sum(before * onehot, axis=1).reshape(tok_count, TOP)
    slots = slot_ranked[rank_rows]
    kept_pair = slots < CAP
    pair_slot = jnp.where(kept_pair, route_rows * CAP + slots, EXPERTS * CAP)
    owners = jnp.broadcast_to(jnp.arange(tok_count, dtype=jnp.int32)[:, None], (tok_count, TOP))
    slot_token = (
        jnp.full((EXPERTS * CAP,), tok_count, jnp.int32)
        .at[pair_slot.reshape(-1)]
        .set(owners.reshape(-1), mode="drop")
    )
    return (kept_pair, pair_slot, slot_token)


def attend_forward(queries, key_rows, value_rows, allowed):
    scores = jnp.einsum(
        "qhgd,khd->hgqk", queries, key_rows, preferred_element_type=jnp.float32
    ) * HEAD_DIM ** (-0.5)
    scores = jnp.where(allowed, scores, -1e30)
    row_max = jnp.max(scores, axis=-1, keepdims=True)
    expd = jnp.exp(scores - row_max)
    row_total = jnp.sum(expd, axis=-1, keepdims=True)
    attn_probs = (expd / row_total).astype(jnp.bfloat16)
    mixed_heads = jnp.einsum(
        "hgqk,khd->qhgd", attn_probs, value_rows, preferred_element_type=jnp.float32
    )
    return (mixed_heads.astype(jnp.bfloat16), row_max + jnp.log(row_total))


def attend_backward(queries, key_rows, value_rows, allowed, log_total, d_mixed):
    scores = jnp.einsum(
        "qhgd,khd->hgqk", queries, key_rows, preferred_element_type=jnp.float32
    ) * HEAD_DIM ** (-0.5)
    scores = jnp.where(allowed, scores, -1e30)
    attn_probs = jnp.exp(scores - log_total)
    low_probs = attn_probs.astype(jnp.bfloat16)
    d_probs = jnp.einsum("qhgd,khd->hgqk", d_mixed, value_rows, preferred_element_type=jnp.float32)
    inner_sum = jnp.sum(attn_probs * d_probs, axis=-1, keepdims=True)
    d_scores = (attn_probs * (d_probs - inner_sum)).astype(jnp.bfloat16)
    d_queries = jnp.einsum(
        "hgqk,khd->qhgd", d_scores, key_rows, preferred_element_type=jnp.float32
    ) * HEAD_DIM ** (-0.5)
    d_keys = jnp.einsum(
        "hgqk,qhgd->khd", d_scores, queries, preferred_element_type=jnp.float32
    ) * HEAD_DIM ** (-0.5)
    d_values = jnp.einsum("hgqk,qhgd->khd", low_probs, d_mixed, preferred_element_type=jnp.float32)
    return (d_queries, d_keys, d_values)


def body(
    tokens,
    attn_norm,
    attention_params,
    ffn_norm,
    expert_weights,
    gate_values,
    routes,
    slot_order,
    cotangent,
):
    sequence_count, block_len, model_width = tokens.shape
    tok_count = sequence_count * block_len
    kv_loc = attention_params.shape[1]
    input_columns = (QUERY_PER_GROUP + 2) * HEAD_DIM
    ctx_size = lax.axis_size("ctx")
    ctx_place = lax.axis_index("ctx")
    sequence_length = block_len * ctx_size
    whole_attn, whole_expert = (
        lax.all_gather(attention_params, "fsdp", axis=0, tiled=True),
        lax.all_gather(expert_weights, "fsdp", axis=0, tiled=True),
    )
    positions = ctx_place * block_len + jnp.arange(block_len, dtype=jnp.int32)
    cosine_table, sine_table = angle_tables(positions)
    cosine_table = jnp.tile(cosine_table, (sequence_count, 1))
    sine_table = jnp.tile(sine_table, (sequence_count, 1))
    cos_four = cosine_table[:, None, None, :]
    sin_four = sine_table[:, None, None, :]
    cos_three = cosine_table[:, None, :]
    sin_three = sine_table[:, None, :]
    allowed = (jnp.arange(sequence_length, dtype=jnp.int32) // block_len <= ctx_place)[
        None, None, None, :
    ]
    tok_float = tokens.reshape(tok_count, model_width).astype(jnp.float32)
    inv_one = lax.rsqrt(jnp.mean(tok_float * tok_float, axis=-1, keepdims=True) + eps)
    first_normed = (tok_float * inv_one * attn_norm).astype(jnp.bfloat16)
    projected_rows = jnp.einsum(
        "td,dhc->thc",
        first_normed,
        whole_attn[:, :, :input_columns],
        preferred_element_type=jnp.float32,
    ).reshape(tok_count, kv_loc, QUERY_PER_GROUP + 2, HEAD_DIM)
    queries = rotate(projected_rows[:, :, :QUERY_PER_GROUP], cos_four, sin_four).astype(
        jnp.bfloat16
    )
    key_rows = rotate(projected_rows[:, :, QUERY_PER_GROUP], cos_three, sin_three).astype(
        jnp.bfloat16
    )
    value_rows = projected_rows[:, :, QUERY_PER_GROUP + 1].astype(jnp.bfloat16)
    key_all, value_all = (
        lax.all_gather(
            key_rows.reshape(sequence_count, block_len, kv_loc, HEAD_DIM), "ctx", axis=1, tiled=True
        ),
        lax.all_gather(
            value_rows.reshape(sequence_count, block_len, kv_loc, HEAD_DIM),
            "ctx",
            axis=1,
            tiled=True,
        ),
    )
    query_seq = queries.reshape(sequence_count, block_len, kv_loc, QUERY_PER_GROUP, HEAD_DIM)
    mixed_heads, log_total = lax.map(
        lambda item_args: attend_forward(item_args[0], item_args[1], item_args[2], allowed),
        (query_seq, key_all, value_all),
    )
    mixed_flat = mixed_heads.reshape(tok_count, kv_loc, QUERY_PER_GROUP * HEAD_DIM)
    attn_part = jnp.einsum(
        "thc,dhc->td",
        mixed_flat,
        whole_attn[:, :, input_columns:],
        preferred_element_type=jnp.float32,
    )
    attn_sum = lax.psum(attn_part, "tp")
    residual = tok_float + attn_sum
    inv_two = lax.rsqrt(jnp.mean(residual * residual, axis=-1, keepdims=True) + eps)
    normed_two = (residual * inv_two * ffn_norm).astype(jnp.bfloat16)
    kept_pair, pair_slot, slot_token = slot_tables(
        routes.reshape(tok_count, TOP), slot_order.reshape(tok_count)
    )
    kept_float = kept_pair.astype(jnp.float32)
    gate_kept = gate_values.reshape(tok_count, TOP) * kept_float
    slot_gate = (
        jnp.zeros((EXPERTS * CAP,), jnp.float32)
        .at[pair_slot.reshape(-1)]
        .set(gate_kept.reshape(-1), mode="drop")
    )
    padded = jnp.concatenate([normed_two, jnp.zeros((1, model_width), jnp.bfloat16)], axis=0)
    inputs = padded[slot_token].reshape(EXPERTS, CAP, model_width)
    gate_act = jnp.einsum(
        "ecd,deh->ech", inputs, whole_expert[:, :, 0], preferred_element_type=jnp.float32
    )
    up_act = jnp.einsum(
        "ecd,deh->ech", inputs, whole_expert[:, :, 1], preferred_element_type=jnp.float32
    )
    gate_sigmoid = jax.nn.sigmoid(gate_act)
    active = gate_act * gate_sigmoid
    hidden = (active * up_act).astype(jnp.bfloat16)
    expert_out = jnp.einsum(
        "ech,deh->ecd", hidden, whole_expert[:, :, 2], preferred_element_type=jnp.float32
    )
    out_pad = jnp.concatenate(
        [expert_out.reshape(EXPERTS * CAP, model_width), jnp.zeros((1, model_width), jnp.float32)],
        axis=0,
    )
    picked = out_pad[pair_slot]
    moe_part = jnp.sum(picked * gate_kept[:, :, None], axis=1)
    moe = lax.psum(moe_part.astype(jnp.bfloat16), "tp").astype(jnp.float32)
    layer_out = (
        (residual + moe).astype(jnp.bfloat16).reshape(sequence_count, block_len, model_width)
    )
    grad_out = cotangent.reshape(tok_count, model_width).astype(jnp.float32)
    gate_part = jnp.sum(picked * grad_out[:, None, :], axis=-1) * kept_float
    grad_pad = jnp.concatenate([grad_out, jnp.zeros((1, model_width), jnp.float32)], axis=0)
    d_expert = (
        (grad_pad[slot_token] * slot_gate[:, None])
        .astype(jnp.bfloat16)
        .reshape(EXPERTS, CAP, model_width)
    )
    d_hidden = jnp.einsum(
        "ecd,deh->ech", d_expert, whole_expert[:, :, 2], preferred_element_type=jnp.float32
    )
    silu_slope = gate_sigmoid * (1.0 + gate_act * (1.0 - gate_sigmoid))
    d_gate_act = (d_hidden * up_act * silu_slope).astype(jnp.bfloat16)
    d_up_act = (d_hidden * active).astype(jnp.bfloat16)
    d_inputs = jnp.einsum(
        "ech,deh->ecd", d_gate_act, whole_expert[:, :, 0], preferred_element_type=jnp.float32
    )
    d_inputs = d_inputs + jnp.einsum(
        "ech,deh->ecd", d_up_act, whole_expert[:, :, 1], preferred_element_type=jnp.float32
    )
    d_in_pad = jnp.concatenate(
        [d_inputs.reshape(EXPERTS * CAP, model_width), jnp.zeros((1, model_width), jnp.float32)],
        axis=0,
    )
    d_normed_part = jnp.sum(d_in_pad[pair_slot], axis=1)
    d_normed_two, gate_grad = lax.psum((d_normed_part, gate_part), "tp")
    d_resid_norm, gain_two = norm_back(residual, inv_two, ffn_norm, d_normed_two)
    d_residual = grad_out + d_resid_norm
    d_attn = d_residual.astype(jnp.bfloat16)
    d_mixed = jnp.einsum(
        "td,dhc->thc", d_attn, whole_attn[:, :, input_columns:], preferred_element_type=jnp.float32
    ).astype(jnp.bfloat16)
    d_mixed_seq = d_mixed.reshape(sequence_count, block_len, kv_loc, QUERY_PER_GROUP, HEAD_DIM)
    d_queries, d_key_all, d_value_all = lax.map(
        lambda item_args: attend_backward(
            item_args[0], item_args[1], item_args[2], allowed, item_args[3], item_args[4]
        ),
        (query_seq, key_all, value_all, log_total, d_mixed_seq),
    )
    d_keys, d_values = (
        lax.psum_scatter(
            d_key_all.astype(jnp.bfloat16), "ctx", scatter_dimension=1, tiled=True
        ).astype(jnp.float32),
        lax.psum_scatter(
            d_value_all.astype(jnp.bfloat16), "ctx", scatter_dimension=1, tiled=True
        ).astype(jnp.float32),
    )
    d_queries = rotate(
        d_queries.reshape(tok_count, kv_loc, QUERY_PER_GROUP, HEAD_DIM), cos_four, -sin_four
    )
    d_keys = rotate(d_keys.reshape(tok_count, kv_loc, HEAD_DIM), cos_three, -sin_three)
    d_values = d_values.reshape(tok_count, kv_loc, HEAD_DIM)
    d_projected = jnp.concatenate([d_queries, d_keys[:, :, None], d_values[:, :, None]], axis=2)
    d_projected = d_projected.astype(jnp.bfloat16).reshape(tok_count, kv_loc, input_columns)
    d_normed_local = jnp.einsum(
        "thc,dhc->td",
        d_projected,
        whole_attn[:, :, :input_columns],
        preferred_element_type=jnp.float32,
    )
    d_normed_one = lax.psum(d_normed_local.astype(jnp.bfloat16), "tp").astype(jnp.float32)
    d_tok_norm, gain_one = norm_back(tok_float, inv_one, attn_norm, d_normed_one)
    tokens_grad = (
        (d_residual + d_tok_norm)
        .astype(jnp.bfloat16)
        .reshape(sequence_count, block_len, model_width)
    )
    gain_one, gain_two = lax.psum((gain_one, gain_two), ("fsdp", "ctx"))
    in_term = jnp.einsum(
        "td,thc->dhc", first_normed, d_projected, preferred_element_type=jnp.float32
    )
    out_term = jnp.einsum("td,thc->dhc", d_attn, mixed_flat, preferred_element_type=jnp.float32)
    attn_grad = lax.psum_scatter(
        jnp.concatenate([in_term, out_term], axis=2),
        ("fsdp", "ctx"),
        scatter_dimension=0,
        tiled=True,
    )
    gate_term = jnp.einsum("ecd,ech->deh", inputs, d_gate_act, preferred_element_type=jnp.float32)
    up_term = jnp.einsum("ecd,ech->deh", inputs, d_up_act, preferred_element_type=jnp.float32)
    down_term = jnp.einsum("ecd,ech->deh", d_expert, hidden, preferred_element_type=jnp.float32)
    expert_grad = lax.psum_scatter(
        jnp.stack([gate_term, up_term, down_term], axis=2),
        ("fsdp", "ctx"),
        scatter_dimension=0,
        tiled=True,
    )
    attn_grad, expert_grad = (
        lax.all_gather(attn_grad.astype(jnp.bfloat16), "ctx", axis=0, tiled=True).astype(
            attn_grad.dtype
        ),
        lax.all_gather(expert_grad.astype(jnp.bfloat16), "ctx", axis=0, tiled=True).astype(
            expert_grad.dtype
        ),
    )
    return (
        layer_out,
        tokens_grad,
        attn_grad,
        expert_grad,
        gain_one,
        gain_two,
        gate_grad.reshape(sequence_count, block_len, TOP),
    )


def solution(mesh):
    in_specs = (
        P("fsdp", "ctx", None),
        P(),
        P("fsdp", "tp", None),
        P(),
        P("fsdp", None, None, "tp"),
        P("fsdp", "ctx", None),
        P("fsdp", "ctx", None),
        P("fsdp", "ctx"),
        P("fsdp", "ctx", None),
    )
    out_specs = (
        P("fsdp", "ctx", None),
        P("fsdp", "ctx", None),
        P("fsdp", "tp", None),
        P("fsdp", None, None, "tp"),
        P(),
        P(),
        P("fsdp", "ctx", None),
    )
    return jax.shard_map(body, mesh=mesh, in_specs=in_specs, out_specs=out_specs, check_vma=False)
```

profile of v0, /device:TPU:0, one launch (start us, length us, event | category | flops | bytes accessed | tf_op | source)
XLA Modules:
  0.0 5023.7 jit_solution(3769000066222413329)
XLA Ops:
  10.3 65.8 %all-gather.6.cloned.1.call-done = bf16[1536,1,1792]{2,0,1:T(8,128)(2,1)} async-done(((bf16[384,1,1792]{2,0,1:T(8,128)(2,1)}), bf16[1536,1,1792]{2,0,1:T(8,128)(2,1)}) %all-gather.6.cloned.1.call-update) | async-done | bytes 5505040 | tf_op jit(solution)/shard_map/all_gather | solution.py:118
  88.3 13.9 all_gather.20
  102.2 14.4 all-gather
  165.5 237.4 %all-gather.8.cloned.1.call-done = bf16[1536,8,3,384]{3,0,1,2:T(8,128)(2,1)} async-done(((bf16[384,8,3,384]{3,0,1,2:T(8,128)(2,1)}), bf16[1536,8,3,384]{3,0,1,2:T(8,128)(2,1)}) %all-gather.8.cloned.1.call-update) | async-done | bytes 28311568 | tf_op jit(solution)/shard_map/all_gather | solution.py:119
  410.0 8.3 fusion.4
  437.2 11.2 gather_fusion.3
  456.1 11.6 convolution_bitcast_fusion.1
  467.7 10.2 fusion
  477.9 12.4 fusion.12
  497.4 11.0 gather_fusion.5
  508.4 8.0 reshape.842
  524.2 11.9 convolution_bitcast_fusion.2
  536.2 12.6 convolution_bitcast_fusion
  548.8 8.2 multiply_reduce_fusion
  580.6 12.4 reduce-scatter.4.cloned.1.call-done
  594.2 19.5 reduce-scatter.6.cloned.1.call-done
  618.5 38.4 pad_maximum_fusion
  656.9 55.6 %copy.68 = f32[1536,8,3,384]{3,1,2,0:T(8,128)} copy(f32[1536,8,3,384]{0,3,1,2:T(8,128)} %pad_maximum_fusion) | data formatting | bytes 113246208 | tf_op jit(solution)/shard_map/stack | solution.py:291
  722.8 9.5 pad_maximum_fusion.1
  732.3 24.6 copy.66
  758.5 4073.6 %all-reduce.17 = (bf16[1536,1,1792]{2,1,0:T(2,128)(2,1)}, f32[1536]{0:T(1024)}, f32[1536]{0:T(1024)}) all-reduce(f32[1536,1,1792]{2,1,0:T(1,128)} %copy.66, f32[1536]{0:T(1024)S(1)} %get-tuple-element.83, f32[1536]{0:T(1024)S(1)} %get-tuple-element.81), channel_id=5, replica_groups=mesh['fsdp'=4,'ctx'=4,'tp'=2] {'fsdp','ctx'}, use_global_device_ids=true, to_apply=%region_21.22.clone | all-reduce | flops 2755584 | bytes 16539648
  4846.1 31.8 all-gather.10.cloned.1.call-done
  4882.9 124.3 %all-gather.12.cloned.1.call-done = bf16[384,8,3,384]{3,1,2,0:T(8,128)(2,1)} async-done(((bf16[96,8,3,384]{3,1,2,0:T(8,128)(2,1)}), bf16[384,8,3,384]{3,1,2,0:T(8,128)(2,1)}) %all-gather.12.cloned.1.call-update) | async-done | bytes 7077904 | tf_op jit(solution)/shard_map/all_gather | solution.py:300
  5007.2 9.2 convert_element_type.254
  (227 shorter events, 171.7 us)
Async XLA Ops:
  7.2 69.0 %all-gather.6.cloned.1.call-start = ((), (), s32[]{:S(2)}) async-start(), calls=%async_computation.3 | async-start | bytes 6881280 | tf_op jit(solution)/shard_map/all_gather | solution.py:118
  7.9 149.5 %all-reduce.12.cloned.1.call-start = ((), (), s32[]{:S(2)}) async-start(), calls=%async_computation.4 | async-start | bytes 3145728 | tf_op jit(solution)/shard_map/psum | solution.py:171
  8.0 79.9 %copy-start.40 = (f32[64]{0:T(128)}, f32[64]{0:T(128)S(1)}, u32[]{:S(2)}) copy-start(f32[64]{0:T(128)S(1)} %multiply_power_fusion) | copy-start | bytes 772
  8.0 79.9 %copy-start.38 = (f32[256]{0:T(256)}, f32[256]{0:T(256)S(1)}, u32[]{:S(2)}) copy-start(f32[256]{0:T(256)S(1)} %add_convert_fusion.3) | copy-start | bytes 3076
  9.4 75.5 %copy-start.36 = (f32[256]{0:T(256)}, f32[256]{0:T(256)S(1)}, u32[]{:S(2)}) copy-start(f32[256]{0:T(256)S(1)} %add_rsqrt_fusion.1) | copy-start | bytes 3076
  10.3 106.3 %copy-start.27 = (f32[256,64]{0,1:T(8,128)}, f32[256,64]{0,1:T(8,128)S(1)}, u32[]{:S(2)}) copy-start(f32[256,64]{0,1:T(8,128)S(1)} %get-tuple-element.107) | copy-start | bytes 196612
  102.2 15.7 copy-start.17
  124.9 278.0 %all-gather.8.cloned.1.call-start = ((), (), s32[]{:S(2)}) async-start(), calls=%async_computation.5 | async-start | bytes 35389440 | tf_op jit(solution)/shard_map/all_gather | solution.py:119
  132.3 17.5 copy-start.15
  132.3 424.7 %all-reduce.14.cloned.1.call-start = ((), (), s32[]{:S(2)}) async-start(), calls=%async_computation.6 | async-start | bytes 3145728 | tf_op jit(solution)/shard_map/psum | solution.py:234
  456.1 11.6 copy-start.9
  524.2 68.8 %reduce-scatter.4.cloned.1.call-start = ((), (), s32[]{:S(2)}) async-start(), calls=%async_computation.7 | async-start | bytes 327680 | tf_op jit(solution)/shard_map/reduce_scatter | solution.py:249
  524.2 12.0 copy-start.13
  524.2 24.6 slice-start.2
  536.2 12.6 slice-start.3
  536.2 12.6 copy-start.7
  536.2 12.6 copy-start.29
  573.0 40.7 reduce-scatter.6.cloned.1.call-start
  575.6 18.3 copy-start.39
  575.6 18.3 copy-start.41
  580.4 176.6 %all-reduce.16.cloned.1.call-start = ((), (), s32[]{:S(2)}) async-start(), calls=%async_computation.12 | async-start | bytes 3145728 | tf_op jit(solution)/shard_map/psum | solution.py:269
  618.5 4216.3 %reduce-scatter.8.cloned.1.call-start = ((), (), s32[]{:S(2)}) async-start(), calls=%async_computation.10 | async-start | bytes 60162048 | tf_op jit(solution)/shard_map/reduce_scatter | solution.py:290
  712.6 4165.3 %all-gather.10.cloned.1.call-start = ((), (), s32[]{:S(2)}) async-start(), calls=%async_computation.9 | async-start | bytes 1720320 | tf_op jit(solution)/shard_map/all_gather | solution.py:297
  4834.7 172.5 %all-gather.12.cloned.1.call-start = ((), (), s32[]{:S(2)}) async-start(), calls=%async_computation.11 | async-start | bytes 8847360 | tf_op jit(solution)/shard_map/all_gather | solution.py:300
  (36 other events, 145.7 us)
Sparse Core Ops, SparseCore 0:
  9.8 66.3 all-gather.5
  125.0 20.4 all-reduce.11
  148.1 254.7 all-gather.7
  524.3 20.3 all-reduce.13
  573.1 19.8 reduce-scatter.3
  595.8 17.9 reduce-scatter.5
  618.6 18.7 all-reduce.15
  712.7 1384.0 reduce-scatter.7
  4834.8 43.0 all-gather.9
  4880.0 127.1 all-gather.11
where the time goes:
time: 5040 us; the launch traced here: 5020 us
  blocking collectives  4110 us (82%)
  waiting for transfers between devices  492 us (10%)
  local copies, waits for them, and re-layouts  186 us (4%)
  matrix products  126 us (2%)
  other arithmetic  97.2 us (2%)
    unnamed x1, blocking collectives  4070 us
    all_gather x1, waiting for transfers between devices, body(): lax.all_gather(expert_weights, 'fsdp', axis=0, tiled=True)  237 us
    all_gather x1, waiting for transfers between devices, body(): lax.all_gather(expert_grad.astype(jnp.bfloat16), 'ctx', axis=0, tiled=True)  124 us
  transfers between devices with their start and end apart: 10, of which 6 were waited for; matrix products, arithmetic and copies ran while one was open for 5% of the time, Pallas kernels for 0%

commit v1 on v0

--- a/solution.py
+++ b/solution.py
@@ -1,6 +1,8 @@
 import jax
 import jax.numpy as jnp
 from jax import lax
+from jax.experimental import pallas as pl
+from jax.experimental.pallas import tpu as pltpu
 from jax.sharding import PartitionSpec as P
 
 HEAD_DIM = 128
@@ -312,6 +314,377 @@
     )
 
 
+MESH_ID = pl.DeviceIdType.MESH
+MIB = 2**20
+
+
+def rel_perm(size, r):
+    return [(i, i ^ r) for i in range(size)]
+
+
+def from_rel(value, r):
+    return lax.ppermute(value, "fsdp", rel_perm(lax.axis_size("fsdp"), r))
+
+
+def swap_core(value):
+    return lax.ppermute(value, "tp", [(0, 1), (1, 0)])
+
+
+def shift_ctx(value, step):
+    size = lax.axis_size("ctx")
+    pairs = [(i, i + step) for i in range(size) if 0 <= i + step < size]
+    return lax.ppermute(value, "ctx", pairs)
+
+
+def sum_ctx(value):
+    place = lax.axis_index("ctx")
+    inner = (place == 1) | (place == 2)
+    arrived = lax.ppermute(value, "ctx", [(0, 1), (3, 2)])
+    pair = jnp.where(
+        inner, value.astype(jnp.float32) + arrived.astype(jnp.float32), value.astype(jnp.float32)
+    ).astype(jnp.bfloat16)
+    across = lax.ppermute(pair, "ctx", [(1, 2), (2, 1)])
+    total = (pair.astype(jnp.float32) + across.astype(jnp.float32)).astype(jnp.bfloat16)
+    back = lax.ppermute(total, "ctx", [(1, 0), (2, 3)])
+    return jnp.where(inner, total, back)
+
+
+def expert_order(place):
+    row = jnp.arange(128, dtype=jnp.int32)
+    expert = (((row // 32) ^ place) * 2) + (row // 16) % 2
+    source = (row % 16) * 8 + expert
+    return (source[:, None] == row[None, :]).astype(jnp.bfloat16)
+
+
+def split_kernel(order_ref, in_ref, out_ref):
+    depth = in_ref.shape[0]
+    for m in range(3):
+        for k in range(depth // 16):
+            block = in_ref[pl.ds(k * 16, 16), m].reshape(128, in_ref.shape[3])
+            moved = jnp.dot(order_ref[...], block, preferred_element_type=jnp.float32)
+            moved = moved.astype(jnp.bfloat16).reshape(8, 16, in_ref.shape[3])
+            out_ref[:, m, pl.ds(k * 16, 16), :] = moved
+
+
+def split_experts(weights, order):
+    rows, _, experts, width = weights.shape
+    step = 64
+    return pl.pallas_call(
+        split_kernel,
+        grid=(rows // step,),
+        in_specs=[
+            pl.BlockSpec((128, 128), lambda i: (0, 0)),
+            pl.BlockSpec((step, 3, experts, width), lambda i: (i, 0, 0, 0)),
+        ],
+        out_specs=pl.BlockSpec((experts, 3, step, width), lambda i: (0, 0, i, 0)),
+        out_shape=jax.ShapeDtypeStruct((experts, 3, rows, width), jnp.bfloat16),
+        compiler_params=pltpu.CompilerParams(vmem_limit_bytes=40 * MIB),
+        name="split_experts",
+    )(order, weights)
+
+
+def join_kernel(order_ref, in_ref, out_ref):
+    width = in_ref.shape[3]
+    for m in range(3):
+        for k in range(in_ref.shape[2] // 16):
+            block = in_ref[:, m, pl.ds(k * 16, 16), :].reshape(128, width)
+            moved = jnp.dot(order_ref[...], block, preferred_element_type=jnp.float32)
+            out_ref[pl.ds(k * 16, 16), m] = moved.reshape(16, 8, width)
+
+
+def join_experts(grads, order):
+    experts, _, rows, width = grads.shape
+    step = 64
+    return pl.pallas_call(
+        join_kernel,
+        grid=(rows // step,),
+        in_specs=[
+            pl.BlockSpec((128, 128), lambda i: (0, 0)),
+            pl.BlockSpec((experts, 3, step, width), lambda i: (0, 0, i, 0)),
+        ],
+        out_specs=pl.BlockSpec((step, 3, experts, width), lambda i: (i, 0, 0, 0)),
+        out_shape=jax.ShapeDtypeStruct((rows, 3, experts, width), jnp.float32),
+        compiler_params=pltpu.CompilerParams(vmem_limit_bytes=40 * MIB),
+        name="join_experts",
+    )(order, grads)
+
+
+NT = (((1,), (1,)), ((), ()))
+TN = (((0,), (0,)), ((), ()))
+
+
+def dot_f32(a, b, dims=(((1,), (0,)), ((), ()))):
+    return lax.dot_general(a, b, dims, preferred_element_type=jnp.float32)
+
+
+def block_probs(place_ref, keys, query):
+    scores = dot_f32(keys, query, NT) * HEAD_DIM ** (-0.5)
+    block = lax.broadcasted_iota(jnp.int32, scores.shape, 0) // query.shape[0]
+    scores = jnp.where(block <= place_ref[0], scores, -1e30)
+    expd = jnp.exp(scores - jnp.max(scores, axis=0, keepdims=True))
+    return expd * (1.0 / jnp.sum(expd, axis=0, keepdims=True))
+
+
+def attend_kernel(place_ref, q_ref, k_ref, v_ref, out_ref):
+    keys = k_ref[...]
+    vals = v_ref[...]
+    for g in range(QUERY_PER_GROUP):
+        cols = pl.ds(g * HEAD_DIM, HEAD_DIM)
+        probs = block_probs(place_ref, keys, q_ref[:, cols]).astype(jnp.bfloat16)
+        out_ref[:, cols] = dot_f32(probs, vals, TN).astype(jnp.bfloat16)
+
+
+def attend_back_kernel(place_ref, q_ref, k_ref, v_ref, dm_ref, dq_ref, dk_ref, dv_ref):
+    keys = k_ref[...]
+    vals = v_ref[...]
+    scale = HEAD_DIM ** (-0.5)
+    dk_ref[...] = jnp.zeros_like(dk_ref)
+    dv_ref[...] = jnp.zeros_like(dv_ref)
+    for g in range(QUERY_PER_GROUP):
+        cols = pl.ds(g * HEAD_DIM, HEAD_DIM)
+        query = q_ref[:, cols]
+        d_mixed = dm_ref[:, cols]
+        probs = block_probs(place_ref, keys, query)
+        d_probs = dot_f32(vals, d_mixed, NT)
+        inner = jnp.sum(probs * d_probs, axis=0, keepdims=True)
+        d_scores = (probs * (d_probs - inner)).astype(jnp.bfloat16)
+        dq_ref[:, cols] = dot_f32(d_scores, keys, TN) * scale
+        dk_ref[...] += dot_f32(d_scores, query) * scale
+        dv_ref[...] += dot_f32(probs.astype(jnp.bfloat16), d_mixed)
+
+
+def attend(place, q, k, v):
+    return pl.pallas_call(
+        attend_kernel,
+        in_specs=[pl.BlockSpec(memory_space=pltpu.SMEM)]
+        + [pl.BlockSpec(memory_space=pltpu.VMEM)] * 3,
+        out_specs=pl.BlockSpec(memory_space=pltpu.VMEM),
+        out_shape=jax.ShapeDtypeStruct(q.shape, jnp.bfloat16),
+        compiler_params=pltpu.CompilerParams(vmem_limit_bytes=40 * MIB),
+        name="attend",
+    )(place, q, k, v)
+
+
+def attend_back(place, q, k, v, d_mixed):
+    return pl.pallas_call(
+        attend_back_kernel,
+        in_specs=[pl.BlockSpec(memory_space=pltpu.SMEM)]
+        + [pl.BlockSpec(memory_space=pltpu.VMEM)] * 4,
+        out_specs=[pl.BlockSpec(memory_space=pltpu.VMEM)] * 3,
+        out_shape=[
+            jax.ShapeDtypeStruct(q.shape, jnp.float32),
+            jax.ShapeDtypeStruct(k.shape, jnp.float32),
+            jax.ShapeDtypeStruct(v.shape, jnp.float32),
+        ],
+        compiler_params=pltpu.CompilerParams(vmem_limit_bytes=40 * MIB),
+        name="attend_back",
+    )(place, q, k, v, d_mixed)
+
+
+def spread_rows(half):
+    mine = jnp.stack([half] + [from_rel(half, r) for r in range(1, 4)])
+    return jnp.stack([mine, swap_core(mine)])
+
+
+def gather_sum(parts):
+    own, other = parts[0], parts[1].astype(jnp.bfloat16)
+    both = own + swap_core(other).astype(jnp.float32)
+    total = both[0]
+    for r in range(1, 4):
+        total = total + from_rel(both[r].astype(jnp.bfloat16), r).astype(jnp.float32)
+    return total
+
+
+def join_halves(core, half):
+    other = swap_core(half)
+    first = jnp.where(core == 0, half, other)
+    second = jnp.where(core == 0, other, half)
+    return jnp.concatenate([first, second], axis=0)
+
+
+def body_fast(
+    tokens,
+    attn_norm,
+    attention_params,
+    ffn_norm,
+    expert_weights,
+    gate_values,
+    routes,
+    slot_order,
+    cotangent,
+):
+    sequence_count, block_len, model_width = tokens.shape
+    count = sequence_count * block_len
+    half = count // 2
+    own_experts = EXPERTS // 4
+    input_columns = (QUERY_PER_GROUP + 2) * HEAD_DIM
+    query_columns = QUERY_PER_GROUP * HEAD_DIM
+    f = lax.axis_index("fsdp")
+    z = lax.axis_index("ctx")
+    core = lax.axis_index("tp")
+    shard = attention_params.shape[0]
+    f32, bf16 = jnp.float32, jnp.bfloat16
+
+    def my_half(value):
+        return lax.dynamic_slice_in_dim(value, core * half, half, 0)
+
+    attn_own = attention_params[:, 0, :]
+    attn_x, attn_y = from_rel(attn_own, 1), from_rel(attn_own, 2)
+    cut = shard // 2
+    attn_d = jnp.concatenate([from_rel(attn_x[:cut], 2), from_rel(attn_y[cut:], 1)], axis=0)
+    place_order = jnp.arange(4, dtype=jnp.int32) ^ f
+    whole_attn = jnp.stack([attn_own, attn_x, attn_y, attn_d])[place_order].reshape(
+        4 * shard, attention_params.shape[2]
+    )
+    attn_in, attn_out = whole_attn[:, :input_columns], whole_attn[:, input_columns:]
+
+    order = expert_order(f)
+    pieces = split_experts(jnp.transpose(expert_weights, (0, 2, 1, 3)), order)
+    pieces = pieces.reshape(4, own_experts, 3, shard, expert_weights.shape[3])
+    arrived = [pieces[0]] + [from_rel(pieces[r], r) for r in range(1, 4)]
+    whole_expert = jnp.stack(arrived, axis=2)
+    whole_expert = jnp.take(whole_expert, place_order, axis=2).reshape(
+        own_experts, 3, 4 * shard, expert_weights.shape[3]
+    )
+
+    route_rows, rank_rows = routes.reshape(count, TOP), slot_order.reshape(count)
+    gates = gate_values.reshape(count, TOP)
+    chosen = route_rows[:, :, None] == jnp.arange(EXPERTS, dtype=jnp.int32)
+    member = jnp.any(chosen, axis=1)
+    ahead = rank_rows[None, :] < rank_rows[:, None]
+    slots = dot_f32(ahead.astype(bf16), member.astype(bf16))
+    kept = member & (slots < CAP - 0.5)
+    weight = jnp.sum(jnp.where(chosen, gates[:, :, None], 0.0), axis=1) * kept.astype(f32)
+    weight_rows = weight.T.reshape(4, own_experts, 2, half)
+    weight_rows = weight_rows[place_order]
+    weights_in = jnp.stack(
+        [weight_rows[0]] + [from_rel(weight_rows[r], r) for r in range(1, 4)]
+    )
+    weights_in = jnp.where(core == 0, weights_in, weights_in[:, :, ::-1])
+    weights_in = jnp.transpose(weights_in, (1, 2, 0, 3)).reshape(own_experts, 8 * half)
+
+    positions = z * block_len + jnp.arange(block_len, dtype=jnp.int32)
+    cosine, sine = angle_tables(positions)
+    cos_three, sin_three = cosine[:, None, :], sine[:, None, :]
+    tok_float = tokens.reshape(count, model_width).astype(f32)
+    inv_one = lax.rsqrt(jnp.mean(tok_float * tok_float, axis=-1, keepdims=True) + eps)
+    first_normed = (tok_float * inv_one * attn_norm).astype(bf16)
+    projected = dot_f32(first_normed, attn_in).reshape(count, QUERY_PER_GROUP + 2, HEAD_DIM)
+    turned = rotate(projected[:, : QUERY_PER_GROUP + 1], cos_three, sin_three).astype(bf16)
+    queries = turned[:, :QUERY_PER_GROUP].reshape(count, query_columns)
+    key_value = jnp.concatenate(
+        [turned[:, QUERY_PER_GROUP], projected[:, QUERY_PER_GROUP + 1].astype(bf16)], axis=1
+    )
+    kv_all = jnp.concatenate([key_value] + [shift_ctx(key_value, s) for s in range(1, 4)], axis=0)
+    key_all, value_all = kv_all[:, :HEAD_DIM], kv_all[:, HEAD_DIM:]
+    place = jnp.reshape(z, (1,)).astype(jnp.int32)
+    mixed = attend(place, queries, key_all, value_all)
+    attn_part = dot_f32(mixed, attn_out, NT)
+    other_rows = lax.dynamic_slice_in_dim(attn_part, (1 - core) * half, half, 0)
+    residual = my_half(tok_float) + (my_half(attn_part) + swap_core(other_rows))
+    inv_two = lax.rsqrt(jnp.mean(residual * residual, axis=-1, keepdims=True) + eps)
+    normed_two = (residual * inv_two * ffn_norm).astype(bf16)
+
+    grad_out = cotangent.reshape(count, model_width)
+    inputs = spread_rows(normed_two).reshape(8 * half, model_width)
+    upstream = spread_rows(my_half(grad_out)).reshape(8 * half, model_width)
+    moe_parts = 0.0
+    d_normed_parts = 0.0
+    gate_parts = []
+    expert_grads = []
+    for e in range(own_experts):
+        gate_act = dot_f32(inputs, whole_expert[e, 0])
+        up_act = dot_f32(inputs, whole_expert[e, 1])
+        d_plain = dot_f32(upstream, whole_expert[e, 2])
+        gate_sigmoid = jax.nn.sigmoid(gate_act)
+        active = gate_act * gate_sigmoid
+        hidden = active * up_act
+        scale = weights_in[e][:, None]
+        hidden_low = (hidden * scale).astype(bf16)
+        gate_parts.append(jnp.sum(hidden * d_plain, axis=1))
+        d_hidden = d_plain * scale
+        silu_slope = gate_sigmoid * (1.0 + gate_act * (1.0 - gate_sigmoid))
+        d_gate = (d_hidden * up_act * silu_slope).astype(bf16)
+        d_up = (d_hidden * active).astype(bf16)
+        moe_parts = moe_parts + dot_f32(hidden_low, whole_expert[e, 2], NT)
+        d_normed_parts = (
+            d_normed_parts
+            + dot_f32(d_gate, whole_expert[e, 0], NT)
+            + dot_f32(d_up, whole_expert[e, 1], NT)
+        )
+        expert_grads.append(
+            jnp.stack(
+                [
+                    dot_f32(inputs, d_gate, TN).astype(bf16),
+                    dot_f32(inputs, d_up, TN).astype(bf16),
+                    dot_f32(upstream, hidden_low, TN).astype(bf16),
+                ]
+            )
+        )
+    d_normed_two = gather_sum(d_normed_parts.reshape(2, 4, half, model_width))
+    moe = gather_sum(moe_parts.reshape(2, 4, half, model_width))
+    layer_out = join_halves(core, (residual + moe).astype(bf16))
+
+    gate_rows = jnp.stack(gate_parts).reshape(own_experts, 2, 4, half)
+    gate_rows = gate_rows[:, 0] + swap_core(gate_rows[:, 1])
+    gate_rows = jnp.stack(
+        [gate_rows[:, 0]] + [from_rel(gate_rows[:, r], r) for r in range(1, 4)]
+    )
+    gate_rows = join_halves(core, gate_rows.reshape(EXPERTS, half).T)
+    rel_ids = (place_order[:, None] * own_experts + jnp.arange(own_experts)).reshape(EXPERTS)
+    kept_rel = kept[:, rel_ids]
+    picked = (route_rows[:, :, None] == rel_ids) & kept_rel[:, None, :]
+    gate_grad = jnp.sum(jnp.where(picked, gate_rows[:, None, :], 0.0), axis=-1)
+
+    d_resid_norm, gain_two = norm_back(residual, inv_two, ffn_norm, d_normed_two)
+    d_residual = my_half(grad_out).astype(f32) + d_resid_norm
+    d_attn = join_halves(core, d_residual.astype(bf16))
+    d_mixed = dot_f32(d_attn, attn_out).astype(bf16)
+    d_queries, d_key_all, d_value_all = attend_back(place, queries, key_all, value_all, d_mixed)
+    d_kv = jnp.concatenate([d_key_all, d_value_all], axis=1).reshape(4, count, 2 * HEAD_DIM)
+    d_key_value = d_kv[0]
+    for s in range(1, 4):
+        d_key_value = d_key_value + shift_ctx(d_kv[s].astype(bf16), -s).astype(f32)
+    d_turned = jnp.concatenate([d_queries, d_key_value[:, :HEAD_DIM]], axis=1)
+    d_turned = rotate(
+        d_turned.reshape(count, QUERY_PER_GROUP + 1, HEAD_DIM), cos_three, -sin_three
+    ).reshape(count, query_columns + HEAD_DIM)
+    d_projected = jnp.concatenate([d_turned, d_key_value[:, HEAD_DIM:]], axis=1).astype(bf16)
+    d_normed_local = dot_f32(d_projected, attn_in, NT)
+    other_rows = lax.dynamic_slice_in_dim(d_normed_local, (1 - core) * half, half, 0)
+    d_normed_one = my_half(d_normed_local) + swap_core(other_rows.astype(bf16)).astype(f32)
+    d_tok_norm, gain_one = norm_back(my_half(tok_float), my_half(inv_one), attn_norm, d_normed_one)
+    tokens_grad = join_halves(core, (d_residual + d_tok_norm).astype(bf16))
+    gains = lax.psum(jnp.stack([gain_one, gain_two]), ("fsdp", "ctx", "tp"))
+
+    attn_grad = jnp.concatenate(
+        [dot_f32(first_normed, d_projected, TN), dot_f32(d_attn, mixed, TN)], axis=1
+    ).reshape(4, shard, -1)[place_order]
+    attn_sum = attn_grad[0]
+    for r in range(1, 4):
+        attn_sum = attn_sum + from_rel(attn_grad[r].astype(bf16), r).astype(f32)
+    attn_total = sum_ctx(attn_sum.astype(bf16)).astype(f32)[:, None, :]
+
+    finals = []
+    for e in range(own_experts):
+        total = sum_ctx(expert_grads[e]).reshape(3, 4, shard, -1)
+        total = jnp.take(total, place_order, axis=1)
+        finals.append(
+            jnp.stack([total[:, 0]] + [from_rel(total[:, r], r) for r in range(1, 4)])
+        )
+    finals = jnp.stack(finals, axis=1).reshape(EXPERTS, 3, shard, -1)
+    expert_grad = jnp.transpose(join_experts(finals, order.T), (0, 2, 1, 3))
+    return (
+        layer_out.reshape(sequence_count, block_len, model_width),
+        tokens_grad.reshape(sequence_count, block_len, model_width),
+        attn_total,
+        expert_grad,
+        gains[0],
+        gains[1],
+        gate_grad.reshape(sequence_count, block_len, TOP),
+    )
+
+
 def solution(mesh):
     in_specs = (
         P("fsdp", "ctx", None),
@@ -333,4 +706,6 @@
         P(),
         P("fsdp", "ctx", None),
     )
-    return jax.shard_map(body, mesh=mesh, in_specs=in_specs, out_specs=out_specs, check_vma=False)
+    four = mesh.shape["fsdp"] == 4 and mesh.shape["ctx"] == 4 and mesh.shape["tp"] == 2
+    body_fn = body_fast if four else body
+    return jax.shard_map(body_fn, mesh=mesh, in_specs=in_specs, out_specs=out_specs, check_vma=False)

time: 5040 us -> 891 us (0.18)
  blocking collectives: 4110 us -> 139 us
  waiting for transfers between devices: 492 us -> 380 us
  local copies, waits for them, and re-layouts: 186 us -> 93.3 us
  starting transfers between devices: 0.41 us -> 88.9 us
  matrix products: 126 us -> 58.4 us
    unnamed x1 -> x0, blocking collectives: 4070 us -> none
    all_gather x4 -> x0, waiting for transfers between devices: 459 us -> none  [the longest x1 237 us: body(): lax.all_gather(expert_weights, 'fsdp', axis=0, tiled=True)]
    ppermute x0 -> x60, waiting for transfers between devices: none -> 380 us  [the longest x34 283 us: from_rel(): return lax.ppermute(value, 'fsdp', rel_perm(lax.axis_size('fsdp'), r))]
    psum x1, blocking collectives: 3.75 us -> 139 us  [body_fast(): gains = lax.psum(jnp.stack([gain_one, gain_two]), ('fsdp', 'ctx', 'tp'))]
    ppermute x0 -> x60, starting transfers between devices: none -> 88.9 us  [the longest x34 47.9 us: from_rel(): return lax.ppermute(value, 'fsdp', rel_perm(lax.axis_size('fsdp'), r))]
    dot_general x21 -> x25, matrix products: 126 us -> 58.4 us  [dot_f32(): return lax.dot_general(a, b, dims, preferred_element_type=jnp.float32)]
    another operation x1 -> x6, local copies, waits for them, and re-layouts: 55.6 us -> 4.04 us  [the longest x1 3.18 us: body_fast(): whole_expert = jnp.stack(arrived, axis=2)]
  transfers between devices with their start and end apart: 10 -> 60, of which waited for: 6 -> 30; matrix products, arithmetic and copies ran while one was open for 5% -> 22% of each run, Pallas kernels for 0% -> 2%
where the time goes in v1:
time: 891 us; the launch traced here: 885 us
  waiting for transfers between devices  380 us (43%)
  blocking collectives  139 us (16%)
  other arithmetic  102 us (11%)
  local copies, waits for them, and re-layouts  93.3 us (10%)
  starting transfers between devices  88.9 us (10%)
  matrix products  58.4 us (7%)
  Pallas kernels  21.8 us (2%)
    ppermute x34, waiting for transfers between devices, from_rel(): return lax.ppermute(value, 'fsdp', rel_perm(lax.axis_size('fsdp'), r))  283 us
    psum x1, blocking collectives, body_fast(): gains = lax.psum(jnp.stack([gain_one, gain_two]), ('fsdp', 'ctx', 'tp'))  139 us
    ppermute x6, waiting for transfers between devices, shift_ctx(): return lax.ppermute(value, 'ctx', pairs)  60 us
    dot_general x25, matrix products, dot_f32(): return lax.dot_general(a, b, dims, preferred_element_type=jnp.float32)  58.4 us
    ppermute x34, starting transfers between devices, from_rel(): return lax.ppermute(value, 'fsdp', rel_perm(lax.axis_size('fsdp'), r))  47.9 us
    ppermute x3, waiting for transfers between devices, sum_ctx(): arrived = lax.ppermute(value, 'ctx', [(0, 1), (3, 2)])  35.2 us
    unnamed x124, local copies, waits for them, and re-layouts  26.1 us
  transfers between devices with their start and end apart: 60, of which 30 were waited for; matrix products, arithmetic and copies ran while one was open for 22% of the time, Pallas kernels for 2%

profile of v1, /device:TPU:0, one launch (start us, length us, event | category | flops | bytes accessed | tf_op | source)
XLA Modules:
  0.0 884.9 jit_solution(18294630847987145551)
XLA Ops:
  9.0 26.6 %collective-permute-done.1 = bf16[384,1792]{1,0:T(8,128)(2,1)S(1)} collective-permute-done((bf16[384,1792]{1,0:T(8,128)(2,1)}, bf16[384,1792]{1,0:T(8,128)(2,1)S(1)}, u32[]{:S(2)}, u32[]{:S(2)}) %collective-permute-start.1) | collective-permute-done | bytes 1376288 | tf_op jit(solution)/shard_map/ppermute | solution.py:326
  42.7 16.1 %collective-permute-done.3 = bf16[192,1792]{1,0:T(8,128)(2,1)S(1)} collective-permute-done((bf16[192,1792]{1,0:T(8,128)(2,1)S(1)}, bf16[192,1792]{1,0:T(8,128)(2,1)S(1)}, u32[]{:S(2)}, u32[]{:S(2)}) %collective-permute-start.3) | collective-permute-done | bytes 688160 | tf_op jit(solution)/shard_map/ppermute | solution.py:326
  58.7 6.9 collective-permute-done.2
  123.6 79.9 %collective-permute-done.23 = bf16[128,1536]{1,0:T(8,128)(2,1)} collective-permute-done((bf16[128,1536]{1,0:T(8,128)(2,1)}, bf16[128,1536]{1,0:T(8,128)(2,1)}, u32[]{:S(2)}, u32[]{:S(2)}) %collective-permute-start.23) | collective-permute-done | bytes 393248 | tf_op jit(solution)/shard_map/ppermute | solution.py:326
  230.6 7.4 gather_fusion.1
  238.0 7.0 copy.58
  332.0 7.4 collective-permute-done.30
  339.3 7.5 collective-permute-done.29
  358.2 7.7 attend_back.1
  372.9 60.0 %collective-permute-done.34 = bf16[256,256]{1,0:T(8,128)(2,1)S(1)} collective-permute-done((bf16[256,256]{1,0:T(8,128)(2,1)S(1)}, bf16[256,256]{1,0:T(8,128)(2,1)S(1)}, u32[]{:S(2)}, u32[]{:S(2)}) %collective-permute-start.34) | collective-permute-done | bytes 131104 | tf_op jit(solution)/shard_map/ppermute | solution.py:336
  455.4 9.5 %pad_maximum_fusion = f32[1536,1792]{0,1:T(8,128)} fusion(f32[1536,768]{0,1:T(8,128)} %fusion.62, f32[1536,1024]{0,1:T(8,128)} %fusion.39), kind=kLoop, calls=%fused_computation.7 | loop fusion | flops 2752512 | bytes 22020096 | tf_op jit(solution)/shard_map/concatenate | solution.py:660
  464.9 12.2 %copy.75 = f32[1536,1792]{1,0:T(8,128)} copy(f32[1536,1792]{0,1:T(8,128)} %pad_maximum_fusion) | data formatting | bytes 22020096 | tf_op jit(solution)/shard_map/reshape | solution.py:662
  477.1 9.6 %gather_fusion.3 = f32[4,384,1792]{2,1,0:T(8,128)} fusion(f32[4,384,1792]{2,1,0:T(8,128)} %bitcast.308, s32[1024]{0:T(1024)S(1)} %pad_clamp_fusion.2), kind=kCustom, calls=%fused_computation.5 | custom fusion | bytes 22020112 | tf_op jit(solution)/shard_map/gather | solution.py:660
  491.5 18.5 %collective-permute-done.49 = bf16[3,1536,384]{2,1,0:T(8,128)(2,1)} collective-permute-done((bf16[3,1536,384]{2,1,0:T(8,128)(2,1)}, bf16[3,1536,384]{2,1,0:T(8,128)(2,1)}, u32[]{:S(2)}, u32[]{:S(2)}) %collective-permute-start.49) | collective-permute-done | bytes 3538976 | tf_op jit(solution)/shard_map/ppermute | solution.py:342
  521.1 26.9 %collective-permute-done.39 = bf16[384,1792]{1,0:T(8,128)(2,1)S(1)} collective-permute-done((bf16[384,1792]{1,0:T(8,128)(2,1)S(1)}, bf16[384,1792]{1,0:T(8,128)(2,1)S(1)}, u32[]{:S(2)}, u32[]{:S(2)}) %collective-permute-start.39) | collective-permute-done | bytes 1376288 | tf_op jit(solution)/shard_map/ppermute | solution.py:326
  549.6 27.8 %collective-permute-done.38 = bf16[384,1792]{1,0:T(8,128)(2,1)S(1)} collective-permute-done((bf16[384,1792]{1,0:T(8,128)(2,1)S(1)}, bf16[384,1792]{1,0:T(8,128)(2,1)S(1)}, u32[]{:S(2)}, u32[]{:S(2)}) %collective-permute-start.38) | collective-permute-done | bytes 1376288 | tf_op jit(solution)/shard_map/ppermute | solution.py:326
  581.3 8.5 collective-permute-start.40
  602.2 16.7 %collective-permute-done.40 = bf16[384,1792]{1,0:T(8,128)(2,1)S(1)} collective-permute-done((bf16[384,1792]{1,0:T(8,128)(2,1)S(1)}, bf16[384,1792]{1,0:T(8,128)(2,1)S(1)}, u32[]{:S(2)}, u32[]{:S(2)}) %collective-permute-start.40) | collective-permute-done | bytes 1376288 | tf_op jit(solution)/shard_map/ppermute | solution.py:342
  631.2 138.9 %psum.7 = f32[2,1536]{1,0:T(2,128)S(1)} all-reduce(f32[2,1536]{1,0:T(2,128)S(1)} %pad_maximum_fusion.21), channel_id=1, replica_groups=mesh['fsdp'=4,'ctx'=4,'tp'=2] {'fsdp','ctx','tp'}, use_global_device_ids=true, to_apply=%region_8.10 | all-reduce | flops 3072 | bytes 24576 | tf_op jit(solution)/shard_map/psum | solution.py:658
  808.8 12.5 %collective-permute-done.54 = bf16[3,384,384]{2,1,0:T(8,128)(2,1)S(1)} collective-permute-done((bf16[3,384,384]{2,1,0:T(8,128)(2,1)S(1)}, bf16[3,384,384]{2,1,0:T(8,128)(2,1)S(1)}, u32[]{:S(2)}, u32[]{:S(2)}) %collective-permute-start.54) | collective-permute-done | bytes 884768 | tf_op jit(solution)/shard_map/ppermute | solution.py:326
  829.4 10.9 %collective-permute-done.53 = bf16[3,384,384]{2,1,0:T(8,128)(2,1)S(1)} collective-permute-done((bf16[3,384,384]{2,1,0:T(8,128)(2,1)S(1)}, bf16[3,384,384]{2,1,0:T(8,128)(2,1)S(1)}, u32[]{:S(2)}, u32[]{:S(2)}) %collective-permute-start.53) | collective-permute-done | bytes 884768 | tf_op jit(solution)/shard_map/ppermute | solution.py:326
  841.6 17.6 %collective-permute-done.48 = bf16[3,384,384]{2,1,0:T(8,128)(2,1)S(1)} collective-permute-done((bf16[3,384,384]{2,1,0:T(8,128)(2,1)S(1)}, bf16[3,384,384]{2,1,0:T(8,128)(2,1)S(1)}, u32[]{:S(2)}, u32[]{:S(2)}) %collective-permute-start.48) | collective-permute-done | bytes 884768 | tf_op jit(solution)/shard_map/ppermute | solution.py:326
  859.2 16.9 %collective-permute-done.47 = bf16[3,384,384]{2,1,0:T(8,128)(2,1)S(1)} collective-permute-done((bf16[3,384,384]{2,1,0:T(8,128)(2,1)S(1)}, bf16[3,384,384]{2,1,0:T(8,128)(2,1)S(1)}, u32[]{:S(2)}, u32[]{:S(2)}) %collective-permute-start.47) | collective-permute-done | bytes 884768 | tf_op jit(solution)/shard_map/ppermute | solution.py:326
  877.9 6.8 join_experts.1
  (383 shorter events, 322.8 us)
Async XLA Ops:
  6.9 112.0 %collective-permute-start.25 = (bf16[128,1536]{1,0:T(8,128)(2,1)}, bf16[128,1536]{1,0:T(8,128)(2,1)}, u32[]{:S(2)}, u32[]{:S(2)}) collective-permute-start(bf16[128,1536]{1,0:T(8,128)(2,1)} %fusion.135), channel_id=1, source_target_pairs={{0,24},{8,16},{16,8},{24,0},{1,25},{9,17},{17,9},{25,1},{2,26},{10... | collective-permute-start | bytes 1179656 | tf_op jit(solution)/shard_map/ppermute | solution.py:326
  7.0 114.2 %collective-permute-start.24 = (bf16[128,1536]{1,0:T(8,128)(2,1)}, bf16[128,1536]{1,0:T(8,128)(2,1)}, u32[]{:S(2)}, u32[]{:S(2)}) collective-permute-start(bf16[128,1536]{1,0:T(8,128)(2,1)} %fusion.135), channel_id=1, source_target_pairs={{0,16},{8,24},{16,0},{24,8},{1,17},{9,25},{17,1},{25,9},{2,18},{10... | collective-permute-start | bytes 1179656 | tf_op jit(solution)/shard_map/ppermute | solution.py:326
  114.4 109.8 %collective-permute-start.14 = (bf16[2,3,384,384]{3,2,1,0:T(8,128)(2,1)}, bf16[2,3,384,384]{3,2,1,0:T(8,128)(2,1)}, u32[]{:S(2)}, u32[]{:S(2)}) collective-permute-start(bf16[2,3,384,384]{3,2,1,0:T(8,128)(2,1)} %get-tuple-element.44), channel_id=1, source_target_pairs={{0,24},{8,16},{16,8},{24,0},{1,25},{9,17},{17,9},{25,1},{2,26},{10... | collective-permute-start | bytes 5308424 | tf_op jit(solution)/shard_map/ppermute | solution.py:326
  116.9 107.4 %collective-permute-start.13 = (bf16[2,3,384,384]{3,2,1,0:T(8,128)(2,1)}, bf16[2,3,384,384]{3,2,1,0:T(8,128)(2,1)}, u32[]{:S(2)}, u32[]{:S(2)}) collective-permute-start(bf16[2,3,384,384]{3,2,1,0:T(8,128)(2,1)} %get-tuple-element.45), channel_id=1, source_target_pairs={{0,16},{8,24},{16,0},{24,8},{1,17},{9,25},{17,1},{25,9},{2,18},{10... | collective-permute-start | bytes 5308424 | tf_op jit(solution)/shard_map/ppermute | solution.py:326
  117.9 106.4 %collective-permute-start.12 = (bf16[2,3,384,384]{3,2,1,0:T(8,128)(2,1)}, bf16[2,3,384,384]{3,2,1,0:T(8,128)(2,1)}, u32[]{:S(2)}, u32[]{:S(2)}) collective-permute-start(bf16[2,3,384,384]{3,2,1,0:T(8,128)(2,1)} %get-tuple-element.46), channel_id=1, source_target_pairs={{0,8},{8,0},{16,24},{24,16},{1,9},{9,1},{17,25},{25,17},{2,10},{10... | collective-permute-start | bytes 5308424 | tf_op jit(solution)/shard_map/ppermute | solution.py:326
  118.9 84.6 %collective-permute-start.23 = (bf16[128,1536]{1,0:T(8,128)(2,1)}, bf16[128,1536]{1,0:T(8,128)(2,1)}, u32[]{:S(2)}, u32[]{:S(2)}) collective-permute-start(bf16[128,1536]{1,0:T(8,128)(2,1)} %fusion.135), channel_id=1, source_target_pairs={{0,8},{8,0},{16,24},{24,16},{1,9},{9,1},{17,25},{25,17},{2,10},{10... | collective-permute-start | bytes 1179656 | tf_op jit(solution)/shard_map/ppermute | solution.py:326
  121.2 90.3 %collective-permute-start.10 = (bf16[128,1536]{1,0:T(8,128)(2,1)}, bf16[128,1536]{1,0:T(8,128)(2,1)S(1)}, u32[]{:S(2)}, u32[]{:S(2)}) collective-permute-start(bf16[128,1536]{1,0:T(8,128)(2,1)} %multiply_convert_fusion.7), channel_id=1, source_target_pairs={{0,24},{8,16},{16,8},{24,0},{1,25},{9,17},{17,9},{25,1},{2,26},{10... | collective-permute-start | bytes 1179656 | tf_op jit(solution)/shard_map/ppermute | solution.py:326
  317.2 198.4 %collective-permute-start.18 = (bf16[4,128,1536]{2,1,0:T(8,128)(2,1)}, bf16[4,128,1536]{2,1,0:T(8,128)(2,1)}, u32[]{:S(2)}, u32[]{:S(2)}) collective-permute-start(bf16[4,128,1536]{2,1,0:T(8,128)(2,1)} %bitcast.54), channel_id=1, source_target_pairs={{0,1},{1,0},{2,3},{3,2},{4,5},{5,4},{6,7},{7,6},{8,9},{9,8},{10,11... | collective-permute-start | bytes 4718600 | tf_op jit(solution)/shard_map/ppermute | solution.py:330
  349.9 99.1 %collective-permute-start.43 = (bf16[3,1536,384]{2,1,0:T(8,128)(2,1)}, bf16[3,1536,384]{2,1,0:T(8,128)(2,1)}, u32[]{:S(2)}, u32[]{:S(2)}) collective-permute-start(bf16[3,1536,384]{2,1,0:T(8,128)(2,1)} %pad_maximum_fusion.4), channel_id=1, source_target_pairs={{0,2},{6,4},{1,3},{7,5},{8,10},{14,12},{9,11},{15,13},{16,18},{22,... | collective-permute-start | bytes 10616840 | tf_op jit(solution)/shard_map/ppermute | solution.py:342
  366.1 66.8 %collective-permute-start.34 = (bf16[256,256]{1,0:T(8,128)(2,1)S(1)}, bf16[256,256]{1,0:T(8,128)(2,1)S(1)}, u32[]{:S(2)}, u32[]{:S(2)}) collective-permute-start(bf16[256,256]{1,0:T(8,128)(2,1)S(1)} %get-tuple-element.89), channel_id=1, source_target_pairs={{6,0},{7,1},{14,8},{15,9},{22,16},{23,17},{30,24},{31,25}} | collective-permute-start | bytes 393224 | tf_op jit(solution)/shard_map/ppermute | solution.py:336
  367.4 69.1 %collective-permute-start.33 = (bf16[256,256]{1,0:T(8,128)(2,1)S(1)}, bf16[256,256]{1,0:T(8,128)(2,1)S(1)}, u32[]{:S(2)}, u32[]{:S(2)}) collective-permute-start(bf16[256,256]{1,0:T(8,128)(2,1)S(1)} %get-tuple-element.90), channel_id=1, source_target_pairs={{4,0},{6,2},{5,1},{7,3},{12,8},{14,10},{13,9},{15,11},{20,16},{22,... | collective-permute-start | bytes 393224 | tf_op jit(solution)/shard_map/ppermute | solution.py:336
  368.7 67.8 %collective-permute-start.32 = (bf16[256,256]{1,0:T(8,128)(2,1)S(1)}, bf16[256,256]{1,0:T(8,128)(2,1)S(1)}, u32[]{:S(2)}, u32[]{:S(2)}) collective-permute-start(bf16[256,256]{1,0:T(8,128)(2,1)S(1)} %get-tuple-element.88), channel_id=1, source_target_pairs={{2,0},{4,2},{6,4},{3,1},{5,3},{7,5},{10,8},{12,10},{14,12},{11,9},... | collective-permute-start | bytes 393224 | tf_op jit(solution)/shard_map/ppermute | solution.py:336
  432.9 77.1 %collective-permute-start.49 = (bf16[3,1536,384]{2,1,0:T(8,128)(2,1)}, bf16[3,1536,384]{2,1,0:T(8,128)(2,1)}, u32[]{:S(2)}, u32[]{:S(2)}) collective-permute-start(bf16[3,1536,384]{2,1,0:T(8,128)(2,1)} %pad_maximum_fusion.5), channel_id=1, source_target_pairs={{0,2},{6,4},{1,3},{7,5},{8,10},{14,12},{9,11},{15,13},{16,18},{22,... | collective-permute-start | bytes 10616840 | tf_op jit(solution)/shard_map/ppermute | solution.py:342
  445.2 71.7 %collective-permute-start.35 = (bf16[128,1536]{1,0:T(8,128)(2,1)}, bf16[128,1536]{1,0:T(8,128)(2,1)}, u32[]{:S(2)}, u32[]{:S(2)}) collective-permute-start(bf16[128,1536]{1,0:T(8,128)(2,1)} %dynamic-slice_convert_fusion), channel_id=1, source_target_pairs={{0,1},{1,0},{2,3},{3,2},{4,5},{5,4},{6,7},{7,6},{8,9},{9,8},{10,11... | collective-permute-start | bytes 1179656 | tf_op jit(solution)/shard_map/ppermute | solution.py:330
  452.9 136.9 %collective-permute-start.44 = (bf16[3,1536,384]{2,1,0:T(8,128)(2,1)}, bf16[3,1536,384]{2,1,0:T(8,128)(2,1)}, u32[]{:S(2)}, u32[]{:S(2)}) collective-permute-start(bf16[3,1536,384]{2,1,0:T(8,128)(2,1)} %fusion), channel_id=1, source_target_pairs={{2,4},{4,2},{3,5},{5,3},{10,12},{12,10},{11,13},{13,11},{18,20},{2... | collective-permute-start | bytes 10616840 | tf_op jit(solution)/shard_map/ppermute | solution.py:346
  512.6 83.8 %collective-permute-start.50 = (bf16[3,1536,384]{2,1,0:T(8,128)(2,1)S(1)}, bf16[3,1536,384]{2,1,0:T(8,128)(2,1)S(1)}, u32[]{:S(2)}, u32[]{:S(2)}) collective-permute-start(bf16[3,1536,384]{2,1,0:T(8,128)(2,1)S(1)} %fusion.1), channel_id=1, source_target_pairs={{2,4},{4,2},{3,5},{5,3},{10,12},{12,10},{11,13},{13,11},{18,20},{2... | collective-permute-start | bytes 10616840 | tf_op jit(solution)/shard_map/ppermute | solution.py:346
  516.9 61.9 %collective-permute-start.37 = (bf16[384,1792]{1,0:T(8,128)(2,1)S(1)}, bf16[384,1792]{1,0:T(8,128)(2,1)S(1)}, u32[]{:S(2)}, u32[]{:S(2)}) collective-permute-start(bf16[384,1792]{1,0:T(8,128)(2,1)S(1)} %get-tuple-element.47), channel_id=1, source_target_pairs={{0,8},{8,0},{16,24},{24,16},{1,9},{9,1},{17,25},{25,17},{2,10},{10... | collective-permute-start | bytes 4128776 | tf_op jit(solution)/shard_map/ppermute | solution.py:326
  548.0 72.4 %collective-permute-start.21 = (bf16[128,1536]{1,0:T(8,128)(2,1)S(1)}, bf16[128,1536]{1,0:T(8,128)(2,1)S(1)}, u32[]{:S(2)}, u32[]{:S(2)}) collective-permute-start(bf16[128,1536]{1,0:T(8,128)(2,1)S(1)} %get-tuple-element.70), channel_id=1, source_target_pairs={{0,24},{8,16},{16,8},{24,0},{1,25},{9,17},{17,9},{25,1},{2,26},{10... | collective-permute-start | bytes 1179656 | tf_op jit(solution)/shard_map/ppermute | solution.py:326
  594.9 180.3 %collective-permute-start.45 = (bf16[3,1536,384]{2,1,0:T(8,128)(2,1)}, bf16[3,1536,384]{2,1,0:T(8,128)(2,1)}, u32[]{:S(2)}, u32[]{:S(2)}) collective-permute-start(bf16[3,1536,384]{2,1,0:T(8,128)(2,1)} %add_convert_fusion.1), channel_id=1, source_target_pairs={{2,0},{4,6},{3,1},{5,7},{10,8},{12,14},{11,9},{13,15},{18,16},{20,... | collective-permute-start | bytes 10616840 | tf_op jit(solution)/shard_map/ppermute | solution.py:348
  600.8 183.5 %collective-permute-start.51 = (bf16[3,1536,384]{2,1,0:T(8,128)(2,1)}, bf16[3,1536,384]{2,1,0:T(8,128)(2,1)}, u32[]{:S(2)}, u32[]{:S(2)}) collective-permute-start(bf16[3,1536,384]{2,1,0:T(8,128)(2,1)} %add_convert_fusion), channel_id=1, source_target_pairs={{2,0},{4,6},{3,1},{5,7},{10,8},{12,14},{11,9},{13,15},{18,16},{20,... | collective-permute-start | bytes 10616840 | tf_op jit(solution)/shard_map/ppermute | solution.py:348
  620.4 151.4 %collective-permute-start.41 = (bf16[384,1792]{1,0:T(8,128)(2,1)S(1)}, bf16[384,1792]{1,0:T(8,128)(2,1)}, u32[]{:S(2)}, u32[]{:S(2)}) collective-permute-start(bf16[384,1792]{1,0:T(8,128)(2,1)S(1)} %fusion.2), channel_id=1, source_target_pairs={{2,4},{4,2},{3,5},{5,3},{10,12},{12,10},{11,13},{13,11},{18,20},{2... | collective-permute-start | bytes 4128776 | tf_op jit(solution)/shard_map/ppermute | solution.py:346
  630.6 140.2 %collective-permute-start.22 = (bf16[128,1536]{1,0:T(8,128)(2,1)S(1)}, bf16[128,1536]{1,0:T(8,128)(2,1)}, u32[]{:S(2)}, u32[]{:S(2)}) collective-permute-start(bf16[128,1536]{1,0:T(8,128)(2,1)S(1)} %get-tuple-element.83), channel_id=1, source_target_pairs={{0,1},{1,0},{2,3},{3,2},{4,5},{5,4},{6,7},{7,6},{8,9},{9,8},{10,11... | collective-permute-start | bytes 1179656 | tf_op jit(solution)/shard_map/ppermute | solution.py:330
  630.7 169.8 %collective-permute-start.36 = (bf16[128,1536]{1,0:T(8,128)(2,1)S(1)}, bf16[128,1536]{1,0:T(8,128)(2,1)}, u32[]{:S(2)}, u32[]{:S(2)}) collective-permute-start(bf16[128,1536]{1,0:T(8,128)(2,1)S(1)} %get-tuple-element.82), channel_id=1, source_target_pairs={{0,1},{1,0},{2,3},{3,2},{4,5},{5,4},{6,7},{7,6},{8,9},{9,8},{10,11... | collective-permute-start | bytes 1179656 | tf_op jit(solution)/shard_map/ppermute | solution.py:330
  807.3 68.8 %collective-permute-start.47 = (bf16[3,384,384]{2,1,0:T(8,128)(2,1)S(1)}, bf16[3,384,384]{2,1,0:T(8,128)(2,1)S(1)}, u32[]{:S(2)}, u32[]{:S(2)}) collective-permute-start(bf16[3,384,384]{2,1,0:T(8,128)(2,1)S(1)} %get-tuple-element.52), channel_id=1, source_target_pairs={{0,16},{8,24},{16,0},{24,8},{1,17},{9,25},{17,1},{25,9},{2,18},{10... | collective-permute-start | bytes 2654216 | tf_op jit(solution)/shard_map/ppermute | solution.py:326
  (97 other events, 1422.4 us)

commit v2 on v1

--- a/solution.py
+++ b/solution.py
@@ -1,6 +1,7 @@
 import jax
 import jax.numpy as jnp
 from jax import lax
+import numpy as np
 from jax.experimental import pallas as pl
 from jax.experimental.pallas import tpu as pltpu
 from jax.sharding import PartitionSpec as P
@@ -417,10 +418,10 @@
     return lax.dot_general(a, b, dims, preferred_element_type=jnp.float32)
 
 
-def block_probs(place_ref, keys, query):
+def block_probs(last, keys, query):
     scores = dot_f32(keys, query, NT) * HEAD_DIM ** (-0.5)
     block = lax.broadcasted_iota(jnp.int32, scores.shape, 0) // query.shape[0]
-    scores = jnp.where(block <= place_ref[0], scores, -1e30)
+    scores = jnp.where(block <= last, scores, -1e30)
     expd = jnp.exp(scores - jnp.max(scores, axis=0, keepdims=True))
     return expd * (1.0 / jnp.sum(expd, axis=0, keepdims=True))
 
@@ -430,7 +431,7 @@
     vals = v_ref[...]
     for g in range(QUERY_PER_GROUP):
         cols = pl.ds(g * HEAD_DIM, HEAD_DIM)
-        probs = block_probs(place_ref, keys, q_ref[:, cols]).astype(jnp.bfloat16)
+        probs = block_probs(place_ref[0], keys, q_ref[:, cols]).astype(jnp.bfloat16)
         out_ref[:, cols] = dot_f32(probs, vals, TN).astype(jnp.bfloat16)
 
 
@@ -444,7 +445,7 @@
         cols = pl.ds(g * HEAD_DIM, HEAD_DIM)
         query = q_ref[:, cols]
         d_mixed = dm_ref[:, cols]
-        probs = block_probs(place_ref, keys, query)
+        probs = block_probs(place_ref[0], keys, query)
         d_probs = dot_f32(vals, d_mixed, NT)
         inner = jnp.sum(probs * d_probs, axis=0, keepdims=True)
         d_scores = (probs * (d_probs - inner)).astype(jnp.bfloat16)
@@ -481,17 +482,12 @@
     )(place, q, k, v, d_mixed)
 
 
-def spread_rows(half):
-    mine = jnp.stack([half] + [from_rel(half, r) for r in range(1, 4)])
-    return jnp.stack([mine, swap_core(mine)])
-
-
-def gather_sum(parts):
-    own, other = parts[0], parts[1].astype(jnp.bfloat16)
+def gather_sum(parts, f, core):
+    own, other = parts[core], parts[1 - core].astype(jnp.bfloat16)
     both = own + swap_core(other).astype(jnp.float32)
-    total = both[0]
+    total = both[f]
     for r in range(1, 4):
-        total = total + from_rel(both[r].astype(jnp.bfloat16), r).astype(jnp.float32)
+        total = total + from_rel(both[f ^ r].astype(jnp.bfloat16), r).astype(jnp.float32)
     return total
 
 
@@ -500,6 +496,299 @@
     first = jnp.where(core == 0, half, other)
     second = jnp.where(core == 0, other, half)
     return jnp.concatenate([first, second], axis=0)
+
+
+def place():
+    return lax.axis_index("fsdp"), lax.axis_index("ctx"), lax.axis_index("tp")
+
+
+def plane_peers(f):
+    return f + 1 - 2 * lax.rem(f, 2), lax.rem(f + 2, 4), 3 - f
+
+
+def rows_of(index, size):
+    return pl.ds(pl.multiple_of(index * size, size), size)
+
+
+def greet(devices):
+    barrier = pltpu.get_barrier_semaphore()
+    for device in devices:
+        pl.semaphore_signal(barrier, inc=1, device_id=device, device_id_type=MESH_ID)
+    pl.semaphore_wait(barrier, len(devices))
+
+
+def turn(value, cosine, sine):
+    return value * cosine + pltpu.roll(value, HEAD_DIM // 2, 1) * sine
+
+
+def front_kernel(
+    tok_ref,
+    gain_one_ref,
+    gain_two_ref,
+    freq_ref,
+    routes_ref,
+    gates_ref,
+    order_ref,
+    attn_hbm,
+    pieces_hbm,
+    cot_hbm,
+    xn_ref,
+    q_ref,
+    kv_ref,
+    mixed_ref,
+    res_ref,
+    wl_ref,
+    wa_hbm,
+    w_hbm,
+    x_hbm,
+    dy_hbm,
+    wa,
+    part,
+    part_in,
+    low_half,
+    send,
+    recv,
+    local,
+):
+    f, z, c = place()
+    fx, fy, fd = plane_peers(f)
+    count, width = tok_ref.shape
+    half = count // 2
+    shard = attn_hbm.shape[0]
+    cut = shard // 2
+    in_cols = (QUERY_PER_GROUP + 2) * HEAD_DIM
+    ins = pl.ds(0, in_cols)
+    outs = pl.ds(in_cols, attn_hbm.shape[1] - in_cols)
+
+    def at(fsdp=f, ctx=z, tp=c):
+        return {"fsdp": fsdp, "ctx": ctx, "tp": tp}
+
+    def remote(src, dst, k, device):
+        return pltpu.make_async_remote_copy(
+            src_ref=src,
+            dst_ref=dst,
+            send_sem=send.at[k],
+            recv_sem=recv.at[k],
+            device_id=device,
+            device_id_type=MESH_ID,
+        )
+
+    plane = [at(fx), at(fy), at(fd)]
+    rel = [fx, fy, fd]
+    line = [at(ctx=lax.rem(z + s, 4)) for s in range(1, 4)]
+    sibling = at(tp=1 - c)
+    greet(plane + line + [sibling])
+
+    mine = rows_of(f, shard)
+    owned = pltpu.make_async_copy(attn_hbm, wa.at[mine], local.at[0])
+    owned.start()
+    in_x = remote(attn_hbm.at[:, ins], wa.at[mine, ins], 0, at(fx))
+    in_y = remote(attn_hbm.at[:, ins], wa.at[mine, ins], 1, at(fy))
+    in_x.start()
+    in_y.start()
+
+    rank = jnp.broadcast_to(order_ref[...].astype(jnp.float32), (count, count))
+    ahead = jnp.where(rank.T < rank, 1.0, 0.0).astype(jnp.bfloat16)
+    expert = lax.broadcasted_iota(jnp.int32, (128, count), 0)
+    member = jnp.zeros((128, count), jnp.float32)
+    gate = jnp.zeros((128, count), jnp.float32)
+    for j in range(TOP):
+        hit = jnp.broadcast_to(routes_ref[j : j + 1, :], (128, count)) == expert
+        member = jnp.where(hit, 1.0, member)
+        gate = jnp.where(hit, jnp.broadcast_to(gates_ref[j : j + 1, :], (128, count)), gate)
+    slots = dot_f32(member.astype(jnp.bfloat16), ahead)
+    gate = jnp.where(slots < CAP - 0.5, gate, 0.0)
+    wl_ref[f] = gate[:EXPERTS]
+    gate_copies = [remote(wl_ref.at[f], wl_ref.at[f], 2 + i, plane[i]) for i in range(3)]
+    for copy in gate_copies:
+        copy.start()
+
+    own_w = pltpu.make_async_copy(pieces_hbm.at[0], w_hbm.at[:, :, mine, :], local.at[1])
+    own_w.start()
+    own_dy = [
+        pltpu.make_async_copy(
+            cot_hbm.at[pl.ds(i * half, half)], dy_hbm.at[i, f], local.at[2 + i]
+        )
+        for i in range(2)
+    ]
+    for copy in own_dy:
+        copy.start()
+
+    tok = tok_ref[...].astype(jnp.float32)
+    inv = lax.rsqrt(jnp.mean(tok * tok, axis=-1, keepdims=True) + eps)
+    xn_ref[...] = (tok * inv * gain_one_ref[...]).astype(jnp.bfloat16)
+    position = z * count + lax.broadcasted_iota(jnp.int32, (count, HEAD_DIM), 0)
+    angle = position.astype(jnp.float32) * freq_ref[...]
+    cosine = jnp.cos(angle)
+    lane = lax.broadcasted_iota(jnp.int32, (count, HEAD_DIM), 1)
+    sine = jnp.where(lane < HEAD_DIM // 2, -jnp.sin(angle), jnp.sin(angle))
+
+    top, low = rows_of(2 * fx, cut), rows_of(2 * fy + 1, cut)
+    in_x.wait_recv()
+    in_xy = remote(wa.at[top, ins], wa.at[top, ins], 5, at(fy))
+    in_xy.start()
+    in_y.wait_recv()
+    in_yx = remote(wa.at[low, ins], wa.at[low, ins], 6, at(fx))
+    in_yx.start()
+    out_x = remote(attn_hbm.at[:, outs], wa.at[mine, outs], 7, at(fx))
+    out_y = remote(attn_hbm.at[:, outs], wa.at[mine, outs], 8, at(fy))
+    out_x.start()
+    out_y.start()
+    owned.wait()
+    in_xy.wait_recv()
+    in_yx.wait_recv()
+
+    normed = xn_ref[...]
+    for h in range(QUERY_PER_GROUP + 2):
+        cols = pl.ds(h * HEAD_DIM, HEAD_DIM)
+        if h % 2 == 0:
+            pair = dot_f32(normed, wa[:, pl.ds(h * HEAD_DIM, 2 * HEAD_DIM)])
+        value = pair[:, (h % 2) * HEAD_DIM : (h % 2 + 1) * HEAD_DIM]
+        if h <= QUERY_PER_GROUP:
+            value = turn(value, cosine, sine)
+        if h < QUERY_PER_GROUP:
+            q_ref[:, cols] = value.astype(jnp.bfloat16)
+        else:
+            kv_ref[0, :, pl.ds((h - QUERY_PER_GROUP) * HEAD_DIM, HEAD_DIM)] = value.astype(
+                jnp.bfloat16
+            )
+    kv_copies = [remote(kv_ref.at[0], kv_ref.at[s], 8 + s, line[s - 1]) for s in range(1, 4)]
+    for s in range(1, 4):
+
+        @pl.when(z + s < 4)
+        def _(s=s):
+            kv_copies[s - 1].start()
+
+        @pl.when(z < s)
+        def _(s=s):
+            kv_ref[s] = jnp.zeros(kv_ref.shape[1:], jnp.bfloat16)
+
+    out_x.wait_recv()
+    out_xy = remote(wa.at[top, outs], wa.at[top, outs], 12, at(fy))
+    out_xy.start()
+    out_y.wait_recv()
+    out_yx = remote(wa.at[low, outs], wa.at[low, outs], 13, at(fx))
+    out_yx.start()
+
+    w_copies = []
+    for m in range(3):
+        for i in range(3):
+            w_copies.append(
+                remote(
+                    pieces_hbm.at[i + 1, :, m], w_hbm.at[:, m, mine, :], 14 + 3 * m + i, plane[i]
+                )
+            )
+    for copy in w_copies:
+        copy.start()
+    dy_copies = [
+        remote(cot_hbm.at[rows_of(c, half)], dy_hbm.at[c, f], 23 + i, plane[i]) for i in range(3)
+    ]
+    for copy in dy_copies:
+        copy.start()
+
+    for s in range(1, 4):
+
+        @pl.when(z >= s)
+        def _(s=s):
+            kv_copies[s - 1].wait_recv()
+
+    keys = kv_ref[:, :, pl.ds(0, HEAD_DIM)].reshape(4 * count, HEAD_DIM)
+    vals = kv_ref[:, :, pl.ds(HEAD_DIM, HEAD_DIM)].reshape(4 * count, HEAD_DIM)
+    for g in range(QUERY_PER_GROUP):
+        cols = pl.ds(g * HEAD_DIM, HEAD_DIM)
+        probs = block_probs(z, keys, q_ref[:, cols]).astype(jnp.bfloat16)
+        mixed_ref[:, cols] = dot_f32(probs, vals, TN).astype(jnp.bfloat16)
+
+    out_xy.wait_recv()
+    out_yx.wait_recv()
+    store_wa = pltpu.make_async_copy(wa, wa_hbm, local.at[4])
+    store_wa.start()
+    for s in range(width // 256):
+        cols = pl.ds(s * 256, 256)
+        part[:, cols] = dot_f32(mixed_ref[...], wa[cols, outs], NT)
+    swap = remote(part.at[rows_of(1 - c, half)], part_in, 26, sibling)
+    swap.start()
+    swap.wait_recv()
+    my_rows = rows_of(c, half)
+    residual = tok_ref[my_rows, :].astype(jnp.float32) + (part[my_rows, :] + part_in[...])
+    res_ref[...] = residual
+    inv = lax.rsqrt(jnp.mean(residual * residual, axis=-1, keepdims=True) + eps)
+    low_half[...] = (residual * inv * gain_two_ref[...]).astype(jnp.bfloat16)
+    own_x = pltpu.make_async_copy(low_half, x_hbm.at[c, f], local.at[5])
+    own_x.start()
+    x_copies = [remote(low_half, x_hbm.at[c, f], 27 + i, plane[i]) for i in range(3)]
+    for copy in x_copies:
+        copy.start()
+    sib_x = [remote(low_half, x_hbm.at[c, f], 30, sibling)]
+    sib_x[0].start()
+
+    sib_dy = []
+    for i in range(3):
+        dy_copies[i].wait_recv()
+        sib_dy.append(remote(dy_hbm.at[c, rel[i]], dy_hbm.at[c, rel[i]], 31 + i, sibling))
+        sib_dy[i].start()
+    for i in range(3):
+        x_copies[i].wait_recv()
+        sib_x.append(remote(x_hbm.at[c, rel[i]], x_hbm.at[c, rel[i]], 34 + i, sibling))
+        sib_x[i + 1].start()
+
+    for copy in w_copies + gate_copies + sib_dy + sib_x:
+        copy.wait_recv()
+    for s in range(1, 4):
+
+        @pl.when(z + s < 4)
+        def _(s=s):
+            kv_copies[s - 1].wait_send()
+
+    for copy in [in_x, in_y, in_xy, in_yx, out_x, out_y, out_xy, out_yx, swap]:
+        copy.wait_send()
+    for copy in w_copies + gate_copies + dy_copies + x_copies + sib_dy + sib_x:
+        copy.wait_send()
+    for copy in [own_w, own_x, store_wa] + own_dy:
+        copy.wait()
+
+
+def front(tok, gain_one, gain_two, routes, gates, order, attn_own, pieces, cot):
+    count, width = tok.shape
+    half = count // 2
+    shard, columns = attn_own.shape
+    experts, hidden = pieces.shape[1], pieces.shape[4]
+    i = np.arange(HEAD_DIM // 2, dtype=np.float32)
+    freq = (theta_base ** (-(i * 2.0) / HEAD_DIM)).astype(np.float32)
+    freq = jnp.asarray(np.concatenate([freq, freq])[None, :])
+    vmem, hbm = pl.BlockSpec(memory_space=pltpu.VMEM), pl.BlockSpec(memory_space=pl.ANY)
+    bf16, f32 = jnp.bfloat16, jnp.float32
+    shape = jax.ShapeDtypeStruct
+    return pl.pallas_call(
+        front_kernel,
+        in_specs=[vmem] * 7 + [hbm] * 3,
+        out_specs=[vmem] * 6 + [hbm] * 4,
+        out_shape=[
+            shape((count, width), bf16),
+            shape((count, QUERY_PER_GROUP * HEAD_DIM), bf16),
+            shape((4, count, 2 * HEAD_DIM), bf16),
+            shape((count, QUERY_PER_GROUP * HEAD_DIM), bf16),
+            shape((half, width), f32),
+            shape((4, EXPERTS, count), f32),
+            shape((4 * shard, columns), bf16),
+            shape((experts, 3, 4 * shard, hidden), bf16),
+            shape((2, 4, half, width), bf16),
+            shape((2, 4, half, width), bf16),
+        ],
+        scratch_shapes=[
+            pltpu.VMEM((4 * shard, columns), bf16),
+            pltpu.VMEM((count, width), f32),
+            pltpu.VMEM((half, width), f32),
+            pltpu.VMEM((half, width), bf16),
+            pltpu.SemaphoreType.DMA((37,)),
+            pltpu.SemaphoreType.DMA((37,)),
+            pltpu.SemaphoreType.DMA((6,)),
+        ],
+        compiler_params=pltpu.CompilerParams(
+            collective_id=0, has_side_effects=True, vmem_limit_bytes=48 * MIB
+        ),
+        name="front",
+    )(tok, gain_one, gain_two, freq, routes, gates, order, attn_own, pieces, cot)
 
 
 def body_fast(
@@ -528,66 +817,43 @@
     def my_half(value):
         return lax.dynamic_slice_in_dim(value, core * half, half, 0)
 
-    attn_own = attention_params[:, 0, :]
-    attn_x, attn_y = from_rel(attn_own, 1), from_rel(attn_own, 2)
-    cut = shard // 2
-    attn_d = jnp.concatenate([from_rel(attn_x[:cut], 2), from_rel(attn_y[cut:], 1)], axis=0)
     place_order = jnp.arange(4, dtype=jnp.int32) ^ f
-    whole_attn = jnp.stack([attn_own, attn_x, attn_y, attn_d])[place_order].reshape(
-        4 * shard, attention_params.shape[2]
-    )
-    attn_in, attn_out = whole_attn[:, :input_columns], whole_attn[:, input_columns:]
-
     order = expert_order(f)
     pieces = split_experts(jnp.transpose(expert_weights, (0, 2, 1, 3)), order)
-    pieces = pieces.reshape(4, own_experts, 3, shard, expert_weights.shape[3])
-    arrived = [pieces[0]] + [from_rel(pieces[r], r) for r in range(1, 4)]
-    whole_expert = jnp.stack(arrived, axis=2)
-    whole_expert = jnp.take(whole_expert, place_order, axis=2).reshape(
-        own_experts, 3, 4 * shard, expert_weights.shape[3]
-    )
-
-    route_rows, rank_rows = routes.reshape(count, TOP), slot_order.reshape(count)
-    gates = gate_values.reshape(count, TOP)
-    chosen = route_rows[:, :, None] == jnp.arange(EXPERTS, dtype=jnp.int32)
-    member = jnp.any(chosen, axis=1)
-    ahead = rank_rows[None, :] < rank_rows[:, None]
-    slots = dot_f32(ahead.astype(bf16), member.astype(bf16))
-    kept = member & (slots < CAP - 0.5)
-    weight = jnp.sum(jnp.where(chosen, gates[:, :, None], 0.0), axis=1) * kept.astype(f32)
-    weight_rows = weight.T.reshape(4, own_experts, 2, half)
-    weight_rows = weight_rows[place_order]
-    weights_in = jnp.stack(
-        [weight_rows[0]] + [from_rel(weight_rows[r], r) for r in range(1, 4)]
-    )
-    weights_in = jnp.where(core == 0, weights_in, weights_in[:, :, ::-1])
-    weights_in = jnp.transpose(weights_in, (1, 2, 0, 3)).reshape(own_experts, 8 * half)
-
+    pieces = jnp.transpose(
+        pieces.reshape(4, own_experts, 3, shard, expert_weights.shape[3]), (0, 1, 2, 3, 4)
+    )
+    tok_low = tokens.reshape(count, model_width)
+    grad_out = cotangent.reshape(count, model_width)
+    first_normed, queries, kv_all, mixed, residual, gate_table, whole_attn, whole_expert, x, dy = front(
+        tok_low,
+        attn_norm[None, :],
+        ffn_norm[None, :],
+        routes.reshape(count, TOP).T,
+        gate_values.reshape(count, TOP).T,
+        slot_order.reshape(1, count),
+        attention_params[:, 0, :],
+        pieces,
+        grad_out,
+    )
+    inputs = x.reshape(8 * half, model_width)
+    upstream = dy.reshape(8 * half, model_width)
+    attn_in, attn_out = whole_attn[:, :input_columns], whole_attn[:, input_columns:]
+    weights_in = lax.dynamic_slice_in_dim(gate_table, f * own_experts, own_experts, 1)
+    weights_in = jnp.transpose(weights_in.reshape(4, own_experts, 2, half), (1, 2, 0, 3))
+    weights_in = weights_in.reshape(own_experts, 8 * half)
+    kept = gate_table[f].T != 0.0
+    route_rows = routes.reshape(count, TOP)
+    kv_all = kv_all.reshape(4 * count, 2 * HEAD_DIM)
+    key_all, value_all = kv_all[:, :HEAD_DIM], kv_all[:, HEAD_DIM:]
+    tok_float = tok_low.astype(f32)
+    inv_one = lax.rsqrt(jnp.mean(tok_float * tok_float, axis=-1, keepdims=True) + eps)
+    inv_two = lax.rsqrt(jnp.mean(residual * residual, axis=-1, keepdims=True) + eps)
     positions = z * block_len + jnp.arange(block_len, dtype=jnp.int32)
     cosine, sine = angle_tables(positions)
     cos_three, sin_three = cosine[:, None, :], sine[:, None, :]
-    tok_float = tokens.reshape(count, model_width).astype(f32)
-    inv_one = lax.rsqrt(jnp.mean(tok_float * tok_float, axis=-1, keepdims=True) + eps)
-    first_normed = (tok_float * inv_one * attn_norm).astype(bf16)
-    projected = dot_f32(first_normed, attn_in).reshape(count, QUERY_PER_GROUP + 2, HEAD_DIM)
-    turned = rotate(projected[:, : QUERY_PER_GROUP + 1], cos_three, sin_three).astype(bf16)
-    queries = turned[:, :QUERY_PER_GROUP].reshape(count, query_columns)
-    key_value = jnp.concatenate(
-        [turned[:, QUERY_PER_GROUP], projected[:, QUERY_PER_GROUP + 1].astype(bf16)], axis=1
-    )
-    kv_all = jnp.concatenate([key_value] + [shift_ctx(key_value, s) for s in range(1, 4)], axis=0)
-    key_all, value_all = kv_all[:, :HEAD_DIM], kv_all[:, HEAD_DIM:]
     place = jnp.reshape(z, (1,)).astype(jnp.int32)
-    mixed = attend(place, queries, key_all, value_all)
-    attn_part = dot_f32(mixed, attn_out, NT)
-    other_rows = lax.dynamic_slice_in_dim(attn_part, (1 - core) * half, half, 0)
-    residual = my_half(tok_float) + (my_half(attn_part) + swap_core(other_rows))
-    inv_two = lax.rsqrt(jnp.mean(residual * residual, axis=-1, keepdims=True) + eps)
-    normed_two = (residual * inv_two * ffn_norm).astype(bf16)
-
-    grad_out = cotangent.reshape(count, model_width)
-    inputs = spread_rows(normed_two).reshape(8 * half, model_width)
-    upstream = spread_rows(my_half(grad_out)).reshape(8 * half, model_width)
+
     moe_parts = 0.0
     d_normed_parts = 0.0
     gate_parts = []
@@ -621,14 +887,14 @@
                 ]
             )
         )
-    d_normed_two = gather_sum(d_normed_parts.reshape(2, 4, half, model_width))
-    moe = gather_sum(moe_parts.reshape(2, 4, half, model_width))
+    d_normed_two = gather_sum(d_normed_parts.reshape(2, 4, half, model_width), f, core)
+    moe = gather_sum(moe_parts.reshape(2, 4, half, model_width), f, core)
     layer_out = join_halves(core, (residual + moe).astype(bf16))
 
     gate_rows = jnp.stack(gate_parts).reshape(own_experts, 2, 4, half)
-    gate_rows = gate_rows[:, 0] + swap_core(gate_rows[:, 1])
+    gate_rows = jnp.take(gate_rows, core, 1) + swap_core(jnp.take(gate_rows, 1 - core, 1))
     gate_rows = jnp.stack(
-        [gate_rows[:, 0]] + [from_rel(gate_rows[:, r], r) for r in range(1, 4)]
+        [gate_rows[:, f]] + [from_rel(gate_rows[:, f ^ r], r) for r in range(1, 4)]
     )
     gate_rows = join_halves(core, gate_rows.reshape(EXPERTS, half).T)
     rel_ids = (place_order[:, None] * own_experts + jnp.arange(own_experts)).reshape(EXPERTS)
@@ -655,7 +921,10 @@
     d_normed_one = my_half(d_normed_local) + swap_core(other_rows.astype(bf16)).astype(f32)
     d_tok_norm, gain_one = norm_back(my_half(tok_float), my_half(inv_one), attn_norm, d_normed_one)
     tokens_grad = join_halves(core, (d_residual + d_tok_norm).astype(bf16))
-    gains = lax.psum(jnp.stack([gain_one, gain_two]), ("fsdp", "ctx", "tp"))
+    gains = jnp.stack([gain_one, gain_two])
+    gains = gains + swap_core(gains)
+    for axis, r in (("fsdp", 1), ("fsdp", 2), ("ctx", 1), ("ctx", 2)):
+        gains = gains + lax.ppermute(gains, axis, rel_perm(4, r))
 
     attn_grad = jnp.concatenate(
         [dot_f32(first_normed, d_projected, TN), dot_f32(d_attn, mixed, TN)], axis=1

time: 891 us -> 822 us (0.923)
  Pallas kernels: 21.8 us -> 184 us
  blocking collectives: 139 us -> 0 us
  waiting for transfers between devices: 380 us -> 333 us
  local copies, waits for them, and re-layouts: 93.3 us -> 57.6 us
  matrix products: 58.4 us -> 88.6 us
  other arithmetic: 102 us -> 77.4 us
  starting transfers between devices: 88.9 us -> 76.4 us
    pallas_call x1, Pallas kernels: 3.83 us -> 165 us  [front(): pl.pallas_call(front_kernel, in_specs=[vmem] * 7 + [hbm] * 3, out_specs=[...]
    ppermute x34 -> x18, waiting for transfers between devices: 283 us -> 144 us  [from_rel(): return lax.ppermute(value, 'fsdp', rel_perm(lax.axis_size('fsdp'), r))]
    psum x1 -> x0, blocking collectives: 139 us -> none  [body_fast(): gains = lax.psum(jnp.stack([gain_one, gain_two]), ('fsdp', 'ctx', 'tp'))]
    ppermute x0 -> x4, waiting for transfers between devices: none -> 108 us  [body_fast(): gains = gains + lax.ppermute(gains, axis, rel_perm(4, r))]
    dot_general x25 -> x22, matrix products: 58.4 us -> 88.6 us  [dot_f32(): return lax.dot_general(a, b, dims, preferred_element_type=jnp.float32)]
    ppermute x34 -> x18, starting transfers between devices: 47.9 us -> 21.3 us  [from_rel(): return lax.ppermute(value, 'fsdp', rel_perm(lax.axis_size('fsdp'), r))]
    ppermute x0 -> x4, starting transfers between devices: none -> 25.7 us  [body_fast(): gains = gains + lax.ppermute(gains, axis, rel_perm(4, r))]
    another operation x17 -> x5, other arithmetic: 29.1 us -> 5.62 us  [the longest x4 10.2 us: spread_rows(): return jnp.stack([mine, swap_core(mine)])]
  transfers between devices with their start and end apart: 60 -> 43, of which waited for: 30 -> 17; matrix products, arithmetic and copies ran while one was open for 22% -> 19% of each run, Pallas kernels for 2% -> 1%
where the time goes in v2:
time: 822 us; the launch traced here: 818 us
  waiting for transfers between devices  333 us (41%)
  Pallas kernels  184 us (22%)
  matrix products  88.6 us (11%)
  other arithmetic  77.4 us (9%)
  starting transfers between devices  76.4 us (9%)
  local copies, waits for them, and re-layouts  57.6 us (7%)
    pallas_call x1, Pallas kernels, front(): pl.pallas_call(front_kernel, in_specs=[vmem] * 7 + [hbm] * 3, out_specs=[...  165 us
    ppermute x18, waiting for transfers between devices, from_rel(): return lax.ppermute(value, 'fsdp', rel_perm(lax.axis_size('fsdp'), r))  144 us
    ppermute x4, waiting for transfers between devices, body_fast(): gains = gains + lax.ppermute(gains, axis, rel_perm(4, r))  108 us
    dot_general x22, matrix products, dot_f32(): return lax.dot_general(a, b, dims, preferred_element_type=jnp.float32)  88.6 us
    ppermute x3, waiting for transfers between devices, shift_ctx(): return lax.ppermute(value, 'ctx', pairs)  63.3 us
    ppermute x4, starting transfers between devices, body_fast(): gains = gains + lax.ppermute(gains, axis, rel_perm(4, r))  25.7 us
    ppermute x18, starting transfers between devices, from_rel(): return lax.ppermute(value, 'fsdp', rel_perm(lax.axis_size('fsdp'), r))  21.3 us
  transfers between devices with their start and end apart: 43, of which 17 were waited for; matrix products, arithmetic and copies ran while one was open for 19% of the time, Pallas kernels for 1%

profile of v2, /device:TPU:0, one launch (start us, length us, event | category | flops | bytes accessed | tf_op | source)
XLA Modules:
  0.0 818.2 jit_solution(4724140381382379824)
XLA Ops:
  11.7 165.5 %front.1 = (bf16[256,1536]{1,0:T(8,128)(2,1)S(1)}, bf16[256,768]{1,0:T(8,128)(2,1)S(1)}, bf16[4,256,256]{2,1,0:T(8,128)(2,1)S(1)}, bf16[256,768]{1,0:T(8,128)(2,...) custom-call(bf16[256,1536]{1,0:T(8,128)(2,1)S(1)} %bitcast.234, ...), custom_call_target="tpu_custom_call" | custom-call | tf_op jit(solution)/shard_map/front/pallas_call | solution.py:762
  191.4 6.5 multiply_reduce_fusion
  197.9 6.6 fusion.30
  209.0 6.4 fusion.42
  221.0 8.9 %add_add_fusion = f32[1024,1536]{1,0:T(8,128)S(1)} fusion(f32[1024,1536]{1,0:T(8,128)} %fusion.30, f32[1024,1536]{1,0:T(8,128)} %fusion.42, f32[1024,1536]{1,0:T(8,128)} %fusion.38, bf16[1024,384]{0,1:T(8,128)(2,1)} %get-tuple-element.94, bf16[2,3,1536,384]{3,2,1,0:T(8,128)(2,1)} %get-tuple-element.24), kind=kOutput, calls=%fused_computation.12 | convolution fusion | flops 1212678144 | bytes 27131904 | tf_op jit(solution)/shard_map/dot_general | solution.py:418
  286.4 7.3 collective-permute-done.8
  295.2 6.9 collective-permute-done.7
  304.5 6.1 collective-permute-done.3
  310.6 7.9 collective-permute-done.2
  332.8 7.8 attend_back.1
  348.1 63.3 %collective-permute-done.12 = bf16[256,256]{1,0:T(8,128)(2,1)S(1)} collective-permute-done((bf16[256,256]{1,0:T(8,128)(2,1)S(1)}, bf16[256,256]{1,0:T(8,128)(2,1)S(1)}, u32[]{:S(2)}, u32[]{:S(2)}) %collective-permute-start.12) | collective-permute-done | bytes 131104 | tf_op jit(solution)/shard_map/ppermute | solution.py:337
  427.0 9.5 %pad_maximum_fusion = f32[1536,1792]{0,1:T(8,128)} fusion(f32[1536,768]{0,1:T(8,128)} %fusion.64, f32[1536,1024]{0,1:T(8,128)} %fusion.71), kind=kLoop, calls=%fused_computation.4 | loop fusion | flops 2752512 | bytes 22020096 | tf_op jit(solution)/shard_map/concatenate | solution.py:929
  436.5 12.1 %copy.44 = f32[1536,1792]{1,0:T(8,128)} copy(f32[1536,1792]{0,1:T(8,128)} %pad_maximum_fusion) | data formatting | bytes 22020096 | tf_op jit(solution)/shard_map/reshape | solution.py:931
  448.7 9.8 %gather_fusion = f32[4,384,1792]{2,1,0:T(8,128)} fusion(f32[4,384,1792]{2,1,0:T(8,128)} %bitcast.241, s32[1024]{0:T(1024)} %get-tuple-element.130), kind=kCustom, calls=%fused_computation.2 | custom fusion | bytes 22020112 | tf_op jit(solution)/shard_map/gather | solution.py:929
  480.9 25.7 %collective-permute-done.17 = bf16[384,1792]{1,0:T(8,128)(2,1)} collective-permute-done((bf16[384,1792]{1,0:T(8,128)(2,1)}, bf16[384,1792]{1,0:T(8,128)(2,1)}, u32[]{:S(2)}, u32[]{:S(2)}) %collective-permute-start.17) | collective-permute-done | bytes 1376288 | tf_op jit(solution)/shard_map/ppermute | solution.py:327
  506.6 28.5 %collective-permute-done.16 = bf16[384,1792]{1,0:T(8,128)(2,1)} collective-permute-done((bf16[384,1792]{1,0:T(8,128)(2,1)}, bf16[384,1792]{1,0:T(8,128)(2,1)}, u32[]{:S(2)}, u32[]{:S(2)}) %collective-permute-start.16) | collective-permute-done | bytes 1376288 | tf_op jit(solution)/shard_map/ppermute | solution.py:327
  558.1 16.1 %collective-permute-done.18 = bf16[384,1792]{1,0:T(8,128)(2,1)S(1)} collective-permute-done((bf16[384,1792]{1,0:T(8,128)(2,1)S(1)}, bf16[384,1792]{1,0:T(8,128)(2,1)S(1)}, u32[]{:S(2)}, u32[]{:S(2)}) %collective-permute-start.18) | collective-permute-done | bytes 1376288 | tf_op jit(solution)/shard_map/ppermute | solution.py:343
  579.2 22.8 %collective-permute-start.36 = (f32[2,1536]{1,0:T(2,128)S(1)}, f32[2,1536]{1,0:T(2,128)S(1)}, u32[]{:S(2)}, u32[]{:S(2)}) collective-permute-start(f32[2,1536]{1,0:T(2,128)S(1)} %add.349), channel_id=1, source_target_pairs={{0,2},{2,0},{4,6},{6,4},{1,3},{3,1},{5,7},{7,5},{8,10},{10,8},{12,... | collective-permute-start | bytes 36872 | tf_op jit(solution)/shard_map/ppermute | solution.py:927
  602.0 102.9 %collective-permute-done.36 = f32[2,1536]{1,0:T(2,128)S(1)} collective-permute-done((f32[2,1536]{1,0:T(2,128)S(1)}, f32[2,1536]{1,0:T(2,128)S(1)}, u32[]{:S(2)}, u32[]{:S(2)}) %collective-permute-start.36) | collective-permute-done | bytes 12320 | tf_op jit(solution)/shard_map/ppermute | solution.py:927
  743.5 12.6 %collective-permute-done.32 = bf16[3,384,384]{2,1,0:T(8,128)(2,1)S(1)} collective-permute-done((bf16[3,384,384]{2,1,0:T(8,128)(2,1)S(1)}, bf16[3,384,384]{2,1,0:T(8,128)(2,1)S(1)}, u32[]{:S(2)}, u32[]{:S(2)}) %collective-permute-start.32) | collective-permute-done | bytes 884768 | tf_op jit(solution)/shard_map/ppermute | solution.py:327
  761.7 13.4 %collective-permute-done.31 = bf16[3,384,384]{2,1,0:T(8,128)(2,1)S(1)} collective-permute-done((bf16[3,384,384]{2,1,0:T(8,128)(2,1)S(1)}, bf16[3,384,384]{2,1,0:T(8,128)(2,1)S(1)}, u32[]{:S(2)}, u32[]{:S(2)}) %collective-permute-start.31) | collective-permute-done | bytes 884768 | tf_op jit(solution)/shard_map/ppermute | solution.py:327
  775.7 18.4 %collective-permute-done.26 = bf16[3,384,384]{2,1,0:T(8,128)(2,1)S(1)} collective-permute-done((bf16[3,384,384]{2,1,0:T(8,128)(2,1)}, bf16[3,384,384]{2,1,0:T(8,128)(2,1)S(1)}, u32[]{:S(2)}, u32[]{:S(2)}) %collective-permute-start.26) | collective-permute-done | bytes 884768 | tf_op jit(solution)/shard_map/ppermute | solution.py:327
  794.1 15.8 %collective-permute-done.25 = bf16[3,384,384]{2,1,0:T(8,128)(2,1)S(1)} collective-permute-done((bf16[3,384,384]{2,1,0:T(8,128)(2,1)S(1)}, bf16[3,384,384]{2,1,0:T(8,128)(2,1)S(1)}, u32[]{:S(2)}, u32[]{:S(2)}) %collective-permute-start.25) | collective-permute-done | bytes 884768 | tf_op jit(solution)/shard_map/ppermute | solution.py:327
  811.2 6.8 join_experts.1
  (327 shorter events, 228.7 us)
Async XLA Ops:
  231.3 46.9 %collective-permute-start.5 = (bf16[4,128,1536]{2,1,0:T(8,128)(2,1)}, bf16[4,128,1536]{2,1,0:T(8,128)(2,1)}, u32[]{:S(2)}, u32[]{:S(2)}) collective-permute-start(bf16[4,128,1536]{2,1,0:T(8,128)(2,1)} %fusion.18), channel_id=1, source_target_pairs={{0,1},{1,0},{2,3},{3,2},{4,5},{5,4},{6,7},{7,6},{8,9},{9,8},{10,11... | collective-permute-start | bytes 4718600 | tf_op jit(solution)/shard_map/ppermute | solution.py:331
  240.5 42.8 %collective-permute-start = (bf16[4,128,1536]{2,1,0:T(8,128)(2,1)}, bf16[4,128,1536]{2,1,0:T(8,128)(2,1)}, u32[]{:S(2)}, u32[]{:S(2)}) collective-permute-start(bf16[4,128,1536]{2,1,0:T(8,128)(2,1)} %fusion.17), channel_id=1, source_target_pairs={{0,1},{1,0},{2,3},{3,2},{4,5},{5,4},{6,7},{7,6},{8,9},{9,8},{10,11... | collective-permute-start | bytes 4718600 | tf_op jit(solution)/shard_map/ppermute | solution.py:331
  251.3 169.2 %collective-permute-start.21 = (bf16[3,1536,384]{2,1,0:T(8,128)(2,1)}, bf16[3,1536,384]{2,1,0:T(8,128)(2,1)}, u32[]{:S(2)}, u32[]{:S(2)}) collective-permute-start(bf16[3,1536,384]{2,1,0:T(8,128)(2,1)} %pad_maximum_fusion.2), channel_id=1, source_target_pairs={{0,2},{6,4},{1,3},{7,5},{8,10},{14,12},{9,11},{15,13},{16,18},{22,... | collective-permute-start | bytes 10616840 | tf_op jit(solution)/shard_map/ppermute | solution.py:343
  256.1 64.0 %collective-permute-start.38 = (f32[2,4,128]{2,1,0:T(4,128)}, f32[2,4,128]{2,1,0:T(4,128)}, u32[]{:S(2)}, u32[]{:S(2)}) collective-permute-start(f32[2,4,128]{2,1,0:T(4,128)} %fusion.80), channel_id=1, source_target_pairs={{0,1},{1,0},{2,3},{3,2},{4,5},{5,4},{6,7},{7,6},{8,9},{9,8},{10,11... | collective-permute-start | bytes 12296 | tf_op jit(solution)/shard_map/ppermute | solution.py:331
  325.4 137.9 %collective-permute-start.27 = (bf16[3,1536,384]{2,1,0:T(8,128)(2,1)}, bf16[3,1536,384]{2,1,0:T(8,128)(2,1)}, u32[]{:S(2)}, u32[]{:S(2)}) collective-permute-start(bf16[3,1536,384]{2,1,0:T(8,128)(2,1)} %pad_maximum_fusion.3), channel_id=1, source_target_pairs={{0,2},{6,4},{1,3},{7,5},{8,10},{14,12},{9,11},{15,13},{16,18},{22,... | collective-permute-start | bytes 10616840 | tf_op jit(solution)/shard_map/ppermute | solution.py:343
  340.8 70.6 %collective-permute-start.12 = (bf16[256,256]{1,0:T(8,128)(2,1)S(1)}, bf16[256,256]{1,0:T(8,128)(2,1)S(1)}, u32[]{:S(2)}, u32[]{:S(2)}) collective-permute-start(bf16[256,256]{1,0:T(8,128)(2,1)S(1)} %get-tuple-element.111), channel_id=1, source_target_pairs={{6,0},{7,1},{14,8},{15,9},{22,16},{23,17},{30,24},{31,25}} | collective-permute-start | bytes 393224 | tf_op jit(solution)/shard_map/ppermute | solution.py:337
  342.1 69.3 %collective-permute-start.11 = (bf16[256,256]{1,0:T(8,128)(2,1)S(1)}, bf16[256,256]{1,0:T(8,128)(2,1)S(1)}, u32[]{:S(2)}, u32[]{:S(2)}) collective-permute-start(bf16[256,256]{1,0:T(8,128)(2,1)S(1)} %get-tuple-element.112), channel_id=1, source_target_pairs={{4,0},{6,2},{5,1},{7,3},{12,8},{14,10},{13,9},{15,11},{20,16},{22,... | collective-permute-start | bytes 393224 | tf_op jit(solution)/shard_map/ppermute | solution.py:337
  343.4 68.5 %collective-permute-start.10 = (bf16[256,256]{1,0:T(8,128)(2,1)S(1)}, bf16[256,256]{1,0:T(8,128)(2,1)S(1)}, u32[]{:S(2)}, u32[]{:S(2)}) collective-permute-start(bf16[256,256]{1,0:T(8,128)(2,1)S(1)} %get-tuple-element.110), channel_id=1, source_target_pairs={{2,0},{4,2},{6,4},{3,1},{5,3},{7,5},{10,8},{12,10},{14,12},{11,9},... | collective-permute-start | bytes 393224 | tf_op jit(solution)/shard_map/ppermute | solution.py:337
  411.4 60.9 %collective-permute-start.42 = (f32[128,8]{0,1:T(8,128)}, f32[128,8]{0,1:T(8,128)S(1)}, u32[]{:S(2)}, u32[]{:S(2)}) collective-permute-start(f32[128,8]{0,1:T(8,128)} %bitcast.92), channel_id=1, source_target_pairs={{0,1},{1,0},{2,3},{3,2},{4,5},{5,4},{6,7},{7,6},{8,9},{9,8},{10,11... | collective-permute-start | bytes 12296 | tf_op jit(solution)/shard_map/ppermute | solution.py:331
  411.4 62.3 %collective-permute-start.4 = (bf16[128,1536]{1,0:T(8,128)(2,1)}, bf16[128,1536]{1,0:T(8,128)(2,1)}, u32[]{:S(2)}, u32[]{:S(2)}) collective-permute-start(bf16[128,1536]{1,0:T(8,128)(2,1)} %get-tuple-element.107), channel_id=1, source_target_pairs={{0,1},{1,0},{2,3},{3,2},{4,5},{5,4},{6,7},{7,6},{8,9},{9,8},{10,11... | collective-permute-start | bytes 1179656 | tf_op jit(solution)/shard_map/ppermute | solution.py:331
  415.8 58.9 %collective-permute-start.13 = (bf16[128,1536]{1,0:T(8,128)(2,1)S(1)}, bf16[128,1536]{1,0:T(8,128)(2,1)S(1)}, u32[]{:S(2)}, u32[]{:S(2)}) collective-permute-start(bf16[128,1536]{1,0:T(8,128)(2,1)S(1)} %dynamic-slice_convert_fusion.2), channel_id=1, source_target_pairs={{0,1},{1,0},{2,3},{3,2},{4,5},{5,4},{6,7},{7,6},{8,9},{9,8},{10,11... | collective-permute-start | bytes 1179656 | tf_op jit(solution)/shard_map/ppermute | solution.py:331
  424.5 120.2 %collective-permute-start.22 = (bf16[3,1536,384]{2,1,0:T(8,128)(2,1)}, bf16[3,1536,384]{2,1,0:T(8,128)(2,1)}, u32[]{:S(2)}, u32[]{:S(2)}) collective-permute-start(bf16[3,1536,384]{2,1,0:T(8,128)(2,1)} %fusion), channel_id=1, source_target_pairs={{2,4},{4,2},{3,5},{5,3},{10,12},{12,10},{11,13},{13,11},{18,20},{2... | collective-permute-start | bytes 10616840 | tf_op jit(solution)/shard_map/ppermute | solution.py:347
  467.5 82.7 %collective-permute-start.28 = (bf16[3,1536,384]{2,1,0:T(8,128)(2,1)}, bf16[3,1536,384]{2,1,0:T(8,128)(2,1)}, u32[]{:S(2)}, u32[]{:S(2)}) collective-permute-start(bf16[3,1536,384]{2,1,0:T(8,128)(2,1)} %fusion.1), channel_id=1, source_target_pairs={{2,4},{4,2},{3,5},{5,3},{10,12},{12,10},{11,13},{13,11},{18,20},{2... | collective-permute-start | bytes 10616840 | tf_op jit(solution)/shard_map/ppermute | solution.py:347
  473.7 61.3 %collective-permute-start.16 = (bf16[384,1792]{1,0:T(8,128)(2,1)}, bf16[384,1792]{1,0:T(8,128)(2,1)}, u32[]{:S(2)}, u32[]{:S(2)}) collective-permute-start(bf16[384,1792]{1,0:T(8,128)(2,1)} %get-tuple-element.78), channel_id=1, source_target_pairs={{0,16},{8,24},{16,0},{24,8},{1,17},{9,25},{17,1},{25,9},{2,18},{10... | collective-permute-start | bytes 4128776 | tf_op jit(solution)/shard_map/ppermute | solution.py:327
  474.7 60.3 %collective-permute-start.15 = (bf16[384,1792]{1,0:T(8,128)(2,1)}, bf16[384,1792]{1,0:T(8,128)(2,1)}, u32[]{:S(2)}, u32[]{:S(2)}) collective-permute-start(bf16[384,1792]{1,0:T(8,128)(2,1)} %get-tuple-element.76), channel_id=1, source_target_pairs={{0,8},{8,0},{16,24},{24,16},{1,9},{9,1},{17,25},{25,17},{2,10},{10... | collective-permute-start | bytes 4128776 | tf_op jit(solution)/shard_map/ppermute | solution.py:327
  506.6 50.4 %collective-permute-start.33 = (f32[2,1536]{1,0:T(2,128)S(1)}, f32[2,1536]{1,0:T(2,128)S(1)}, u32[]{:S(2)}, u32[]{:S(2)}) collective-permute-start(f32[2,1536]{1,0:T(2,128)S(1)} %pad_maximum_fusion.12), channel_id=1, source_target_pairs={{0,1},{1,0},{2,3},{3,2},{4,5},{5,4},{6,7},{7,6},{8,9},{9,8},{10,11... | collective-permute-start | bytes 36872 | tf_op jit(solution)/shard_map/ppermute | solution.py:331
  548.7 163.1 %collective-permute-start.23 = (bf16[3,1536,384]{2,1,0:T(8,128)(2,1)S(1)}, bf16[3,1536,384]{2,1,0:T(8,128)(2,1)S(1)}, u32[]{:S(2)}, u32[]{:S(2)}) collective-permute-start(bf16[3,1536,384]{2,1,0:T(8,128)(2,1)S(1)} %add_convert_fusion.1), channel_id=1, source_target_pairs={{2,0},{4,6},{3,1},{5,7},{10,8},{12,14},{11,9},{13,15},{18,16},{20,... | collective-permute-start | bytes 10616840 | tf_op jit(solution)/shard_map/ppermute | solution.py:349
  555.4 163.6 %collective-permute-start.29 = (bf16[3,1536,384]{2,1,0:T(8,128)(2,1)}, bf16[3,1536,384]{2,1,0:T(8,128)(2,1)}, u32[]{:S(2)}, u32[]{:S(2)}) collective-permute-start(bf16[3,1536,384]{2,1,0:T(8,128)(2,1)} %add_convert_fusion), channel_id=1, source_target_pairs={{2,0},{4,6},{3,1},{5,7},{10,8},{12,14},{11,9},{13,15},{18,16},{20,... | collective-permute-start | bytes 10616840 | tf_op jit(solution)/shard_map/ppermute | solution.py:349
  574.7 135.5 %collective-permute-start.19 = (bf16[384,1792]{1,0:T(8,128)(2,1)S(1)}, bf16[384,1792]{1,0:T(8,128)(2,1)S(1)}, u32[]{:S(2)}, u32[]{:S(2)}) collective-permute-start(bf16[384,1792]{1,0:T(8,128)(2,1)S(1)} %fusion.4), channel_id=1, source_target_pairs={{2,4},{4,2},{3,5},{5,3},{10,12},{12,10},{11,13},{13,11},{18,20},{2... | collective-permute-start | bytes 4128776 | tf_op jit(solution)/shard_map/ppermute | solution.py:347
  579.2 125.6 %collective-permute-start.36 = (f32[2,1536]{1,0:T(2,128)S(1)}, f32[2,1536]{1,0:T(2,128)S(1)}, u32[]{:S(2)}, u32[]{:S(2)}) collective-permute-start(f32[2,1536]{1,0:T(2,128)S(1)} %add.349), channel_id=1, source_target_pairs={{0,2},{2,0},{4,6},{6,4},{1,3},{3,1},{5,7},{7,5},{8,10},{10,8},{12,... | collective-permute-start | bytes 36872 | tf_op jit(solution)/shard_map/ppermute | solution.py:927
  735.1 40.0 %collective-permute-start.31 = (bf16[3,384,384]{2,1,0:T(8,128)(2,1)S(1)}, bf16[3,384,384]{2,1,0:T(8,128)(2,1)S(1)}, u32[]{:S(2)}, u32[]{:S(2)}) collective-permute-start(bf16[3,384,384]{2,1,0:T(8,128)(2,1)S(1)} %get-tuple-element.89), channel_id=1, source_target_pairs={{0,16},{8,24},{16,0},{24,8},{1,17},{9,25},{17,1},{25,9},{2,18},{10... | collective-permute-start | bytes 2654216 | tf_op jit(solution)/shard_map/ppermute | solution.py:327
  739.4 54.6 %collective-permute-start.26 = (bf16[3,384,384]{2,1,0:T(8,128)(2,1)}, bf16[3,384,384]{2,1,0:T(8,128)(2,1)S(1)}, u32[]{:S(2)}, u32[]{:S(2)}) collective-permute-start(bf16[3,384,384]{2,1,0:T(8,128)(2,1)} %get-tuple-element.84), channel_id=1, source_target_pairs={{0,24},{8,16},{16,8},{24,0},{1,25},{9,17},{17,9},{25,1},{2,26},{10... | collective-permute-start | bytes 2654216 | tf_op jit(solution)/shard_map/ppermute | solution.py:327
  742.4 67.4 %collective-permute-start.25 = (bf16[3,384,384]{2,1,0:T(8,128)(2,1)S(1)}, bf16[3,384,384]{2,1,0:T(8,128)(2,1)S(1)}, u32[]{:S(2)}, u32[]{:S(2)}) collective-permute-start(bf16[3,384,384]{2,1,0:T(8,128)(2,1)S(1)} %get-tuple-element.85), channel_id=1, source_target_pairs={{0,16},{8,24},{16,0},{24,8},{1,17},{9,25},{17,1},{25,9},{2,18},{10... | collective-permute-start | bytes 2654216 | tf_op jit(solution)/shard_map/ppermute | solution.py:327
  756.1 53.7 %collective-permute-start.24 = (bf16[3,384,384]{2,1,0:T(8,128)(2,1)S(1)}, bf16[3,384,384]{2,1,0:T(8,128)(2,1)S(1)}, u32[]{:S(2)}, u32[]{:S(2)}) collective-permute-start(bf16[3,384,384]{2,1,0:T(8,128)(2,1)S(1)} %get-tuple-element.86), channel_id=1, source_target_pairs={{0,8},{8,0},{16,24},{24,16},{1,9},{9,1},{17,25},{25,17},{2,10},{10... | collective-permute-start | bytes 2654216 | tf_op jit(solution)/shard_map/ppermute | solution.py:327
  (86 other events, 1403.4 us)

commit v3 on v2

--- a/solution.py
+++ b/solution.py
@@ -319,37 +319,6 @@
 MIB = 2**20
 
 
-def rel_perm(size, r):
-    return [(i, i ^ r) for i in range(size)]
-
-
-def from_rel(value, r):
-    return lax.ppermute(value, "fsdp", rel_perm(lax.axis_size("fsdp"), r))
-
-
-def swap_core(value):
-    return lax.ppermute(value, "tp", [(0, 1), (1, 0)])
-
-
-def shift_ctx(value, step):
-    size = lax.axis_size("ctx")
-    pairs = [(i, i + step) for i in range(size) if 0 <= i + step < size]
-    return lax.ppermute(value, "ctx", pairs)
-
-
-def sum_ctx(value):
-    place = lax.axis_index("ctx")
-    inner = (place == 1) | (place == 2)
-    arrived = lax.ppermute(value, "ctx", [(0, 1), (3, 2)])
-    pair = jnp.where(
-        inner, value.astype(jnp.float32) + arrived.astype(jnp.float32), value.astype(jnp.float32)
-    ).astype(jnp.bfloat16)
-    across = lax.ppermute(pair, "ctx", [(1, 2), (2, 1)])
-    total = (pair.astype(jnp.float32) + across.astype(jnp.float32)).astype(jnp.bfloat16)
-    back = lax.ppermute(total, "ctx", [(1, 0), (2, 3)])
-    return jnp.where(inner, total, back)
-
-
 def expert_order(place):
     row = jnp.arange(128, dtype=jnp.int32)
     expert = (((row // 32) ^ place) * 2) + (row // 16) % 2
@@ -426,78 +395,6 @@
     return expd * (1.0 / jnp.sum(expd, axis=0, keepdims=True))
 
 
-def attend_kernel(place_ref, q_ref, k_ref, v_ref, out_ref):
-    keys = k_ref[...]
-    vals = v_ref[...]
-    for g in range(QUERY_PER_GROUP):
-        cols = pl.ds(g * HEAD_DIM, HEAD_DIM)
-        probs = block_probs(place_ref[0], keys, q_ref[:, cols]).astype(jnp.bfloat16)
-        out_ref[:, cols] = dot_f32(probs, vals, TN).astype(jnp.bfloat16)
-
-
-def attend_back_kernel(place_ref, q_ref, k_ref, v_ref, dm_ref, dq_ref, dk_ref, dv_ref):
-    keys = k_ref[...]
-    vals = v_ref[...]
-    scale = HEAD_DIM ** (-0.5)
-    dk_ref[...] = jnp.zeros_like(dk_ref)
-    dv_ref[...] = jnp.zeros_like(dv_ref)
-    for g in range(QUERY_PER_GROUP):
-        cols = pl.ds(g * HEAD_DIM, HEAD_DIM)
-        query = q_ref[:, cols]
-        d_mixed = dm_ref[:, cols]
-        probs = block_probs(place_ref[0], keys, query)
-        d_probs = dot_f32(vals, d_mixed, NT)
-        inner = jnp.sum(probs * d_probs, axis=0, keepdims=True)
-        d_scores = (probs * (d_probs - inner)).astype(jnp.bfloat16)
-        dq_ref[:, cols] = dot_f32(d_scores, keys, TN) * scale
-        dk_ref[...] += dot_f32(d_scores, query) * scale
-        dv_ref[...] += dot_f32(probs.astype(jnp.bfloat16), d_mixed)
-
-
-def attend(place, q, k, v):
-    return pl.pallas_call(
-        attend_kernel,
-        in_specs=[pl.BlockSpec(memory_space=pltpu.SMEM)]
-        + [pl.BlockSpec(memory_space=pltpu.VMEM)] * 3,
-        out_specs=pl.BlockSpec(memory_space=pltpu.VMEM),
-        out_shape=jax.ShapeDtypeStruct(q.shape, jnp.bfloat16),
-        compiler_params=pltpu.CompilerParams(vmem_limit_bytes=40 * MIB),
-        name="attend",
-    )(place, q, k, v)
-
-
-def attend_back(place, q, k, v, d_mixed):
-    return pl.pallas_call(
-        attend_back_kernel,
-        in_specs=[pl.BlockSpec(memory_space=pltpu.SMEM)]
-        + [pl.BlockSpec(memory_space=pltpu.VMEM)] * 4,
-        out_specs=[pl.BlockSpec(memory_space=pltpu.VMEM)] * 3,
-        out_shape=[
-            jax.ShapeDtypeStruct(q.shape, jnp.float32),
-            jax.ShapeDtypeStruct(k.shape, jnp.float32),
-            jax.ShapeDtypeStruct(v.shape, jnp.float32),
-        ],
-        compiler_params=pltpu.CompilerParams(vmem_limit_bytes=40 * MIB),
-        name="attend_back",
-    )(place, q, k, v, d_mixed)
-
-
-def gather_sum(parts, f, core):
-    own, other = parts[core], parts[1 - core].astype(jnp.bfloat16)
-    both = own + swap_core(other).astype(jnp.float32)
-    total = both[f]
-    for r in range(1, 4):
-        total = total + from_rel(both[f ^ r].astype(jnp.bfloat16), r).astype(jnp.float32)
-    return total
-
-
-def join_halves(core, half):
-    other = swap_core(half)
-    first = jnp.where(core == 0, half, other)
-    second = jnp.where(core == 0, other, half)
-    return jnp.concatenate([first, second], axis=0)
-
-
 def place():
     return lax.axis_index("fsdp"), lax.axis_index("ctx"), lax.axis_index("tp")
 
@@ -519,6 +416,12 @@
 
 def turn(value, cosine, sine):
     return value * cosine + pltpu.roll(value, HEAD_DIM // 2, 1) * sine
+
+
+def frequencies():
+    i = np.arange(HEAD_DIM // 2, dtype=np.float32)
+    freq = (theta_base ** (-(i * 2.0) / HEAD_DIM)).astype(np.float32)
+    return jnp.asarray(np.concatenate([freq, freq])[None, :])
 
 
 def front_kernel(
@@ -753,9 +656,6 @@
     half = count // 2
     shard, columns = attn_own.shape
     experts, hidden = pieces.shape[1], pieces.shape[4]
-    i = np.arange(HEAD_DIM // 2, dtype=np.float32)
-    freq = (theta_base ** (-(i * 2.0) / HEAD_DIM)).astype(np.float32)
-    freq = jnp.asarray(np.concatenate([freq, freq])[None, :])
     vmem, hbm = pl.BlockSpec(memory_space=pltpu.VMEM), pl.BlockSpec(memory_space=pl.ANY)
     bf16, f32 = jnp.bfloat16, jnp.float32
     shape = jax.ShapeDtypeStruct
@@ -788,7 +688,625 @@
             collective_id=0, has_side_effects=True, vmem_limit_bytes=48 * MIB
         ),
         name="front",
-    )(tok, gain_one, gain_two, freq, routes, gates, order, attn_own, pieces, cot)
+    )(tok, gain_one, gain_two, frequencies(), routes, gates, order, attn_own, pieces, cot)
+
+
+def moe_kernel(
+    x_hbm, dy_hbm, w_hbm, wl_ref, ge_hbm, dn_ref, mo_ref, gg_ref, x, dy, wgu, wd, gu, hid, ge, scales, sem, out_sem
+):
+    f = lax.axis_index("fsdp")
+    tokens, width = x.shape
+    hidden = w_hbm.shape[3]
+    half = tokens // 8
+    tile = 2 * half
+    own = w_hbm.shape[0]
+    loads = [pltpu.make_async_copy(x_hbm, x, sem.at[0])]
+    for e in range(own):
+        for m in range(2):
+            loads.append(
+                pltpu.make_async_copy(
+                    w_hbm.at[e, m], wgu.at[:, pl.ds((2 * e + m) * hidden, hidden)], sem.at[1 + 3 * e + m]
+                )
+            )
+    loads.append(pltpu.make_async_copy(dy_hbm, dy, sem.at[7]))
+    for e in range(own):
+        loads.append(
+            pltpu.make_async_copy(w_hbm.at[e, 2], wd.at[:, pl.ds(e * hidden, hidden)], sem.at[3 + 3 * e])
+        )
+    for copy in loads:
+        copy.start()
+    lane = lax.broadcasted_iota(jnp.int32, (half, 128), 1)
+    for b in range(8):
+        rows = wl_ref[b % 4, :, pl.ds((b // 4) * half, half)]
+        rows = jnp.concatenate([rows, jnp.zeros((128 - EXPERTS, half), jnp.float32)], axis=0)
+        scales[pl.ds(b * half, half), :] = rows.T
+    for copy in loads:
+        copy.wait()
+
+    lanes = lax.broadcasted_iota(jnp.int32, (tile, 128), 1)
+
+    def step(i, _):
+        rows = pl.ds(pl.multiple_of(i * tile, tile), tile)
+        acts = dot_f32(x[rows, :], wgu[...])
+        plain = dot_f32(dy[rows, :], wd[...])
+        table = scales[rows, :]
+        sums = jnp.zeros((tile, 128), jnp.float32)
+        for e in range(own):
+            gate_act = acts[:, 2 * e * hidden : (2 * e + 1) * hidden]
+            up_act = acts[:, (2 * e + 1) * hidden : (2 * e + 2) * hidden]
+            d_plain = plain[:, e * hidden : (e + 1) * hidden]
+            here = lanes == own * f + e
+            scale = jnp.sum(jnp.where(here, table, 0.0), axis=1, keepdims=True)
+            sigmoid = 1.0 / (1.0 + jnp.exp(-gate_act))
+            active = gate_act * sigmoid
+            act = active * up_act
+            total = jnp.sum(act * d_plain, axis=1, keepdims=True)
+            sums = jnp.where(here, jnp.where(scale != 0.0, total, 0.0), sums)
+            d_hidden = d_plain * scale
+            slope = sigmoid * (1.0 + gate_act * (1.0 - sigmoid))
+            hid[rows, pl.ds(e * hidden, hidden)] = (act * scale).astype(jnp.bfloat16)
+            gu[rows, pl.ds(2 * e * hidden, hidden)] = (d_hidden * up_act * slope).astype(jnp.bfloat16)
+            gu[rows, pl.ds((2 * e + 1) * hidden, hidden)] = (d_hidden * active).astype(jnp.bfloat16)
+        gg_ref[rows, :] = sums
+        return 0
+
+    lax.fori_loop(0, tokens // tile, step, 0)
+
+    block = width // 4
+
+    def grad_step(s, _):
+        cols = pl.ds(pl.multiple_of(s * block, 128), block)
+        inner = dot_f32(x[:, cols], gu[...], TN).astype(jnp.bfloat16)
+        outer = dot_f32(dy[:, cols], hid[...], TN).astype(jnp.bfloat16)
+        for e in range(own):
+            for m in range(2):
+                k = 2 * e + m
+                ge[3 * e + m, cols, :] = inner[:, k * hidden : (k + 1) * hidden]
+            ge[3 * e + 2, cols, :] = outer[:, e * hidden : (e + 1) * hidden]
+        return 0
+
+    lax.fori_loop(0, 4, grad_step, 0)
+    store = pltpu.make_async_copy(ge, ge_hbm, out_sem)
+    store.start()
+
+    def down_step(i, _):
+        rows = pl.ds(pl.multiple_of(i * tile, tile), tile)
+        dn_ref[rows, :] = dot_f32(gu[rows, :], wgu[...], NT).astype(jnp.bfloat16)
+        mo_ref[rows, :] = dot_f32(hid[rows, :], wd[...], NT).astype(jnp.bfloat16)
+        return 0
+
+    lax.fori_loop(0, tokens // tile, down_step, 0)
+    store.wait()
+
+
+def moe_layer(x, dy, weights, gate_table):
+    tokens, width = x.shape
+    own, _, _, hidden = weights.shape
+    vmem, hbm = pl.BlockSpec(memory_space=pltpu.VMEM), pl.BlockSpec(memory_space=pl.ANY)
+    bf16, f32 = jnp.bfloat16, jnp.float32
+    shape = jax.ShapeDtypeStruct
+    return pl.pallas_call(
+        moe_kernel,
+        in_specs=[hbm] * 3 + [vmem],
+        out_specs=[hbm, vmem, vmem, vmem],
+        out_shape=[
+            shape((3 * own, width, hidden), bf16),
+            shape((tokens, width), bf16),
+            shape((tokens, width), bf16),
+            shape((tokens, 128), f32),
+        ],
+        scratch_shapes=[
+            pltpu.VMEM((tokens, width), bf16),
+            pltpu.VMEM((tokens, width), bf16),
+            pltpu.VMEM((width, 2 * own * hidden), bf16),
+            pltpu.VMEM((width, own * hidden), bf16),
+            pltpu.VMEM((tokens, 2 * own * hidden), bf16),
+            pltpu.VMEM((tokens, own * hidden), bf16),
+            pltpu.VMEM((3 * own, width, hidden), bf16),
+            pltpu.VMEM((tokens, 128), f32),
+            pltpu.SemaphoreType.DMA((8,)),
+            pltpu.SemaphoreType.DMA,
+        ],
+        compiler_params=pltpu.CompilerParams(vmem_limit_bytes=58 * MIB),
+        name="experts",
+    )(x, dy, weights, gate_table)
+
+
+def rear_kernel(
+    res_ref,
+    xn_ref,
+    q_ref,
+    kv_ref,
+    mixed_ref,
+    gain_one_ref,
+    gain_two_ref,
+    freq_ref,
+    tok_hbm,
+    cot_hbm,
+    ge_hbm,
+    dn_hbm,
+    mo_hbm,
+    gg_hbm,
+    wa_hbm,
+    layer_ref,
+    tokgrad_ref,
+    gains_ref,
+    gate_ref,
+    attn_hbm,
+    fin_hbm,
+    ge,
+    r1,
+    r2,
+    wa,
+    dn_own,
+    dn_in,
+    dn_got,
+    mo_own,
+    mo_in,
+    mo_got,
+    gg_own,
+    gg_in,
+    gg_sum,
+    gg_got,
+    dres,
+    dattn,
+    dmixed,
+    dproj,
+    dkv,
+    dkv_low,
+    dkv_got,
+    d1,
+    d1_low,
+    d1_in,
+    ga,
+    ra,
+    a1,
+    a2,
+    gacc,
+    gin,
+    tok_half,
+    cot_half,
+    send,
+    recv,
+    local,
+    z_out,
+    z_across,
+    z_back,
+    z_r1,
+    z_r2,
+    f_out,
+    f_in,
+):
+    f, z, c = place()
+    fx, fy, fd = plane_peers(f)
+    rel = [f, fx, fy, fd]
+    f32, bf16 = jnp.float32, jnp.bfloat16
+    count, width = tok_hbm.shape
+    half = count // 2
+    shard = attn_hbm.shape[0]
+    in_cols = (QUERY_PER_GROUP + 2) * HEAD_DIM
+    q_cols = QUERY_PER_GROUP * HEAD_DIM
+    ins = pl.ds(0, in_cols)
+    outs = pl.ds(in_cols, attn_hbm.shape[1] - in_cols)
+    scale = HEAD_DIM ** (-0.5)
+
+    def at(fsdp=f, ctx=z, tp=c):
+        return {"fsdp": fsdp, "ctx": ctx, "tp": tp}
+
+    def copy_to(src, dst, send_sem, recv_sem, device):
+        return pltpu.make_async_remote_copy(
+            src_ref=src,
+            dst_ref=dst,
+            send_sem=send_sem,
+            recv_sem=recv_sem,
+            device_id=device,
+            device_id_type=MESH_ID,
+        )
+
+    def remote(src, dst, k, device):
+        return copy_to(src, dst, send.at[k], recv.at[k], device)
+
+    plane = [at(fx), at(fy), at(fd)]
+    line = [at(ctx=lax.rem(z + s, 4)) for s in range(1, 4)]
+    sibling = at(tp=1 - c)
+    partner = at(ctx=z + 1 - 2 * lax.rem(z, 2))
+    opposite = at(ctx=3 - z)
+    inner = (z == 1) | (z == 2)
+    outer = (z == 0) | (z == 3)
+
+    loads = [pltpu.make_async_copy(ge_hbm, ge, local.at[0])]
+    loads.append(pltpu.make_async_copy(dn_hbm.at[c], dn_own, local.at[1]))
+    loads.append(pltpu.make_async_copy(gg_hbm.at[c], gg_own, local.at[2]))
+    loads.append(pltpu.make_async_copy(wa_hbm, wa, local.at[3]))
+    loads.append(pltpu.make_async_copy(mo_hbm.at[c], mo_own, local.at[4]))
+    loads.append(pltpu.make_async_copy(tok_hbm.at[rows_of(c, half)], tok_half, local.at[5]))
+    loads.append(pltpu.make_async_copy(cot_hbm.at[rows_of(c, half)], cot_half, local.at[6]))
+    for copy in loads:
+        copy.start()
+    greet(plane + line + [sibling])
+    dn_swap = remote(dn_hbm.at[1 - c], dn_in, 0, sibling)
+    gg_swap = remote(gg_hbm.at[1 - c], gg_in, 1, sibling)
+    mo_swap = remote(mo_hbm.at[1 - c], mo_in, 2, sibling)
+    dn_swap.start()
+    gg_swap.start()
+    mo_swap.start()
+
+    mats = ge.shape[0]
+    n_expert = 4 * mats
+    n_attn = 4
+    n_all = n_expert + n_attn
+    a_rows = shard // n_attn
+
+    def chunk(k):
+        if k < n_expert:
+            j, r = k // 4, k % 4
+            rows = rows_of(rel[r], shard)
+            return ge.at[j, rows], r1.at[j, rows], r2.at[j, rows]
+        rows = pl.ds((k - n_expert) * a_rows, a_rows)
+        return ra.at[0, rows], a1.at[rows], a2.at[rows]
+
+    def add_into(dst, left, right):
+        size = dst.shape[0] // 6
+
+        def body(i, _):
+            rows = pl.ds(pl.multiple_of(i * size, size), size)
+            dst[rows, :] = (left[rows, :].astype(f32) + right[rows, :].astype(f32)).astype(bf16)
+            return 0
+
+        lax.fori_loop(0, 6, body, 0)
+
+    def first(k):
+        own, one, _ = chunk(k)
+        return copy_to(own, one, z_out.at[k], z_r1.at[k], partner)
+
+    def across(k):
+        own, _, two = chunk(k)
+        return copy_to(own, two, z_across.at[k], z_r2.at[k], opposite)
+
+    def back(k):
+        _, one, _ = chunk(k)
+        return copy_to(one, one, z_back.at[k], z_r1.at[k], partner)
+
+    def final(k):
+        _, one, _ = chunk(k)
+        j, r = k // 4, k % 4
+        if r == 0:
+            return pltpu.make_async_copy(one, fin_hbm.at[0, j], f_out.at[k])
+        return copy_to(one, fin_hbm.at[r, j], f_out.at[k], f_in.at[k], plane[r - 1])
+
+    def z_step(i):
+        if i < n_all:
+
+            @pl.when(outer)
+            def _():
+                if i >= 2:
+                    first(i - 2).wait_send()
+                first(i).start()
+
+        if 1 <= i <= n_all:
+            k = i - 1
+
+            @pl.when(inner)
+            def _():
+                own, one, _ = chunk(k)
+                first(k).wait_recv()
+                add_into(own, own, one)
+                across(k).start()
+
+        if 2 <= i <= n_all + 1:
+            k = i - 2
+
+            @pl.when(inner)
+            def _():
+                own, one, two = chunk(k)
+                across(k).wait_recv()
+                add_into(one, own, two)
+                back(k).start()
+                if k < n_expert:
+                    final(k).start()
+
+        if 3 <= i <= n_all + 2:
+            k = i - 3
+
+            @pl.when(outer)
+            def _():
+                back(k).wait_recv()
+                if k < n_expert:
+                    final(k).start()
+
+    loads[0].wait()
+    z_step(0)
+    loads[5].wait()
+    loads[6].wait()
+
+    loads[1].wait()
+    loads[2].wait()
+    gg_swap.wait_recv()
+    gg_sum[...] = gg_own[...] + gg_in[...]
+    dn_swap.wait_recv()
+    for g in range(4):
+        dn_own[g] = (dn_own[g].astype(f32) + dn_in[g].astype(f32)).astype(bf16)
+    dn_out = [remote(dn_own.at[rel[i + 1]], dn_got.at[i], 3 + i, plane[i]) for i in range(3)]
+    gg_out = [remote(gg_sum.at[rel[i + 1]], gg_got.at[i], 6 + i, plane[i]) for i in range(3)]
+    for copy in dn_out + gg_out:
+        copy.start()
+    z_step(1)
+    loads[4].wait()
+    mo_swap.wait_recv()
+    for g in range(4):
+        mo_own[g] = (mo_own[g].astype(f32) + mo_in[g].astype(f32)).astype(bf16)
+    mo_out = [remote(mo_own.at[rel[i + 1]], mo_got.at[i], 9 + i, plane[i]) for i in range(3)]
+    for copy in mo_out:
+        copy.start()
+    z_step(2)
+    for copy in dn_out:
+        copy.wait_recv()
+    d_two = dn_own[f].astype(f32)
+    for i in range(3):
+        d_two = d_two + dn_got[i].astype(f32)
+    residual = res_ref[...]
+    inv = lax.rsqrt(jnp.mean(residual * residual, axis=-1, keepdims=True) + eps)
+    scaled = d_two * gain_two_ref[...]
+    inside = jnp.mean(scaled * residual, axis=-1, keepdims=True)
+    d_norm = inv * scaled - residual * (inv * inv * inv * inside)
+    gacc[0] = jnp.zeros(gacc.shape[1:], f32)
+    gacc[0, 1:2, :] = jnp.sum(d_two * residual * inv, axis=0, keepdims=True)
+    my_rows = rows_of(c, half)
+    d_res = cot_half[...].astype(f32) + d_norm
+    dres[...] = d_res
+    dattn[my_rows, :] = d_res.astype(bf16)
+    da_swap = remote(dattn.at[my_rows], dattn.at[my_rows], 12, sibling)
+    da_swap.start()
+    loads[3].wait()
+    z_step(3)
+    da_swap.wait_recv()
+    dmixed[...] = dot_f32(dattn[...], wa[:, outs]).astype(bf16)
+    z_step(4)
+
+    position = z * count + lax.broadcasted_iota(jnp.int32, (count, HEAD_DIM), 0)
+    angle = position.astype(f32) * freq_ref[...]
+    cosine = jnp.cos(angle)
+    lane = lax.broadcasted_iota(jnp.int32, (count, HEAD_DIM), 1)
+    sine = jnp.where(lane < HEAD_DIM // 2, jnp.sin(angle), -jnp.sin(angle))
+    keys = kv_ref[:, :, pl.ds(0, HEAD_DIM)].reshape(4 * count, HEAD_DIM)
+    vals = kv_ref[:, :, pl.ds(HEAD_DIM, HEAD_DIM)].reshape(4 * count, HEAD_DIM)
+    key_cols, val_cols = pl.ds(0, HEAD_DIM), pl.ds(HEAD_DIM, HEAD_DIM)
+    dkv[...] = jnp.zeros_like(dkv)
+    for g in range(QUERY_PER_GROUP):
+        cols = pl.ds(g * HEAD_DIM, HEAD_DIM)
+        query = q_ref[:, cols]
+        d_mix = dmixed[:, cols]
+        probs = block_probs(z, keys, query)
+        d_probs = dot_f32(vals, d_mix, NT)
+        inside = jnp.sum(probs * d_probs, axis=0, keepdims=True)
+        d_scores = (probs * (d_probs - inside)).astype(bf16)
+        d_query = dot_f32(d_scores, keys, TN) * scale
+        dproj[:, cols] = turn(d_query, cosine, sine).astype(bf16)
+        dkv[:, key_cols] += dot_f32(d_scores, query) * scale
+        dkv[:, val_cols] += dot_f32(probs.astype(bf16), d_mix)
+        if g % 2 == 1:
+            z_step(5 + g // 2)
+    dkv_low[...] = dkv[...].reshape(dkv_low.shape).astype(bf16)
+    dkv_out = [
+        remote(dkv_low.at[s], dkv_got.at[s - 1], 12 + s, at(ctx=lax.rem(z + 4 - s, 4)))
+        for s in range(1, 4)
+    ]
+    for s in range(1, 4):
+
+        @pl.when(z >= s)
+        def _(s=s):
+            dkv_out[s - 1].start()
+
+    def weight_grad(left, right, cols):
+        def body(i, _):
+            rows = pl.ds(pl.multiple_of(i * 256, 256), 256)
+            ga[rows, cols] = dot_f32(left[:, rows], right, TN).astype(bf16)
+            return 0
+
+        lax.fori_loop(0, width // 256, body, 0)
+
+    def send_grad(cols, k):
+        copies = [
+            remote(ga.at[rows_of(rel[i + 1], shard), cols], ra.at[i, :, cols], k + i, plane[i])
+            for i in range(3)
+        ]
+        for copy in copies:
+            copy.start()
+        return copies
+
+    weight_grad(dattn, mixed_ref[...], outs)
+    ga_copies = send_grad(outs, 16)
+    z_step(8)
+    q_part = pl.ds(0, q_cols)
+    weight_grad(xn_ref, dproj[:, q_part], q_part)
+    ga_copies += send_grad(q_part, 19)
+    z_step(9)
+    for s in range(1, 4):
+
+        @pl.when(z + s < 4)
+        def _(s=s):
+            dkv_out[s - 1].wait_recv()
+            dkv[0:count, :] += dkv_got[s - 1].astype(f32)
+
+    kv_part = pl.ds(q_cols, 2 * HEAD_DIM)
+    dproj[:, pl.ds(q_cols, HEAD_DIM)] = turn(dkv[0:count, key_cols], cosine, sine).astype(bf16)
+    dproj[:, pl.ds(q_cols + HEAD_DIM, HEAD_DIM)] = dkv[0:count, val_cols].astype(bf16)
+    weight_grad(xn_ref, dproj[:, kv_part], kv_part)
+    ga_copies += send_grad(kv_part, 22)
+    z_step(10)
+
+    for s in range(width // 256):
+        rows = pl.ds(s * 256, 256)
+        d1[:, rows] = dot_f32(dproj[my_rows, :], wa[rows, ins], NT)
+        d1_low[:, rows] = dot_f32(dproj[rows_of(1 - c, half), :], wa[rows, ins], NT).astype(bf16)
+    d1_swap = remote(d1_low, d1_in, 25, sibling)
+    d1_swap.start()
+    z_step(11)
+    d1_swap.wait_recv()
+    d_one = d1[...] + d1_in[...].astype(f32)
+    tok = tok_half[...].astype(f32)
+    inv = lax.rsqrt(jnp.mean(tok * tok, axis=-1, keepdims=True) + eps)
+    scaled = d_one * gain_one_ref[...]
+    inside = jnp.mean(scaled * tok, axis=-1, keepdims=True)
+    d_norm = inv * scaled - tok * (inv * inv * inv * inside)
+    gacc[0, 0:1, :] = jnp.sum(d_one * tok * inv, axis=0, keepdims=True)
+    tokgrad_ref[my_rows, :] = (dres[...] + d_norm).astype(bf16)
+    tg_swap = remote(tokgrad_ref.at[my_rows], tokgrad_ref.at[my_rows], 26, sibling)
+    tg_swap.start()
+    z_step(12)
+
+    for copy in mo_out + gg_out:
+        copy.wait_recv()
+    moe = mo_own[f].astype(f32)
+    gates = gg_sum[f]
+    for i in range(3):
+        moe = moe + mo_got[i].astype(f32)
+        gates = gates + gg_got[i]
+    layer_ref[my_rows, :] = (res_ref[...] + moe).astype(bf16)
+    gate_ref[my_rows, :] = gates
+    lo_swap = remote(layer_ref.at[my_rows], layer_ref.at[my_rows], 27, sibling)
+    gt_swap = remote(gate_ref.at[my_rows], gate_ref.at[my_rows], 28, sibling)
+    lo_swap.start()
+    gt_swap.start()
+    z_step(13)
+
+    stages = [sibling, at(fx), at(fy), partner, at(ctx=lax.rem(z + 2, 4))]
+    gain_copies = [remote(gacc.at[i], gin.at[i], 29 + i, stages[i]) for i in range(5)]
+    for i in range(5):
+        gain_copies[i].start()
+        z_step(14 + i)
+        gain_copies[i].wait_recv()
+        total = gacc[i] + gin[i]
+        if i < 4:
+            gacc[i + 1] = total
+        else:
+            gains_ref[...] = total
+
+    for i in range(19, n_expert):
+        z_step(i)
+    for copy in ga_copies:
+        copy.wait_recv()
+
+    def attn_sum(i, _):
+        size = shard // 8
+        here = pl.ds(pl.multiple_of(i * size, size), size)
+        total = ga[pl.ds(pl.multiple_of(f * shard + i * size, size), size), :].astype(f32)
+        for r in range(3):
+            total = total + ra[r, here, :].astype(f32)
+        ra[0, here, :] = total.astype(bf16)
+        return 0
+
+    lax.fori_loop(0, 8, attn_sum, 0)
+    for i in range(n_expert, n_all + 3):
+        z_step(i)
+    store = pltpu.make_async_copy(a1, attn_hbm, local.at[0])
+    store.start()
+
+    store.wait()
+    for k in range(n_all):
+
+        @pl.when(outer)
+        def _(k=k):
+            if k >= n_all - 2:
+                first(k).wait_send()
+
+        @pl.when(inner)
+        def _(k=k):
+            across(k).wait_send()
+            back(k).wait_send()
+
+    for k in range(n_expert):
+        if k % 4 == 0:
+            final(k).wait()
+        else:
+            final(k).wait_send()
+            final(k).wait_recv()
+    for s in range(1, 4):
+
+        @pl.when(z >= s)
+        def _(s=s):
+            dkv_out[s - 1].wait_send()
+
+    for copy in [tg_swap, lo_swap, gt_swap]:
+        copy.wait_recv()
+    swaps = [dn_swap, gg_swap, mo_swap, da_swap, d1_swap, tg_swap, lo_swap, gt_swap]
+    for copy in swaps + dn_out + gg_out + mo_out + ga_copies + gain_copies:
+        copy.wait_send()
+
+
+def rear(tok, cot, res, xn, q, kv, mixed, gain_one, gain_two, ge, dn, mo, gg, wa):
+    count, width = tok.shape
+    half = count // 2
+    columns = wa.shape[1]
+    shard = width // 4
+    mats, _, hidden = ge.shape
+    q_cols = q.shape[1]
+    vmem, hbm = pl.BlockSpec(memory_space=pltpu.VMEM), pl.BlockSpec(memory_space=pl.ANY)
+    bf16, f32 = jnp.bfloat16, jnp.float32
+    shape = jax.ShapeDtypeStruct
+    dma = pltpu.SemaphoreType.DMA
+    n_all = 4 * mats + 4
+    return pl.pallas_call(
+        rear_kernel,
+        in_specs=[vmem] * 8 + [hbm] * 7,
+        out_specs=[vmem] * 4 + [hbm] * 2,
+        out_shape=[
+            shape((count, width), bf16),
+            shape((count, width), bf16),
+            shape((8, width), f32),
+            shape((count, 128), f32),
+            shape((shard, columns), bf16),
+            shape((4, mats, shard, hidden), bf16),
+        ],
+        scratch_shapes=[
+            pltpu.VMEM((mats, width, hidden), bf16),
+            pltpu.VMEM((mats, width, hidden), bf16),
+            pltpu.VMEM((mats, width, hidden), bf16),
+            pltpu.VMEM((width, columns), bf16),
+            pltpu.VMEM((4, half, width), bf16),
+            pltpu.VMEM((4, half, width), bf16),
+            pltpu.VMEM((3, half, width), bf16),
+            pltpu.VMEM((4, half, width), bf16),
+            pltpu.VMEM((4, half, width), bf16),
+            pltpu.VMEM((3, half, width), bf16),
+            pltpu.VMEM((4, half, 128), f32),
+            pltpu.VMEM((4, half, 128), f32),
+            pltpu.VMEM((4, half, 128), f32),
+            pltpu.VMEM((3, half, 128), f32),
+            pltpu.VMEM((half, width), f32),
+            pltpu.VMEM((count, width), bf16),
+            pltpu.VMEM((count, q_cols), bf16),
+            pltpu.VMEM((count, q_cols + 2 * HEAD_DIM), bf16),
+            pltpu.VMEM((4 * count, 2 * HEAD_DIM), f32),
+            pltpu.VMEM((4, count, 2 * HEAD_DIM), bf16),
+            pltpu.VMEM((3, count, 2 * HEAD_DIM), bf16),
+            pltpu.VMEM((half, width), f32),
+            pltpu.VMEM((half, width), bf16),
+            pltpu.VMEM((half, width), bf16),
+            pltpu.VMEM((width, columns), bf16),
+            pltpu.VMEM((3, shard, columns), bf16),
+            pltpu.VMEM((shard, columns), bf16),
+            pltpu.VMEM((shard, columns), bf16),
+            pltpu.VMEM((5, 8, width), f32),
+            pltpu.VMEM((5, 8, width), f32),
+            pltpu.VMEM((half, width), bf16),
+            pltpu.VMEM((half, width), bf16),
+            dma((34,)),
+            dma((34,)),
+            dma((7,)),
+            dma((n_all,)),
+            dma((n_all,)),
+            dma((n_all,)),
+            dma((n_all,)),
+            dma((n_all,)),
+            dma((4 * mats,)),
+            dma((4 * mats,)),
+        ],
+        compiler_params=pltpu.CompilerParams(
+            collective_id=1, has_side_effects=True, vmem_limit_bytes=62 * MIB
+        ),
+        name="rear",
+    )(res, xn, q, kv, mixed, gain_one, gain_two, frequencies(), tok, cot, ge, dn, mo, gg, wa)
 
 
 def body_fast(
@@ -806,147 +1324,53 @@
     count = sequence_count * block_len
     half = count // 2
     own_experts = EXPERTS // 4
-    input_columns = (QUERY_PER_GROUP + 2) * HEAD_DIM
-    query_columns = QUERY_PER_GROUP * HEAD_DIM
     f = lax.axis_index("fsdp")
-    z = lax.axis_index("ctx")
-    core = lax.axis_index("tp")
-    shard = attention_params.shape[0]
-    f32, bf16 = jnp.float32, jnp.bfloat16
-
-    def my_half(value):
-        return lax.dynamic_slice_in_dim(value, core * half, half, 0)
-
-    place_order = jnp.arange(4, dtype=jnp.int32) ^ f
+    shard, hidden = attention_params.shape[0], expert_weights.shape[3]
     order = expert_order(f)
     pieces = split_experts(jnp.transpose(expert_weights, (0, 2, 1, 3)), order)
-    pieces = jnp.transpose(
-        pieces.reshape(4, own_experts, 3, shard, expert_weights.shape[3]), (0, 1, 2, 3, 4)
-    )
-    tok_low = tokens.reshape(count, model_width)
-    grad_out = cotangent.reshape(count, model_width)
-    first_normed, queries, kv_all, mixed, residual, gate_table, whole_attn, whole_expert, x, dy = front(
-        tok_low,
-        attn_norm[None, :],
-        ffn_norm[None, :],
-        routes.reshape(count, TOP).T,
+    pieces = pieces.reshape(4, own_experts, 3, shard, hidden)
+    tok = tokens.reshape(count, model_width)
+    cot = cotangent.reshape(count, model_width)
+    gain_one, gain_two = attn_norm[None, :], ffn_norm[None, :]
+    route_rows = routes.reshape(count, TOP)
+    normed, queries, kv, mixed, residual, gate_table, whole_attn, whole_expert, x, dy = front(
+        tok,
+        gain_one,
+        gain_two,
+        route_rows.T,
         gate_values.reshape(count, TOP).T,
         slot_order.reshape(1, count),
         attention_params[:, 0, :],
         pieces,
-        grad_out,
-    )
-    inputs = x.reshape(8 * half, model_width)
-    upstream = dy.reshape(8 * half, model_width)
-    attn_in, attn_out = whole_attn[:, :input_columns], whole_attn[:, input_columns:]
-    weights_in = lax.dynamic_slice_in_dim(gate_table, f * own_experts, own_experts, 1)
-    weights_in = jnp.transpose(weights_in.reshape(4, own_experts, 2, half), (1, 2, 0, 3))
-    weights_in = weights_in.reshape(own_experts, 8 * half)
-    kept = gate_table[f].T != 0.0
-    route_rows = routes.reshape(count, TOP)
-    kv_all = kv_all.reshape(4 * count, 2 * HEAD_DIM)
-    key_all, value_all = kv_all[:, :HEAD_DIM], kv_all[:, HEAD_DIM:]
-    tok_float = tok_low.astype(f32)
-    inv_one = lax.rsqrt(jnp.mean(tok_float * tok_float, axis=-1, keepdims=True) + eps)
-    inv_two = lax.rsqrt(jnp.mean(residual * residual, axis=-1, keepdims=True) + eps)
-    positions = z * block_len + jnp.arange(block_len, dtype=jnp.int32)
-    cosine, sine = angle_tables(positions)
-    cos_three, sin_three = cosine[:, None, :], sine[:, None, :]
-    place = jnp.reshape(z, (1,)).astype(jnp.int32)
-
-    moe_parts = 0.0
-    d_normed_parts = 0.0
-    gate_parts = []
-    expert_grads = []
-    for e in range(own_experts):
-        gate_act = dot_f32(inputs, whole_expert[e, 0])
-        up_act = dot_f32(inputs, whole_expert[e, 1])
-        d_plain = dot_f32(upstream, whole_expert[e, 2])
-        gate_sigmoid = jax.nn.sigmoid(gate_act)
-        active = gate_act * gate_sigmoid
-        hidden = active * up_act
-        scale = weights_in[e][:, None]
-        hidden_low = (hidden * scale).astype(bf16)
-        gate_parts.append(jnp.sum(hidden * d_plain, axis=1))
-        d_hidden = d_plain * scale
-        silu_slope = gate_sigmoid * (1.0 + gate_act * (1.0 - gate_sigmoid))
-        d_gate = (d_hidden * up_act * silu_slope).astype(bf16)
-        d_up = (d_hidden * active).astype(bf16)
-        moe_parts = moe_parts + dot_f32(hidden_low, whole_expert[e, 2], NT)
-        d_normed_parts = (
-            d_normed_parts
-            + dot_f32(d_gate, whole_expert[e, 0], NT)
-            + dot_f32(d_up, whole_expert[e, 1], NT)
-        )
-        expert_grads.append(
-            jnp.stack(
-                [
-                    dot_f32(inputs, d_gate, TN).astype(bf16),
-                    dot_f32(inputs, d_up, TN).astype(bf16),
-                    dot_f32(upstream, hidden_low, TN).astype(bf16),
-                ]
-            )
-        )
-    d_normed_two = gather_sum(d_normed_parts.reshape(2, 4, half, model_width), f, core)
-    moe = gather_sum(moe_parts.reshape(2, 4, half, model_width), f, core)
-    layer_out = join_halves(core, (residual + moe).astype(bf16))
-
-    gate_rows = jnp.stack(gate_parts).reshape(own_experts, 2, 4, half)
-    gate_rows = jnp.take(gate_rows, core, 1) + swap_core(jnp.take(gate_rows, 1 - core, 1))
-    gate_rows = jnp.stack(
-        [gate_rows[:, f]] + [from_rel(gate_rows[:, f ^ r], r) for r in range(1, 4)]
-    )
-    gate_rows = join_halves(core, gate_rows.reshape(EXPERTS, half).T)
-    rel_ids = (place_order[:, None] * own_experts + jnp.arange(own_experts)).reshape(EXPERTS)
-    kept_rel = kept[:, rel_ids]
-    picked = (route_rows[:, :, None] == rel_ids) & kept_rel[:, None, :]
-    gate_grad = jnp.sum(jnp.where(picked, gate_rows[:, None, :], 0.0), axis=-1)
-
-    d_resid_norm, gain_two = norm_back(residual, inv_two, ffn_norm, d_normed_two)
-    d_residual = my_half(grad_out).astype(f32) + d_resid_norm
-    d_attn = join_halves(core, d_residual.astype(bf16))
-    d_mixed = dot_f32(d_attn, attn_out).astype(bf16)
-    d_queries, d_key_all, d_value_all = attend_back(place, queries, key_all, value_all, d_mixed)
-    d_kv = jnp.concatenate([d_key_all, d_value_all], axis=1).reshape(4, count, 2 * HEAD_DIM)
-    d_key_value = d_kv[0]
-    for s in range(1, 4):
-        d_key_value = d_key_value + shift_ctx(d_kv[s].astype(bf16), -s).astype(f32)
-    d_turned = jnp.concatenate([d_queries, d_key_value[:, :HEAD_DIM]], axis=1)
-    d_turned = rotate(
-        d_turned.reshape(count, QUERY_PER_GROUP + 1, HEAD_DIM), cos_three, -sin_three
-    ).reshape(count, query_columns + HEAD_DIM)
-    d_projected = jnp.concatenate([d_turned, d_key_value[:, HEAD_DIM:]], axis=1).astype(bf16)
-    d_normed_local = dot_f32(d_projected, attn_in, NT)
-    other_rows = lax.dynamic_slice_in_dim(d_normed_local, (1 - core) * half, half, 0)
-    d_normed_one = my_half(d_normed_local) + swap_core(other_rows.astype(bf16)).astype(f32)
-    d_tok_norm, gain_one = norm_back(my_half(tok_float), my_half(inv_one), attn_norm, d_normed_one)
-    tokens_grad = join_halves(core, (d_residual + d_tok_norm).astype(bf16))
-    gains = jnp.stack([gain_one, gain_two])
-    gains = gains + swap_core(gains)
-    for axis, r in (("fsdp", 1), ("fsdp", 2), ("ctx", 1), ("ctx", 2)):
-        gains = gains + lax.ppermute(gains, axis, rel_perm(4, r))
-
-    attn_grad = jnp.concatenate(
-        [dot_f32(first_normed, d_projected, TN), dot_f32(d_attn, mixed, TN)], axis=1
-    ).reshape(4, shard, -1)[place_order]
-    attn_sum = attn_grad[0]
-    for r in range(1, 4):
-        attn_sum = attn_sum + from_rel(attn_grad[r].astype(bf16), r).astype(f32)
-    attn_total = sum_ctx(attn_sum.astype(bf16)).astype(f32)[:, None, :]
-
-    finals = []
-    for e in range(own_experts):
-        total = sum_ctx(expert_grads[e]).reshape(3, 4, shard, -1)
-        total = jnp.take(total, place_order, axis=1)
-        finals.append(
-            jnp.stack([total[:, 0]] + [from_rel(total[:, r], r) for r in range(1, 4)])
-        )
-    finals = jnp.stack(finals, axis=1).reshape(EXPERTS, 3, shard, -1)
+        cot,
+    )
+    grads, d_normed, moe, gate_parts = moe_layer(
+        x.reshape(8 * half, model_width), dy.reshape(8 * half, model_width), whole_expert, gate_table
+    )
+    layer_out, tokens_grad, gains, gate_rows, attn_grad, finals = rear(
+        tok,
+        cot,
+        residual,
+        normed,
+        queries,
+        kv,
+        mixed,
+        gain_one,
+        gain_two,
+        grads,
+        d_normed.reshape(2, 4, half, model_width),
+        moe.reshape(2, 4, half, model_width),
+        gate_parts.reshape(2, 4, half, 128),
+        whole_attn,
+    )
+    picked = route_rows[:, :, None] == jnp.arange(EXPERTS, dtype=jnp.int32)
+    gate_grad = jnp.sum(jnp.where(picked, gate_rows[:, None, :EXPERTS], 0.0), axis=-1)
+    finals = finals.reshape(EXPERTS, 3, shard, hidden)
     expert_grad = jnp.transpose(join_experts(finals, order.T), (0, 2, 1, 3))
     return (
         layer_out.reshape(sequence_count, block_len, model_width),
         tokens_grad.reshape(sequence_count, block_len, model_width),
-        attn_total,
+        attn_grad.astype(jnp.float32)[:, None, :],
         expert_grad,
         gains[0],
         gains[1],

time: 822 us -> 484 us (0.59)
  waiting for transfers between devices: 333 us -> 0 us
  Pallas kernels: 184 us -> 460 us
  matrix products: 88.6 us -> 0 us
  starting transfers between devices: 76.4 us -> 0 us
  other arithmetic: 77.4 us -> 2.39 us
  local copies, waits for them, and re-layouts: 57.6 us -> 20.7 us
    ppermute x43 -> x0, waiting for transfers between devices: 333 us -> none  [the longest x18 144 us: from_rel(): return lax.ppermute(value, 'fsdp', rel_perm(lax.axis_size('fsdp'), r))]
    pallas_call x1 -> x2, Pallas kernels: 7.81 us -> 284 us  [the longest x1 250 us: rear(): pl.pallas_call(rear_kernel, in_specs=[vmem] * 8 + [hbm] * 7, out_specs=[v...]
    dot_general x22 -> x0, matrix products: 88.6 us -> none  [dot_f32(): return lax.dot_general(a, b, dims, preferred_element_type=jnp.float32)]
    ppermute x43 -> x0, starting transfers between devices: 76.4 us -> none  [the longest x4 25.7 us: body_fast(): gains = gains + lax.ppermute(gains, axis, rel_perm(4, r))]
    convert_element_type x11 -> x0, other arithmetic: 24.7 us -> none  [the longest x3 9.48 us: sum_ctx(): (pair.astype(jnp.float32) + across.astype(jnp.float32)).astype(jnp.bfloat16)]
    gather x4 -> x0, local copies, waits for them, and re-layouts: 20.4 us -> none  [the longest x2 9.95 us: body_fast(): total = jnp.take(total, place_order, axis=1)]
    select_n x11 -> x0, other arithmetic: 16 us -> none  [the longest x2 6.41 us: sum_ctx(): return jnp.where(inner, total, back)]
    reshape x2 -> x0, local copies, waits for them, and re-layouts: 12.1 us -> none  [the longest x1 12.1 us: body_fast(): attn_grad = jnp.concatenate([dot_f32(first_normed, d_projected, TN), dot_...]
  transfers between devices with their start and end apart: 43 -> 0, of which waited for: 17 -> 0; matrix products, arithmetic and copies ran while one was open for 19% -> 0% of each run, Pallas kernels for 1% -> 0%
where the time goes in v3:
time: 484 us
  Pallas kernels  460 us (95%)
  local copies, waits for them, and re-layouts  20.7 us (4%)
    pallas_call x1, Pallas kernels, rear(): pl.pallas_call(rear_kernel, in_specs=[vmem] * 8 + [hbm] * 7, out_specs=[v...  250 us
    pallas_call x1, Pallas kernels, front(): pl.pallas_call(front_kernel, in_specs=[vmem] * 7 + [hbm] * 3, out_specs=[...  165 us
    pallas_call x1, Pallas kernels, moe_layer(): pl.pallas_call(moe_kernel, in_specs=[hbm] * 3 + [vmem], out_specs=[hbm, v...  33.8 us
    unnamed x43, local copies, waits for them, and re-layouts  16.8 us

profile of v3, /device:TPU:0, one launch (start us, length us, event | category | flops | bytes accessed | tf_op | source)
XLA Modules:
  0.0 483.8 jit_solution(2359039717458081571)
XLA Ops:
  0.6 0.7 broadcast_in_dim.28.gain_one_ref
  1.4 0.7 broadcast_in_dim.29.gain_two_ref
  2.1 0.1 fusion.1
  2.2 3.0 copy-done.1
  5.2 0.0 copy-start.16
  5.2 3.5 split_experts.1
  8.7 3.0 copy-done
  11.7 165.5 %front.1 = (bf16[256,1536]{1,0:T(8,128)(2,1)S(1)}, bf16[256,768]{1,0:T(8,128)(2,1)S(1)}, bf16[4,256,256]{2,1,0:T(8,128)(2,1)S(1)}, bf16[256,768]{1,0:T(8,128)(2,...) custom-call(bf16[256,1536]{1,0:T(8,128)(2,1)S(1)} %bitcast.29, ...), custom_call_target="tpu_custom_call" | custom-call | tf_op jit(solution)/shard_map/front/pallas_call | solution.py:662
  177.2 0.9 copy-done.6
  178.1 0.9 copy-done.7
  179.0 0.8 copy-done.8
  179.7 0.8 copy-done.9
  180.5 0.7 copy-done.10
  181.3 0.6 copy-done.13
  181.9 33.8 %experts.1 = (bf16[6,1536,384]{2,1,0:T(8,128)(2,1)}, bf16[1024,1536]{1,0:T(8,128)(2,1)}, bf16[1024,1536]{1,0:T(8,128)(2,1)}, f32[1024,128]{1,0:T(8,128)}) custom-call(bf16[1024,1536]{1,0:T(8,128)(2,1)} %bitcast.37, bf16[1024,1536]{1,0:T(8,128)(2,1)} %bitcast.38, bf16[2,3,1536,384]{3,2,1,0:T(8,128)(2,1)} %get-tuple-element.34.w_hbm, f32[4,8,256]{2,1,0:T(8,128)} %copy-done.13), custom_call_target="tpu_custom_call" | custom-call | tf_op jit(solution)/shard_map/experts/pallas_call | solution.py:788
  215.7 250.3 %rear.1 = (bf16[256,1536]{1,0:T(8,128)(2,1)}, bf16[256,1536]{1,0:T(8,128)(2,1)}, f32[8,1536]{1,0:T(8,128)}, f32[256,128]{1,0:T(8,128)}, bf16[384,1792]{1,0:T(8,128)(2,1)}, /*index=5*/bf16[4,6,384,384]{3,2,1,0:T(8,128)(2,1)}) custom-call(f32[128,1536]{1,0:T(8,128)} %copy-done.7, bf16[256,1536]{1,0:T(8,128)(2,1)} %copy-done.6, bf16[256,768]{1,0:T(8,128)(2,1)} %copy-done.9, ...), custom_call_target="tpu_custom_call" | custom-call | tf_op jit(solution)/shard_map/rear/pallas_call | solution.py:1249
  466.0 1.0 copy.20
  467.0 0.6 select_reduce_fusion
  467.6 1.5 slice_reduce_fusion
  469.1 1.7 bitcast_convert_fusion
  470.8 4.4 copy.21
  475.2 6.8 %join_experts.1 = f32[384,3,8,384]{3,2,1,0:T(8,128)} custom-call(bf16[128,128]{1,0:T(8,128)(2,1)S(1)} %get-tuple-element.63.order_ref, bf16[8,3,384,384]{3,2,1,0:T(8,128)(2,1)S(1)} %bitcast.27), custom_call_target="tpu_custom_call" | custom-call | tf_op jit(solution)/shard_map/join_experts/pallas_call | solution.py:368
  482.0 0.9 copy.24
  482.9 0.9 copy.25
  (32 shorter events, 0.1 us)
Async XLA Ops:
  1.4 10.3 %copy-start.11 = (f32[1,1536]{1,0:T(1,128)}, f32[1,1536]{1,0:T(1,128)S(1)}, u32[]{:S(2)}) copy-start(f32[1,1536]{1,0:T(1,128)S(1)} %broadcast_in_dim.28.gain_one_ref) | copy-start | bytes 18436
  2.1 9.6 %copy-start.12 = (f32[1,1536]{1,0:T(1,128)}, f32[1,1536]{1,0:T(1,128)S(1)}, u32[]{:S(2)}) copy-start(f32[1,1536]{1,0:T(1,128)S(1)} %broadcast_in_dim.29.gain_two_ref) | copy-start | bytes 18436
  2.2 3.0 copy-start.1
  5.2 6.5 %copy-start.3 = (bf16[1,256,1536]{2,1,0:T(8,128)(2,1)S(1)}, bf16[1,256,1536]{2,1,0:T(8,128)(2,1)}, u32[]{:S(2)}) copy-start(bf16[1,256,1536]{2,1,0:T(8,128)(2,1)} %param.11) | copy-start | bytes 2359300
  5.2 6.5 %copy-start.4 = (bf16[1,256,1536]{2,1,0:T(8,128)(2,1)S(1)}, bf16[1,256,1536]{2,1,0:T(8,128)(2,1)}, u32[]{:S(2)}) copy-start(bf16[1,256,1536]{2,1,0:T(8,128)(2,1)} %param.19) | copy-start | bytes 2359300
  5.2 6.5 %copy-start.5 = (bf16[384,1,1792]{2,0,1:T(8,128)(2,1)S(1)}, bf16[384,1,1792]{2,0,1:T(8,128)(2,1)}, u32[]{:S(2)}) copy-start(bf16[384,1,1792]{2,0,1:T(8,128)(2,1)} %param.13) | copy-start | bytes 4128772
  5.2 6.5 %copy-start.14 = (s32[1,256,4]{1,2,0:T(4,128)S(1)}, s32[1,256,4]{1,2,0:T(4,128)}, u32[]{:S(2)}) copy-start(s32[1,256,4]{1,2,0:T(4,128)} %param.17) | copy-start | bytes 12292
  5.2 6.5 %copy-start.15 = (f32[1,256,4]{1,2,0:T(4,128)S(1)}, f32[1,256,4]{1,2,0:T(4,128)}, u32[]{:S(2)}) copy-start(f32[1,256,4]{1,2,0:T(4,128)} %param.16) | copy-start | bytes 12292
  5.2 6.5 %copy-start.16 = (f32[1,128]{1,0:T(1,128)S(1)}, f32[1,128]{1,0:T(1,128)}, u32[]{:S(2)}) copy-start(f32[1,128]{1,0:T(1,128)} %constant.66.clone.freq_ref) | copy-start | bytes 1540
  5.2 6.5 %copy-start.17 = (s32[1,256]{1,0:T(1,128)S(1)}, s32[1,256]{1,0:T(1,128)}, u32[]{:S(2)}) copy-start(s32[1,256]{1,0:T(1,128)} %order_ref.1) | copy-start | bytes 3076
  8.7 3.0 copy-start
  177.2 0.9 copy-start.6
  178.1 0.9 copy-start.7
  179.0 0.8 copy-start.8
  179.7 0.8 copy-start.9
  180.5 0.8 copy-start.10
  181.3 0.6 copy-start.13
  469.1 6.0 %copy-start.2 = (bf16[4,6,384,384]{3,2,1,0:T(8,128)(2,1)S(1)}, bf16[4,6,384,384]{3,2,1,0:T(8,128)(2,1)}, u32[]{:S(2)}) copy-start(bf16[4,6,384,384]{3,2,1,0:T(8,128)(2,1)} %get-tuple-element.44) | copy-start | bytes 21233668
  475.2 6.8 %copy-start.19 = (bf16[256,1536]{1,0:T(8,128)(2,1)S(1)}, bf16[256,1536]{1,0:T(8,128)(2,1)}, u32[]{:S(2)}) copy-start(bf16[256,1536]{1,0:T(8,128)(2,1)} %get-tuple-element.41) | copy-start | bytes 2359300
  475.2 7.7 %copy-start.18 = (bf16[256,1536]{1,0:T(8,128)(2,1)S(1)}, bf16[256,1536]{1,0:T(8,128)(2,1)}, u32[]{:S(2)}) copy-start(bf16[256,1536]{1,0:T(8,128)(2,1)} %get-tuple-element.42) | copy-start | bytes 2359300

commit v4 on v3

--- a/solution.py
+++ b/solution.py
@@ -326,33 +326,6 @@
     return (source[:, None] == row[None, :]).astype(jnp.bfloat16)
 
 
-def split_kernel(order_ref, in_ref, out_ref):
-    depth = in_ref.shape[0]
-    for m in range(3):
-        for k in range(depth // 16):
-            block = in_ref[pl.ds(k * 16, 16), m].reshape(128, in_ref.shape[3])
-            moved = jnp.dot(order_ref[...], block, preferred_element_type=jnp.float32)
-            moved = moved.astype(jnp.bfloat16).reshape(8, 16, in_ref.shape[3])
-            out_ref[:, m, pl.ds(k * 16, 16), :] = moved
-
-
-def split_experts(weights, order):
-    rows, _, experts, width = weights.shape
-    step = 64
-    return pl.pallas_call(
-        split_kernel,
-        grid=(rows // step,),
-        in_specs=[
-            pl.BlockSpec((128, 128), lambda i: (0, 0)),
-            pl.BlockSpec((step, 3, experts, width), lambda i: (i, 0, 0, 0)),
-        ],
-        out_specs=pl.BlockSpec((experts, 3, step, width), lambda i: (0, 0, i, 0)),
-        out_shape=jax.ShapeDtypeStruct((experts, 3, rows, width), jnp.bfloat16),
-        compiler_params=pltpu.CompilerParams(vmem_limit_bytes=40 * MIB),
-        name="split_experts",
-    )(order, weights)
-
-
 def join_kernel(order_ref, in_ref, out_ref):
     width = in_ref.shape[3]
     for m in range(3):
@@ -433,7 +406,7 @@
     gates_ref,
     order_ref,
     attn_hbm,
-    pieces_hbm,
+    experts_hbm,
     cot_hbm,
     xn_ref,
     q_ref,
@@ -445,6 +418,8 @@
     w_hbm,
     x_hbm,
     dy_hbm,
+    raw,
+    pieces,
     wa,
     part,
     part_in,
@@ -480,9 +455,11 @@
     rel = [fx, fy, fd]
     line = [at(ctx=lax.rem(z + s, 4)) for s in range(1, 4)]
     sibling = at(tp=1 - c)
+    mine = rows_of(f, shard)
+    load = pltpu.make_async_copy(experts_hbm, raw, local.at[6])
+    load.start()
     greet(plane + line + [sibling])
 
-    mine = rows_of(f, shard)
     owned = pltpu.make_async_copy(attn_hbm, wa.at[mine], local.at[0])
     owned.start()
     in_x = remote(attn_hbm.at[:, ins], wa.at[mine, ins], 0, at(fx))
@@ -506,8 +483,6 @@
     for copy in gate_copies:
         copy.start()
 
-    own_w = pltpu.make_async_copy(pieces_hbm.at[0], w_hbm.at[:, :, mine, :], local.at[1])
-    own_w.start()
     own_dy = [
         pltpu.make_async_copy(
             cot_hbm.at[pl.ds(i * half, half)], dy_hbm.at[i, f], local.at[2 + i]
@@ -515,6 +490,48 @@
         for i in range(2)
     ]
     for copy in own_dy:
+        copy.start()
+
+    row = lax.broadcasted_iota(jnp.int32, (128, 128), 0)
+    column = lax.broadcasted_iota(jnp.int32, (128, 128), 1)
+    owner = jnp.where(row < 64, jnp.where(row < 32, f, fx), jnp.where(row < 96, fy, fd))
+    source = (row % 16) * 8 + owner * 2 + (row // 16) % 2
+    order = jnp.where(source == column, 1.0, 0.0).astype(jnp.bfloat16)
+
+    def split(m):
+        def body(k, _):
+            rows = pl.ds(pl.multiple_of(k * 16, 16), 16)
+            block = raw[rows, m].reshape(128, raw.shape[3])
+            moved = dot_f32(order, block).astype(jnp.bfloat16)
+            pieces[:, m, rows, :] = moved.reshape(8, 16, raw.shape[3])
+            return 0
+
+        lax.fori_loop(0, shard // 16, body, 0)
+
+    cut_rows = shard // 4
+    from_rows = rows_of(z, cut_rows)
+    to_rows = rows_of(4 * f + z, cut_rows)
+
+    def quarter(m, i):
+        return remote(
+            pieces.at[pl.ds(2 * (i + 1), 2), m, from_rows],
+            w_hbm.at[:, m, to_rows, :],
+            37 + 3 * m + i,
+            plane[i],
+        )
+
+    def hand_on(m, i):
+        quarters[3 * m + i].wait_recv()
+        here = w_hbm.at[:, m, rows_of(4 * rel[i] + z, cut_rows), :]
+        copies = [remote(here, here, 43 + 9 * m + 3 * i + s, line[s]) for s in range(3)]
+        for copy in copies:
+            copy.start()
+        return copies
+
+    load.wait()
+    split(0)
+    quarters = [quarter(0, i) for i in range(3)]
+    for copy in quarters:
         copy.start()
 
     tok = tok_ref[...].astype(jnp.float32)
@@ -535,8 +552,16 @@
     in_yx.start()
     out_x = remote(attn_hbm.at[:, outs], wa.at[mine, outs], 7, at(fx))
     out_y = remote(attn_hbm.at[:, outs], wa.at[mine, outs], 8, at(fy))
+    split(1)
+    quarters += [quarter(1, i) for i in range(3)]
+    for copy in quarters[3:]:
+        copy.start()
     out_x.start()
     out_y.start()
+    handed = hand_on(0, 0) + hand_on(0, 1)
+    split(2)
+    own_w = pltpu.make_async_copy(pieces.at[pl.ds(0, 2)], w_hbm.at[:, :, mine, :], local.at[1])
+    own_w.start()
     owned.wait()
     in_xy.wait_recv()
     in_yx.wait_recv()
@@ -566,6 +591,7 @@
         def _(s=s):
             kv_ref[s] = jnp.zeros(kv_ref.shape[1:], jnp.bfloat16)
 
+    handed += hand_on(0, 2)
     out_x.wait_recv()
     out_xy = remote(wa.at[top, outs], wa.at[top, outs], 12, at(fy))
     out_xy.start()
@@ -573,14 +599,10 @@
     out_yx = remote(wa.at[low, outs], wa.at[low, outs], 13, at(fx))
     out_yx.start()
 
-    w_copies = []
-    for m in range(3):
-        for i in range(3):
-            w_copies.append(
-                remote(
-                    pieces_hbm.at[i + 1, :, m], w_hbm.at[:, m, mine, :], 14 + 3 * m + i, plane[i]
-                )
-            )
+    w_copies = [
+        remote(pieces.at[pl.ds(2 * (i + 1), 2), 2], w_hbm.at[:, 2, mine, :], 14 + i, plane[i])
+        for i in range(3)
+    ]
     for copy in w_copies:
         copy.start()
     dy_copies = [
@@ -588,6 +610,8 @@
     ]
     for copy in dy_copies:
         copy.start()
+    for i in range(3):
+        handed += hand_on(1, i)
 
     for s in range(1, 4):
 
@@ -635,7 +659,7 @@
         sib_x.append(remote(x_hbm.at[c, rel[i]], x_hbm.at[c, rel[i]], 34 + i, sibling))
         sib_x[i + 1].start()
 
-    for copy in w_copies + gate_copies + sib_dy + sib_x:
+    for copy in w_copies + gate_copies + handed + sib_dy + sib_x:
         copy.wait_recv()
     for s in range(1, 4):
 
@@ -645,17 +669,17 @@
 
     for copy in [in_x, in_y, in_xy, in_yx, out_x, out_y, out_xy, out_yx, swap]:
         copy.wait_send()
-    for copy in w_copies + gate_copies + dy_copies + x_copies + sib_dy + sib_x:
+    for copy in w_copies + quarters + handed + gate_copies + dy_copies + x_copies + sib_dy + sib_x:
         copy.wait_send()
     for copy in [own_w, own_x, store_wa] + own_dy:
         copy.wait()
 
 
-def front(tok, gain_one, gain_two, routes, gates, order, attn_own, pieces, cot):
+def front(tok, gain_one, gain_two, routes, gates, order, attn_own, weights, cot):
     count, width = tok.shape
     half = count // 2
     shard, columns = attn_own.shape
-    experts, hidden = pieces.shape[1], pieces.shape[4]
+    experts, hidden = EXPERTS // 4, weights.shape[3]
     vmem, hbm = pl.BlockSpec(memory_space=pltpu.VMEM), pl.BlockSpec(memory_space=pl.ANY)
     bf16, f32 = jnp.bfloat16, jnp.float32
     shape = jax.ShapeDtypeStruct
@@ -676,19 +700,21 @@
             shape((2, 4, half, width), bf16),
         ],
         scratch_shapes=[
+            pltpu.VMEM(weights.shape, bf16),
+            pltpu.VMEM((EXPERTS, 3, shard, hidden), bf16),
             pltpu.VMEM((4 * shard, columns), bf16),
             pltpu.VMEM((count, width), f32),
             pltpu.VMEM((half, width), f32),
             pltpu.VMEM((half, width), bf16),
-            pltpu.SemaphoreType.DMA((37,)),
-            pltpu.SemaphoreType.DMA((37,)),
-            pltpu.SemaphoreType.DMA((6,)),
+            pltpu.SemaphoreType.DMA((61,)),
+            pltpu.SemaphoreType.DMA((61,)),
+            pltpu.SemaphoreType.DMA((7,)),
         ],
         compiler_params=pltpu.CompilerParams(
             collective_id=0, has_side_effects=True, vmem_limit_bytes=48 * MIB
         ),
         name="front",
-    )(tok, gain_one, gain_two, frequencies(), routes, gates, order, attn_own, pieces, cot)
+    )(tok, gain_one, gain_two, frequencies(), routes, gates, order, attn_own, weights, cot)
 
 
 def moe_kernel(
@@ -1323,12 +1349,8 @@
     sequence_count, block_len, model_width = tokens.shape
     count = sequence_count * block_len
     half = count // 2
-    own_experts = EXPERTS // 4
     f = lax.axis_index("fsdp")
     shard, hidden = attention_params.shape[0], expert_weights.shape[3]
-    order = expert_order(f)
-    pieces = split_experts(jnp.transpose(expert_weights, (0, 2, 1, 3)), order)
-    pieces = pieces.reshape(4, own_experts, 3, shard, hidden)
     tok = tokens.reshape(count, model_width)
     cot = cotangent.reshape(count, model_width)
     gain_one, gain_two = attn_norm[None, :], ffn_norm[None, :]
@@ -1341,7 +1363,7 @@
         gate_values.reshape(count, TOP).T,
         slot_order.reshape(1, count),
         attention_params[:, 0, :],
-        pieces,
+        jnp.transpose(expert_weights, (0, 2, 1, 3)),
         cot,
     )
     grads, d_normed, moe, gate_parts = moe_layer(
@@ -1366,7 +1388,7 @@
     picked = route_rows[:, :, None] == jnp.arange(EXPERTS, dtype=jnp.int32)
     gate_grad = jnp.sum(jnp.where(picked, gate_rows[:, None, :EXPERTS], 0.0), axis=-1)
     finals = finals.reshape(EXPERTS, 3, shard, hidden)
-    expert_grad = jnp.transpose(join_experts(finals, order.T), (0, 2, 1, 3))
+    expert_grad = jnp.transpose(join_experts(finals, expert_order(f).T), (0, 2, 1, 3))
     return (
         layer_out.reshape(sequence_count, block_len, model_width),
         tokens_grad.reshape(sequence_count, block_len, model_width),

time: 484 us -> 445 us (0.919)
  Pallas kernels: 460 us -> 419 us
    pallas_call x1, Pallas kernels: 165 us -> 128 us  [front(): pl.pallas_call(front_kernel, in_specs=[vmem] * 7 + [hbm] * 3, out_specs=[...]
    unnamed x43 -> x45, local copies, waits for them, and re-layouts: 16.8 us -> 20.1 us
where the time goes in v4:
time: 445 us; the launch traced here: 444 us
  Pallas kernels  419 us (94%)
  local copies, waits for them, and re-layouts  23.1 us (5%)
    pallas_call x1, Pallas kernels, rear(): pl.pallas_call(rear_kernel, in_specs=[vmem] * 8 + [hbm] * 7, out_specs=[v...  251 us
    pallas_call x1, Pallas kernels, front(): pl.pallas_call(front_kernel, in_specs=[vmem] * 7 + [hbm] * 3, out_specs=[...  128 us
    pallas_call x1, Pallas kernels, moe_layer(): pl.pallas_call(moe_kernel, in_specs=[hbm] * 3 + [vmem], out_specs=[hbm, v...  33.8 us
    unnamed x45, local copies, waits for them, and re-layouts  20.1 us

profile of v4, /device:TPU:0, one launch (start us, length us, event | category | flops | bytes accessed | tf_op | source)
XLA Modules:
  0.0 444.0 jit_solution(15796969151824654086)
XLA Ops:
  0.6 0.7 broadcast_in_dim.28.gain_one_ref
  1.3 0.7 broadcast_in_dim.29.gain_two_ref
  2.0 1.1 copy-done.1
  3.2 1.1 copy-done.2
  4.3 1.3 copy-done.3
  5.7 0.7 copy-done.12
  6.3 0.7 copy-done.14
  7.0 0.7 copy-done.15
  7.7 0.7 copy-done.16
  8.4 127.8 %front.1 = (bf16[256,1536]{1,0:T(8,128)(2,1)S(1)}, bf16[256,768]{1,0:T(8,128)(2,1)S(1)}, bf16[4,256,256]{2,1,0:T(8,128)(2,1)S(1)}, bf16[256,768]{1,0:T(8,128)(2,...) custom-call(bf16[256,1536]{1,0:T(8,128)(2,1)S(1)} %bitcast.26, ...), custom_call_target="tpu_custom_call" | custom-call | tf_op jit(solution)/shard_map/front/pallas_call | solution.py:686
  136.2 0.9 copy-done.4
  137.1 0.9 copy-done.5
  137.9 0.8 copy-done.6
  138.7 0.8 copy-done.7
  139.5 0.7 copy-done.8
  140.9 33.8 %experts.1 = (bf16[6,1536,384]{2,1,0:T(8,128)(2,1)}, bf16[1024,1536]{1,0:T(8,128)(2,1)}, bf16[1024,1536]{1,0:T(8,128)(2,1)}, f32[1024,128]{1,0:T(8,128)}) custom-call(bf16[1024,1536]{1,0:T(8,128)(2,1)} %bitcast.35, bf16[1024,1536]{1,0:T(8,128)(2,1)} %bitcast.36, bf16[2,3,1536,384]{3,2,1,0:T(8,128)(2,1)} %get-tuple-element.34.w_hbm, f32[4,8,256]{2,1,0:T(8,128)} %copy-done.11), custom_call_target="tpu_custom_call" | custom-call | tf_op jit(solution)/shard_map/experts/pallas_call | solution.py:814
  174.7 250.8 %rear.1 = (bf16[256,1536]{1,0:T(8,128)(2,1)}, bf16[256,1536]{1,0:T(8,128)(2,1)}, f32[8,1536]{1,0:T(8,128)}, f32[256,128]{1,0:T(8,128)}, bf16[384,1792]{1,0:T(8,128)(2,1)}, /*index=5*/bf16[4,6,384,384]{3,2,1,0:T(8,128)(2,1)}) custom-call(f32[128,1536]{1,0:T(8,128)} %copy-done.5, bf16[256,1536]{1,0:T(8,128)(2,1)} %copy-done.4, bf16[256,768]{1,0:T(8,128)(2,1)} %copy-done.7, ...), custom_call_target="tpu_custom_call" | custom-call | tf_op jit(solution)/shard_map/rear/pallas_call | solution.py:1275
  425.6 3.0 copy-done
  428.6 6.8 %join_experts.1 = f32[384,3,8,384]{3,2,1,0:T(8,128)} custom-call(bf16[128,128]{1,0:T(8,128)(2,1)S(1)} %fusion.order_ref, bf16[8,3,384,384]{3,2,1,0:T(8,128)(2,1)S(1)} %bitcast.24), custom_call_target="tpu_custom_call" | custom-call | tf_op jit(solution)/shard_map/join_experts/pallas_call | solution.py:341
  435.6 4.4 copy.21
  440.0 1.5 slice_reduce_fusion
  441.6 0.6 select_reduce_fusion
  442.2 0.9 copy.24
  443.1 0.9 copy.25
  (33 shorter events, 0.9 us)
Async XLA Ops:
  1.3 134.8 %copy-start.9 = (f32[1,1536]{1,0:T(1,128)}, f32[1,1536]{1,0:T(1,128)S(1)}, u32[]{:S(2)}) copy-start(f32[1,1536]{1,0:T(1,128)S(1)} %broadcast_in_dim.28.gain_one_ref) | copy-start | bytes 18436
  2.0 134.1 %copy-start.10 = (f32[1,1536]{1,0:T(1,128)}, f32[1,1536]{1,0:T(1,128)S(1)}, u32[]{:S(2)}) copy-start(f32[1,1536]{1,0:T(1,128)S(1)} %broadcast_in_dim.29.gain_two_ref) | copy-start | bytes 18436
  2.0 1.1 copy-start.1
  3.2 1.1 copy-start.2
  4.3 1.3 copy-start.3
  5.7 0.7 copy-start.12
  6.3 0.7 copy-start.14
  7.0 0.7 copy-start.15
  7.7 0.7 copy-start.16
  136.2 0.9 copy-start.4
  137.1 0.9 copy-start.5
  137.9 0.8 copy-start.6
  138.7 0.8 copy-start.7
  139.5 0.8 copy-start.8
  140.3 0.6 copy-start.11
  425.6 3.0 copy-start
  428.6 6.8 %copy-start.17 = (bf16[384,1792]{1,0:T(8,128)(2,1)S(1)}, bf16[384,1792]{1,0:T(8,128)(2,1)}, u32[]{:S(2)}) copy-start(bf16[384,1792]{1,0:T(8,128)(2,1)} %get-tuple-element.43) | copy-start | bytes 4128772
  435.6 5.9 %copy-start.20 = (f32[256,128]{1,0:T(8,128)S(1)}, f32[256,128]{1,0:T(8,128)}, u32[]{:S(2)}) copy-start(f32[256,128]{1,0:T(8,128)} %get-tuple-element.46) | copy-start | bytes 393220
  435.6 6.0 %copy-start.13 = (s32[1,256,4]{1,2,0:T(4,128)S(1)}, s32[1,256,4]{1,2,0:T(4,128)}, u32[]{:S(2)}) copy-start(s32[1,256,4]{1,2,0:T(4,128)} %param.17) | copy-start | bytes 12292
  435.6 6.6 %copy-start.19 = (bf16[256,1536]{1,0:T(8,128)(2,1)S(1)}, bf16[256,1536]{1,0:T(8,128)(2,1)}, u32[]{:S(2)}) copy-start(bf16[256,1536]{1,0:T(8,128)(2,1)} %get-tuple-element.41) | copy-start | bytes 2359300
  435.6 7.5 %copy-start.18 = (bf16[256,1536]{1,0:T(8,128)(2,1)S(1)}, bf16[256,1536]{1,0:T(8,128)(2,1)}, u32[]{:S(2)}) copy-start(bf16[256,1536]{1,0:T(8,128)(2,1)} %get-tuple-element.42) | copy-start | bytes 2359300

commit v5 on v4

--- a/solution.py
+++ b/solution.py
@@ -959,7 +959,7 @@
 
     mats = ge.shape[0]
     n_expert = 4 * mats
-    n_attn = 4
+    n_attn = 8
     n_all = n_expert + n_attn
     a_rows = shard // n_attn
 
@@ -972,14 +972,14 @@
         return ra.at[0, rows], a1.at[rows], a2.at[rows]
 
     def add_into(dst, left, right):
-        size = dst.shape[0] // 6
+        size = dst.shape[0] // 3 if dst.shape[0] < 64 else 64
 
         def body(i, _):
             rows = pl.ds(pl.multiple_of(i * size, size), size)
             dst[rows, :] = (left[rows, :].astype(f32) + right[rows, :].astype(f32)).astype(bf16)
             return 0
 
-        lax.fori_loop(0, 6, body, 0)
+        lax.fori_loop(0, dst.shape[0] // size, body, 0)
 
     def first(k):
         own, one, _ = chunk(k)
@@ -1000,13 +1000,20 @@
             return pltpu.make_async_copy(one, fin_hbm.at[0, j], f_out.at[k])
         return copy_to(one, fin_hbm.at[r, j], f_out.at[k], f_in.at[k], plane[r - 1])
 
+    pending = []
+    pace = 2
+    lag_b, lag_c, window = 3, 7, 3
+
     def z_step(i):
+        for copy in pending[:pace]:
+            copy.start()
+        del pending[:pace]
         if i < n_all:
 
             @pl.when(outer)
             def _():
-                if i >= 2:
-                    first(i - 2).wait_send()
+                if i >= window:
+                    first(i - window).wait_send()
                 first(i).start()
 
         if 1 <= i <= n_all:
@@ -1019,8 +1026,8 @@
                 add_into(own, own, one)
                 across(k).start()
 
-        if 2 <= i <= n_all + 1:
-            k = i - 2
+        if lag_b <= i < n_all + lag_b:
+            k = i - lag_b
 
             @pl.when(inner)
             def _():
@@ -1031,8 +1038,8 @@
                 if k < n_expert:
                     final(k).start()
 
-        if 3 <= i <= n_all + 2:
-            k = i - 3
+        if lag_c <= i < n_all + lag_c:
+            k = i - lag_c
 
             @pl.when(outer)
             def _():
@@ -1040,8 +1047,14 @@
                 if k < n_expert:
                     final(k).start()
 
+    steps = iter(range(n_all + max(lag_b, lag_c)))
+
+    def go_on(count=1):
+        for _ in range(count):
+            z_step(next(steps))
+
     loads[0].wait()
-    z_step(0)
+    go_on()
     loads[5].wait()
     loads[6].wait()
 
@@ -1056,7 +1069,9 @@
     gg_out = [remote(gg_sum.at[rel[i + 1]], gg_got.at[i], 6 + i, plane[i]) for i in range(3)]
     for copy in dn_out + gg_out:
         copy.start()
-    z_step(1)
+    go_on(3)
+    for copy in dn_out:
+        copy.wait_recv()
     loads[4].wait()
     mo_swap.wait_recv()
     for g in range(4):
@@ -1064,9 +1079,6 @@
     mo_out = [remote(mo_own.at[rel[i + 1]], mo_got.at[i], 9 + i, plane[i]) for i in range(3)]
     for copy in mo_out:
         copy.start()
-    z_step(2)
-    for copy in dn_out:
-        copy.wait_recv()
     d_two = dn_own[f].astype(f32)
     for i in range(3):
         d_two = d_two + dn_got[i].astype(f32)
@@ -1084,10 +1096,10 @@
     da_swap = remote(dattn.at[my_rows], dattn.at[my_rows], 12, sibling)
     da_swap.start()
     loads[3].wait()
-    z_step(3)
+    go_on()
     da_swap.wait_recv()
     dmixed[...] = dot_f32(dattn[...], wa[:, outs]).astype(bf16)
-    z_step(4)
+    go_on()
 
     position = z * count + lax.broadcasted_iota(jnp.int32, (count, HEAD_DIM), 0)
     angle = position.astype(f32) * freq_ref[...]
@@ -1111,7 +1123,7 @@
         dkv[:, key_cols] += dot_f32(d_scores, query) * scale
         dkv[:, val_cols] += dot_f32(probs.astype(bf16), d_mix)
         if g % 2 == 1:
-            z_step(5 + g // 2)
+            go_on()
     dkv_low[...] = dkv[...].reshape(dkv_low.shape).astype(bf16)
     dkv_out = [
         remote(dkv_low.at[s], dkv_got.at[s - 1], 12 + s, at(ctx=lax.rem(z + 4 - s, 4)))
@@ -1132,21 +1144,30 @@
         lax.fori_loop(0, width // 256, body, 0)
 
     def send_grad(cols, k):
-        copies = [
-            remote(ga.at[rows_of(rel[i + 1], shard), cols], ra.at[i, :, cols], k + i, plane[i])
-            for i in range(3)
-        ]
-        for copy in copies:
-            copy.start()
+        third = shard // 3
+        copies = []
+        for p in range(1 if cols.size < q_cols else 3):
+            size = shard if cols.size < q_cols else third
+            for i in range(3):
+                rows = pl.ds(pl.multiple_of(rel[i + 1] * shard + p * size, size), size)
+                copies.append(
+                    remote(
+                        ga.at[rows, cols],
+                        ra.at[i, pl.ds(p * size, size), cols],
+                        k + 3 * p + i,
+                        plane[i],
+                    )
+                )
+        pending.extend(copies)
         return copies
 
     weight_grad(dattn, mixed_ref[...], outs)
-    ga_copies = send_grad(outs, 16)
-    z_step(8)
+    ga_copies = send_grad(outs, 34)
+    go_on()
     q_part = pl.ds(0, q_cols)
     weight_grad(xn_ref, dproj[:, q_part], q_part)
-    ga_copies += send_grad(q_part, 19)
-    z_step(9)
+    ga_copies += send_grad(q_part, 43)
+    go_on()
     for s in range(1, 4):
 
         @pl.when(z + s < 4)
@@ -1158,8 +1179,8 @@
     dproj[:, pl.ds(q_cols, HEAD_DIM)] = turn(dkv[0:count, key_cols], cosine, sine).astype(bf16)
     dproj[:, pl.ds(q_cols + HEAD_DIM, HEAD_DIM)] = dkv[0:count, val_cols].astype(bf16)
     weight_grad(xn_ref, dproj[:, kv_part], kv_part)
-    ga_copies += send_grad(kv_part, 22)
-    z_step(10)
+    ga_copies += send_grad(kv_part, 16)
+    go_on()
 
     for s in range(width // 256):
         rows = pl.ds(s * 256, 256)
@@ -1167,7 +1188,7 @@
         d1_low[:, rows] = dot_f32(dproj[rows_of(1 - c, half), :], wa[rows, ins], NT).astype(bf16)
     d1_swap = remote(d1_low, d1_in, 25, sibling)
     d1_swap.start()
-    z_step(11)
+    go_on()
     d1_swap.wait_recv()
     d_one = d1[...] + d1_in[...].astype(f32)
     tok = tok_half[...].astype(f32)
@@ -1179,7 +1200,7 @@
     tokgrad_ref[my_rows, :] = (dres[...] + d_norm).astype(bf16)
     tg_swap = remote(tokgrad_ref.at[my_rows], tokgrad_ref.at[my_rows], 26, sibling)
     tg_swap.start()
-    z_step(12)
+    go_on()
 
     for copy in mo_out + gg_out:
         copy.wait_recv()
@@ -1194,13 +1215,13 @@
     gt_swap = remote(gate_ref.at[my_rows], gate_ref.at[my_rows], 28, sibling)
     lo_swap.start()
     gt_swap.start()
-    z_step(13)
+    go_on()
 
     stages = [sibling, at(fx), at(fy), partner, at(ctx=lax.rem(z + 2, 4))]
     gain_copies = [remote(gacc.at[i], gin.at[i], 29 + i, stages[i]) for i in range(5)]
     for i in range(5):
         gain_copies[i].start()
-        z_step(14 + i)
+        go_on()
         gain_copies[i].wait_recv()
         total = gacc[i] + gin[i]
         if i < 4:
@@ -1208,8 +1229,12 @@
         else:
             gains_ref[...] = total
 
-    for i in range(19, n_expert):
+    while (i := next(steps)) < n_expert - 1:
         z_step(i)
+    z_step(i)
+    for copy in pending:
+        copy.start()
+    del pending[:]
     for copy in ga_copies:
         copy.wait_recv()
 
@@ -1223,7 +1248,7 @@
         return 0
 
     lax.fori_loop(0, 8, attn_sum, 0)
-    for i in range(n_expert, n_all + 3):
+    for i in steps:
         z_step(i)
     store = pltpu.make_async_copy(a1, attn_hbm, local.at[0])
     store.start()
@@ -1233,7 +1258,7 @@
 
         @pl.when(outer)
         def _(k=k):
-            if k >= n_all - 2:
+            if k >= n_all - window:
                 first(k).wait_send()
 
         @pl.when(inner)
@@ -1271,7 +1296,7 @@
     bf16, f32 = jnp.bfloat16, jnp.float32
     shape = jax.ShapeDtypeStruct
     dma = pltpu.SemaphoreType.DMA
-    n_all = 4 * mats + 4
+    n_all = 4 * mats + 8
     return pl.pallas_call(
         rear_kernel,
         in_specs=[vmem] * 8 + [hbm] * 7,
@@ -1317,8 +1342,8 @@
             pltpu.VMEM((5, 8, width), f32),
             pltpu.VMEM((half, width), bf16),
             pltpu.VMEM((half, width), bf16),
-            dma((34,)),
-            dma((34,)),
+            dma((52,)),
+            dma((52,)),
             dma((7,)),
             dma((n_all,)),
             dma((n_all,)),

time: 445 us -> 421 us (0.946)
  Pallas kernels: 419 us -> 395 us
    pallas_call x1, Pallas kernels: 251 us -> 227 us  [rear(): pl.pallas_call(rear_kernel, in_specs=[vmem] * 8 + [hbm] * 7, out_specs=[v...]
where the time goes in v5:
time: 421 us; the launch traced here: 420 us
  Pallas kernels  395 us (94%)
  local copies, waits for them, and re-layouts  23.1 us (5%)
    pallas_call x1, Pallas kernels, rear(): pl.pallas_call(rear_kernel, in_specs=[vmem] * 8 + [hbm] * 7, out_specs=[v...  227 us
    pallas_call x1, Pallas kernels, front(): pl.pallas_call(front_kernel, in_specs=[vmem] * 7 + [hbm] * 3, out_specs=[...  128 us
    pallas_call x1, Pallas kernels, moe_layer(): pl.pallas_call(moe_kernel, in_specs=[hbm] * 3 + [vmem], out_specs=[hbm, v...  33.8 us
    unnamed x45, local copies, waits for them, and re-layouts  20.1 us

profile of v5, /device:TPU:0, one launch (start us, length us, event | category | flops | bytes accessed | tf_op | source)
XLA Modules:
  0.0 420.2 jit_solution(344844326269901796)
XLA Ops:
  0.6 0.7 broadcast_in_dim.28.gain_one_ref
  1.3 0.7 broadcast_in_dim.29.gain_two_ref
  2.0 1.1 copy-done.1
  3.2 1.1 copy-done.2
  4.3 1.3 copy-done.3
  5.7 0.7 copy-done.12
  6.3 0.7 copy-done.14
  7.0 0.7 copy-done.15
  7.7 0.7 copy-done.16
  8.4 127.8 %front.1 = (bf16[256,1536]{1,0:T(8,128)(2,1)S(1)}, bf16[256,768]{1,0:T(8,128)(2,1)S(1)}, bf16[4,256,256]{2,1,0:T(8,128)(2,1)S(1)}, bf16[256,768]{1,0:T(8,128)(2,...) custom-call(bf16[256,1536]{1,0:T(8,128)(2,1)S(1)} %bitcast.26, ...), custom_call_target="tpu_custom_call" | custom-call | tf_op jit(solution)/shard_map/front/pallas_call | solution.py:686
  136.2 0.9 copy-done.4
  137.1 0.9 copy-done.5
  137.9 0.8 copy-done.6
  138.7 0.8 copy-done.7
  139.5 0.7 copy-done.8
  140.9 33.8 %experts.1 = (bf16[6,1536,384]{2,1,0:T(8,128)(2,1)}, bf16[1024,1536]{1,0:T(8,128)(2,1)}, bf16[1024,1536]{1,0:T(8,128)(2,1)}, f32[1024,128]{1,0:T(8,128)}) custom-call(bf16[1024,1536]{1,0:T(8,128)(2,1)} %bitcast.35, bf16[1024,1536]{1,0:T(8,128)(2,1)} %bitcast.36, bf16[2,3,1536,384]{3,2,1,0:T(8,128)(2,1)} %get-tuple-element.34.w_hbm, f32[4,8,256]{2,1,0:T(8,128)} %copy-done.11), custom_call_target="tpu_custom_call" | custom-call | tf_op jit(solution)/shard_map/experts/pallas_call | solution.py:814
  174.7 227.0 %rear.1 = (bf16[256,1536]{1,0:T(8,128)(2,1)}, bf16[256,1536]{1,0:T(8,128)(2,1)}, f32[8,1536]{1,0:T(8,128)}, f32[256,128]{1,0:T(8,128)}, bf16[384,1792]{1,0:T(8,128)(2,1)}, /*index=5*/bf16[4,6,384,384]{3,2,1,0:T(8,128)(2,1)}) custom-call(f32[128,1536]{1,0:T(8,128)} %copy-done.5, bf16[256,1536]{1,0:T(8,128)(2,1)} %copy-done.4, bf16[256,768]{1,0:T(8,128)(2,1)} %copy-done.7, ...), custom_call_target="tpu_custom_call" | custom-call | tf_op jit(solution)/shard_map/rear/pallas_call | solution.py:1300
  401.8 3.0 copy-done
  404.8 6.8 %join_experts.1 = f32[384,3,8,384]{3,2,1,0:T(8,128)} custom-call(bf16[128,128]{1,0:T(8,128)(2,1)S(1)} %fusion.order_ref, bf16[8,3,384,384]{3,2,1,0:T(8,128)(2,1)S(1)} %bitcast.24), custom_call_target="tpu_custom_call" | custom-call | tf_op jit(solution)/shard_map/join_experts/pallas_call | solution.py:341
  411.8 4.4 %copy.21 = f32[384,1,1792]{2,1,0:T(1,128)} copy(f32[384,1,1792]{2,0,1:T(8,128)S(1)} %bitcast_convert_fusion) | data formatting | bytes 5505024
  416.2 1.5 slice_reduce_fusion
  417.8 0.6 select_reduce_fusion
  418.4 0.9 copy.24
  419.3 0.9 copy.25
  (33 shorter events, 0.9 us)
Async XLA Ops:
  1.3 134.8 %copy-start.9 = (f32[1,1536]{1,0:T(1,128)}, f32[1,1536]{1,0:T(1,128)S(1)}, u32[]{:S(2)}) copy-start(f32[1,1536]{1,0:T(1,128)S(1)} %broadcast_in_dim.28.gain_one_ref) | copy-start | bytes 18436
  2.0 134.1 %copy-start.10 = (f32[1,1536]{1,0:T(1,128)}, f32[1,1536]{1,0:T(1,128)S(1)}, u32[]{:S(2)}) copy-start(f32[1,1536]{1,0:T(1,128)S(1)} %broadcast_in_dim.29.gain_two_ref) | copy-start | bytes 18436
  2.0 1.1 copy-start.1
  3.2 1.1 copy-start.2
  4.3 1.3 copy-start.3
  5.7 0.7 copy-start.12
  6.3 0.7 copy-start.14
  7.0 0.7 copy-start.15
  7.7 0.7 copy-start.16
  136.2 0.9 copy-start.4
  137.1 0.9 copy-start.5
  137.9 0.8 copy-start.6
  138.7 0.8 copy-start.7
  139.5 0.8 copy-start.8
  140.3 0.6 copy-start.11
  401.8 3.0 copy-start
  404.8 6.8 %copy-start.17 = (bf16[384,1792]{1,0:T(8,128)(2,1)S(1)}, bf16[384,1792]{1,0:T(8,128)(2,1)}, u32[]{:S(2)}) copy-start(bf16[384,1792]{1,0:T(8,128)(2,1)} %get-tuple-element.43) | copy-start | bytes 4128772
  411.8 5.9 %copy-start.20 = (f32[256,128]{1,0:T(8,128)S(1)}, f32[256,128]{1,0:T(8,128)}, u32[]{:S(2)}) copy-start(f32[256,128]{1,0:T(8,128)} %get-tuple-element.46) | copy-start | bytes 393220
  411.8 6.0 %copy-start.13 = (s32[1,256,4]{1,2,0:T(4,128)S(1)}, s32[1,256,4]{1,2,0:T(4,128)}, u32[]{:S(2)}) copy-start(s32[1,256,4]{1,2,0:T(4,128)} %param.17) | copy-start | bytes 12292
  411.8 6.6 %copy-start.19 = (bf16[256,1536]{1,0:T(8,128)(2,1)S(1)}, bf16[256,1536]{1,0:T(8,128)(2,1)}, u32[]{:S(2)}) copy-start(bf16[256,1536]{1,0:T(8,128)(2,1)} %get-tuple-element.41) | copy-start | bytes 2359300
  411.8 7.5 %copy-start.18 = (bf16[256,1536]{1,0:T(8,128)(2,1)S(1)}, bf16[256,1536]{1,0:T(8,128)(2,1)}, u32[]{:S(2)}) copy-start(bf16[256,1536]{1,0:T(8,128)(2,1)} %get-tuple-element.42) | copy-start | bytes 2359300

commit v6 on v5

--- a/solution.py
+++ b/solution.py
@@ -1,6 +1,7 @@
 import jax
 import jax.numpy as jnp
 from jax import lax
+import math
 import numpy as np
 from jax.experimental import pallas as pl
 from jax.experimental.pallas import tpu as pltpu
@@ -326,30 +327,44 @@
     return (source[:, None] == row[None, :]).astype(jnp.bfloat16)
 
 
-def join_kernel(order_ref, in_ref, out_ref):
+def join_kernel(order_ref, in_ref, attn_in_ref, out_ref, attn_out_ref):
     width = in_ref.shape[3]
     for m in range(3):
         for k in range(in_ref.shape[2] // 16):
             block = in_ref[:, m, pl.ds(k * 16, 16), :].reshape(128, width)
             moved = jnp.dot(order_ref[...], block, preferred_element_type=jnp.float32)
             out_ref[pl.ds(k * 16, 16), m] = moved.reshape(16, 8, width)
-
-
-def join_experts(grads, order):
+    rows, columns = attn_in_ref.shape
+    parts = columns // 128
+    for j in range(parts):
+        part = attn_in_ref[:, pl.ds(j * 128, 128)].astype(jnp.float32)
+        attn_out_ref[pl.ds(j, rows, stride=parts), :] = part
+
+
+def join_experts(grads, attn_grad, order):
     experts, _, rows, width = grads.shape
+    columns = attn_grad.shape[1]
     step = 64
+    lines = step * columns // 128
     return pl.pallas_call(
         join_kernel,
         grid=(rows // step,),
         in_specs=[
             pl.BlockSpec((128, 128), lambda i: (0, 0)),
             pl.BlockSpec((experts, 3, step, width), lambda i: (0, 0, i, 0)),
+            pl.BlockSpec((step, columns), lambda i: (i, 0)),
         ],
-        out_specs=pl.BlockSpec((step, 3, experts, width), lambda i: (i, 0, 0, 0)),
-        out_shape=jax.ShapeDtypeStruct((rows, 3, experts, width), jnp.float32),
-        compiler_params=pltpu.CompilerParams(vmem_limit_bytes=40 * MIB),
+        out_specs=[
+            pl.BlockSpec((step, 3, experts, width), lambda i: (i, 0, 0, 0)),
+            pl.BlockSpec((lines, 128), lambda i: (i, 0)),
+        ],
+        out_shape=[
+            jax.ShapeDtypeStruct((rows, 3, experts, width), jnp.float32),
+            jax.ShapeDtypeStruct((rows * columns // 128, 128), jnp.float32),
+        ],
+        compiler_params=pltpu.CompilerParams(vmem_limit_bytes=60 * MIB),
         name="join_experts",
-    )(order, grads)
+    )(order, grads, attn_grad)
 
 
 NT = (((1,), (1,)), ((), ()))
@@ -711,131 +726,17 @@
             pltpu.SemaphoreType.DMA((7,)),
         ],
         compiler_params=pltpu.CompilerParams(
-            collective_id=0, has_side_effects=True, vmem_limit_bytes=48 * MIB
+            collective_id=0, has_side_effects=True, vmem_limit_bytes=60 * MIB
         ),
         name="front",
     )(tok, gain_one, gain_two, frequencies(), routes, gates, order, attn_own, weights, cot)
 
 
-def moe_kernel(
-    x_hbm, dy_hbm, w_hbm, wl_ref, ge_hbm, dn_ref, mo_ref, gg_ref, x, dy, wgu, wd, gu, hid, ge, scales, sem, out_sem
-):
-    f = lax.axis_index("fsdp")
-    tokens, width = x.shape
-    hidden = w_hbm.shape[3]
-    half = tokens // 8
-    tile = 2 * half
-    own = w_hbm.shape[0]
-    loads = [pltpu.make_async_copy(x_hbm, x, sem.at[0])]
-    for e in range(own):
-        for m in range(2):
-            loads.append(
-                pltpu.make_async_copy(
-                    w_hbm.at[e, m], wgu.at[:, pl.ds((2 * e + m) * hidden, hidden)], sem.at[1 + 3 * e + m]
-                )
-            )
-    loads.append(pltpu.make_async_copy(dy_hbm, dy, sem.at[7]))
-    for e in range(own):
-        loads.append(
-            pltpu.make_async_copy(w_hbm.at[e, 2], wd.at[:, pl.ds(e * hidden, hidden)], sem.at[3 + 3 * e])
-        )
-    for copy in loads:
-        copy.start()
-    lane = lax.broadcasted_iota(jnp.int32, (half, 128), 1)
-    for b in range(8):
-        rows = wl_ref[b % 4, :, pl.ds((b // 4) * half, half)]
-        rows = jnp.concatenate([rows, jnp.zeros((128 - EXPERTS, half), jnp.float32)], axis=0)
-        scales[pl.ds(b * half, half), :] = rows.T
-    for copy in loads:
-        copy.wait()
-
-    lanes = lax.broadcasted_iota(jnp.int32, (tile, 128), 1)
-
-    def step(i, _):
-        rows = pl.ds(pl.multiple_of(i * tile, tile), tile)
-        acts = dot_f32(x[rows, :], wgu[...])
-        plain = dot_f32(dy[rows, :], wd[...])
-        table = scales[rows, :]
-        sums = jnp.zeros((tile, 128), jnp.float32)
-        for e in range(own):
-            gate_act = acts[:, 2 * e * hidden : (2 * e + 1) * hidden]
-            up_act = acts[:, (2 * e + 1) * hidden : (2 * e + 2) * hidden]
-            d_plain = plain[:, e * hidden : (e + 1) * hidden]
-            here = lanes == own * f + e
-            scale = jnp.sum(jnp.where(here, table, 0.0), axis=1, keepdims=True)
-            sigmoid = 1.0 / (1.0 + jnp.exp(-gate_act))
-            active = gate_act * sigmoid
-            act = active * up_act
-            total = jnp.sum(act * d_plain, axis=1, keepdims=True)
-            sums = jnp.where(here, jnp.where(scale != 0.0, total, 0.0), sums)
-            d_hidden = d_plain * scale
-            slope = sigmoid * (1.0 + gate_act * (1.0 - sigmoid))
-            hid[rows, pl.ds(e * hidden, hidden)] = (act * scale).astype(jnp.bfloat16)
-            gu[rows, pl.ds(2 * e * hidden, hidden)] = (d_hidden * up_act * slope).astype(jnp.bfloat16)
-            gu[rows, pl.ds((2 * e + 1) * hidden, hidden)] = (d_hidden * active).astype(jnp.bfloat16)
-        gg_ref[rows, :] = sums
-        return 0
-
-    lax.fori_loop(0, tokens // tile, step, 0)
-
-    block = width // 4
-
-    def grad_step(s, _):
-        cols = pl.ds(pl.multiple_of(s * block, 128), block)
-        inner = dot_f32(x[:, cols], gu[...], TN).astype(jnp.bfloat16)
-        outer = dot_f32(dy[:, cols], hid[...], TN).astype(jnp.bfloat16)
-        for e in range(own):
-            for m in range(2):
-                k = 2 * e + m
-                ge[3 * e + m, cols, :] = inner[:, k * hidden : (k + 1) * hidden]
-            ge[3 * e + 2, cols, :] = outer[:, e * hidden : (e + 1) * hidden]
-        return 0
-
-    lax.fori_loop(0, 4, grad_step, 0)
-    store = pltpu.make_async_copy(ge, ge_hbm, out_sem)
-    store.start()
-
-    def down_step(i, _):
-        rows = pl.ds(pl.multiple_of(i * tile, tile), tile)
-        dn_ref[rows, :] = dot_f32(gu[rows, :], wgu[...], NT).astype(jnp.bfloat16)
-        mo_ref[rows, :] = dot_f32(hid[rows, :], wd[...], NT).astype(jnp.bfloat16)
-        return 0
-
-    lax.fori_loop(0, tokens // tile, down_step, 0)
-    store.wait()
-
-
-def moe_layer(x, dy, weights, gate_table):
-    tokens, width = x.shape
-    own, _, _, hidden = weights.shape
-    vmem, hbm = pl.BlockSpec(memory_space=pltpu.VMEM), pl.BlockSpec(memory_space=pl.ANY)
-    bf16, f32 = jnp.bfloat16, jnp.float32
-    shape = jax.ShapeDtypeStruct
-    return pl.pallas_call(
-        moe_kernel,
-        in_specs=[hbm] * 3 + [vmem],
-        out_specs=[hbm, vmem, vmem, vmem],
-        out_shape=[
-            shape((3 * own, width, hidden), bf16),
-            shape((tokens, width), bf16),
-            shape((tokens, width), bf16),
-            shape((tokens, 128), f32),
-        ],
-        scratch_shapes=[
-            pltpu.VMEM((tokens, width), bf16),
-            pltpu.VMEM((tokens, width), bf16),
-            pltpu.VMEM((width, 2 * own * hidden), bf16),
-            pltpu.VMEM((width, own * hidden), bf16),
-            pltpu.VMEM((tokens, 2 * own * hidden), bf16),
-            pltpu.VMEM((tokens, own * hidden), bf16),
-            pltpu.VMEM((3 * own, width, hidden), bf16),
-            pltpu.VMEM((tokens, 128), f32),
-            pltpu.SemaphoreType.DMA((8,)),
-            pltpu.SemaphoreType.DMA,
-        ],
-        compiler_params=pltpu.CompilerParams(vmem_limit_bytes=58 * MIB),
-        name="experts",
-    )(x, dy, weights, gate_table)
+def ctx_chunks(mats, shard):
+    early = [(0, 0), (1, 0)]
+    chunks = [(j, r, 0, shard) for j, r in early]
+    chunks += [(j, r, 0, shard) for j in range(mats) for r in range(4) if (j, r) not in early]
+    return chunks, [shard // 8] * 8
 
 
 def rear_kernel(
@@ -849,10 +750,10 @@
     freq_ref,
     tok_hbm,
     cot_hbm,
-    ge_hbm,
-    dn_hbm,
-    mo_hbm,
-    gg_hbm,
+    x_hbm,
+    dy_hbm,
+    w_hbm,
+    wl_ref,
     wa_hbm,
     layer_ref,
     tokgrad_ref,
@@ -860,17 +761,18 @@
     gate_ref,
     attn_hbm,
     fin_hbm,
+    xy,
+    wgu,
+    wd,
+    gu,
+    hid,
+    table,
     ge,
     r1,
-    r2,
-    wa,
-    dn_own,
     dn_in,
     dn_got,
-    mo_own,
     mo_in,
     mo_got,
-    gg_own,
     gg_in,
     gg_sum,
     gg_got,
@@ -884,10 +786,8 @@
     d1,
     d1_low,
     d1_in,
-    ga,
     ra,
     a1,
-    a2,
     gacc,
     gin,
     tok_half,
@@ -902,6 +802,7 @@
     z_r2,
     f_out,
     f_in,
+    credit,
 ):
     f, z, c = place()
     fx, fy, fd = plane_peers(f)
@@ -940,39 +841,99 @@
     inner = (z == 1) | (z == 2)
     outer = (z == 0) | (z == 3)
 
-    loads = [pltpu.make_async_copy(ge_hbm, ge, local.at[0])]
-    loads.append(pltpu.make_async_copy(dn_hbm.at[c], dn_own, local.at[1]))
-    loads.append(pltpu.make_async_copy(gg_hbm.at[c], gg_own, local.at[2]))
-    loads.append(pltpu.make_async_copy(wa_hbm, wa, local.at[3]))
-    loads.append(pltpu.make_async_copy(mo_hbm.at[c], mo_own, local.at[4]))
-    loads.append(pltpu.make_async_copy(tok_hbm.at[rows_of(c, half)], tok_half, local.at[5]))
-    loads.append(pltpu.make_async_copy(cot_hbm.at[rows_of(c, half)], cot_half, local.at[6]))
+    own = w_hbm.shape[0]
+    hidden = w_hbm.shape[3]
+    tokens = 8 * half
+    tile = 2 * half
+    loads = [pltpu.make_async_copy(x_hbm, xy.at[pl.ds(0, tokens)], local.at[0])]
+    for e in range(own):
+        for m in range(2):
+            cols = pl.ds((2 * e + m) * hidden, hidden)
+            loads.append(pltpu.make_async_copy(w_hbm.at[e, m], wgu.at[:, cols], local.at[1 + 2 * e + m]))
+    loads.append(pltpu.make_async_copy(dy_hbm, xy.at[pl.ds(tokens, tokens)], local.at[5]))
+    for e in range(own):
+        cols = pl.ds(e * hidden, hidden)
+        loads.append(pltpu.make_async_copy(w_hbm.at[e, 2], wd.at[:, cols], local.at[6 + e]))
+    my_rows = rows_of(c, half)
+    loads.append(pltpu.make_async_copy(tok_hbm.at[my_rows], tok_half, local.at[8]))
+    loads.append(pltpu.make_async_copy(cot_hbm.at[my_rows], cot_half, local.at[9]))
     for copy in loads:
         copy.start()
     greet(plane + line + [sibling])
-    dn_swap = remote(dn_hbm.at[1 - c], dn_in, 0, sibling)
-    gg_swap = remote(gg_hbm.at[1 - c], gg_in, 1, sibling)
-    mo_swap = remote(mo_hbm.at[1 - c], mo_in, 2, sibling)
-    dn_swap.start()
+    for b in range(8):
+        rows = wl_ref[b % 4, :, pl.ds((b // 4) * half, half)]
+        rows = jnp.concatenate([rows, jnp.zeros((128 - EXPERTS, half), f32)], axis=0)
+        table[pl.ds(b * half, half), :] = rows.T
+    for copy in loads:
+        copy.wait()
+
+    lanes = lax.broadcasted_iota(jnp.int32, (tile, 128), 1)
+
+    def act_step(i, _):
+        rows = pl.ds(pl.multiple_of(i * tile, tile), tile)
+        acts = dot_f32(xy[rows, :], wgu[...])
+        plain = dot_f32(xy[pl.ds(pl.multiple_of(tokens + i * tile, tile), tile), :], wd[...])
+        scales = table[rows, :]
+        sums = jnp.zeros((tile, 128), f32)
+        for e in range(own):
+            gate_act = acts[:, 2 * e * hidden : (2 * e + 1) * hidden]
+            up_act = acts[:, (2 * e + 1) * hidden : (2 * e + 2) * hidden]
+            d_plain = plain[:, e * hidden : (e + 1) * hidden]
+            here = lanes == own * f + e
+            factor = jnp.sum(jnp.where(here, scales, 0.0), axis=1, keepdims=True)
+            sigmoid = 1.0 / (1.0 + jnp.exp(-gate_act))
+            active = gate_act * sigmoid
+            act = active * up_act
+            total = jnp.sum(act * d_plain, axis=1, keepdims=True)
+            sums = jnp.where(here, jnp.where(factor != 0.0, total, 0.0), sums)
+            d_hidden = d_plain * factor
+            slope = sigmoid * (1.0 + gate_act * (1.0 - sigmoid))
+            hid[rows, pl.ds(e * hidden, hidden)] = (act * factor).astype(bf16)
+            gu[rows, pl.ds(2 * e * hidden, hidden)] = (d_hidden * up_act * slope).astype(bf16)
+            gu[rows, pl.ds((2 * e + 1) * hidden, hidden)] = (d_hidden * active).astype(bf16)
+        table[rows, :] = sums
+        return 0
+
+    lax.fori_loop(0, tokens // tile, act_step, 0)
+    side, far = rows_of(c, 4 * half), rows_of(1 - c, 4 * half)
+    gg_swap = remote(table.at[far], gg_in, 1, sibling)
     gg_swap.start()
-    mo_swap.start()
-
-    mats = ge.shape[0]
-    n_expert = 4 * mats
-    n_attn = 8
-    n_all = n_expert + n_attn
-    a_rows = shard // n_attn
+
+    def grad_step(t, _):
+        cols = pl.ds(pl.multiple_of(lax.rem(f + t, 4) * shard, 128), shard)
+        into_in = dot_f32(xy[pl.ds(0, tokens), cols], gu[...], TN).astype(bf16)
+        into_out = dot_f32(xy[pl.ds(tokens, tokens), cols], hid[...], TN).astype(bf16)
+        for e in range(own):
+            for m in range(2):
+                k = 2 * e + m
+                ge[3 * e + m, cols, :] = into_in[:, k * hidden : (k + 1) * hidden]
+            ge[3 * e + 2, cols, :] = into_out[:, e * hidden : (e + 1) * hidden]
+        return 0
+
+    def down_step(i, _):
+        rows = pl.ds(pl.multiple_of(i * tile, tile), tile)
+        ra[rows, pl.ds(0, width)] = dot_f32(gu[rows, :], wgu[...], NT).astype(bf16)
+        return 0
+
+    def out_step(i, _):
+        rows = pl.ds(pl.multiple_of(i * tile, tile), tile)
+        xy[rows, :] = dot_f32(hid[rows, :], wd[...], NT).astype(bf16)
+        return 0
+
+    chunks, attn_rows = ctx_chunks(ge.shape[0], shard)
+    n_expert = len(chunks)
+    n_all = n_expert + len(attn_rows)
 
     def chunk(k):
         if k < n_expert:
-            j, r = k // 4, k % 4
-            rows = rows_of(rel[r], shard)
-            return ge.at[j, rows], r1.at[j, rows], r2.at[j, rows]
-        rows = pl.ds((k - n_expert) * a_rows, a_rows)
-        return ra.at[0, rows], a1.at[rows], a2.at[rows]
+            j, r, low, size = chunks[k]
+            rows = pl.ds(pl.multiple_of(rel[r] * shard + low, 16), size)
+            return ge.at[j, rows], r1.at[j, rows]
+        rows = pl.ds(sum(attn_rows[: k - n_expert]), attn_rows[k - n_expert])
+        return ra.at[rows], a1.at[rows]
 
     def add_into(dst, left, right):
-        size = dst.shape[0] // 3 if dst.shape[0] < 64 else 64
+        size = math.gcd(dst.shape[0], 64)
 
         def body(i, _):
             rows = pl.ds(pl.multiple_of(i * size, size), size)
@@ -982,32 +943,30 @@
         lax.fori_loop(0, dst.shape[0] // size, body, 0)
 
     def first(k):
-        own, one, _ = chunk(k)
+        own, one = chunk(k)
         return copy_to(own, one, z_out.at[k], z_r1.at[k], partner)
 
     def across(k):
-        own, _, two = chunk(k)
-        return copy_to(own, two, z_across.at[k], z_r2.at[k], opposite)
+        own, one = chunk(k)
+        return copy_to(own, one, z_across.at[k], z_r2.at[k], opposite)
 
     def back(k):
-        _, one, _ = chunk(k)
+        _, one = chunk(k)
         return copy_to(one, one, z_back.at[k], z_r1.at[k], partner)
 
     def final(k):
-        _, one, _ = chunk(k)
-        j, r = k // 4, k % 4
+        _, one = chunk(k)
+        j, r, low, size = chunks[k]
+        there = fin_hbm.at[r, j, pl.ds(low, size)]
         if r == 0:
-            return pltpu.make_async_copy(one, fin_hbm.at[0, j], f_out.at[k])
-        return copy_to(one, fin_hbm.at[r, j], f_out.at[k], f_in.at[k], plane[r - 1])
-
-    pending = []
+            return pltpu.make_async_copy(one, there, f_out.at[k])
+        return copy_to(one, there, f_out.at[k], f_in.at[k], plane[r - 1])
+
+    pending, ready = [], []
     pace = 2
-    lag_b, lag_c, window = 3, 7, 3
+    lag_a, lag_b, lag_c, window = 1, 3, 6, 3
 
     def z_step(i):
-        for copy in pending[:pace]:
-            copy.start()
-        del pending[:pace]
         if i < n_all:
 
             @pl.when(outer)
@@ -1016,14 +975,22 @@
                     first(i - window).wait_send()
                 first(i).start()
 
-        if 1 <= i <= n_all:
-            k = i - 1
+        if lag_a <= i < n_all + lag_a:
+            k = i - lag_a
 
             @pl.when(inner)
             def _():
-                own, one, _ = chunk(k)
+                own, one = chunk(k)
                 first(k).wait_recv()
                 add_into(own, own, one)
+                pl.semaphore_signal(credit, inc=1, device_id=opposite, device_id_type=MESH_ID)
+
+        if lag_a <= i < n_all + lag_a:
+            k = i - lag_a
+
+            @pl.when(inner)
+            def _():
+                pl.semaphore_wait(credit, 1)
                 across(k).start()
 
         if lag_b <= i < n_all + lag_b:
@@ -1031,12 +998,10 @@
 
             @pl.when(inner)
             def _():
-                own, one, two = chunk(k)
+                own, one = chunk(k)
                 across(k).wait_recv()
-                add_into(one, own, two)
+                add_into(one, own, one)
                 back(k).start()
-                if k < n_expert:
-                    final(k).start()
 
         if lag_c <= i < n_all + lag_c:
             k = i - lag_c
@@ -1044,8 +1009,15 @@
             @pl.when(outer)
             def _():
                 back(k).wait_recv()
-                if k < n_expert:
-                    final(k).start()
+
+            if k < n_expert:
+                ready.append(k)
+
+        for _ in range(pace):
+            if pending:
+                pending.pop(0).start()
+            elif ready:
+                final(ready.pop(0)).start()
 
     steps = iter(range(n_all + max(lag_b, lag_c)))
 
@@ -1053,33 +1025,59 @@
         for _ in range(count):
             z_step(next(steps))
 
-    loads[0].wait()
+    wide = pl.ds(0, width)
+    lax.fori_loop(0, 1, grad_step, 0)
     go_on()
-    loads[5].wait()
-    loads[6].wait()
-
-    loads[1].wait()
-    loads[2].wait()
+    lax.fori_loop(2 * (1 - c), 2 * (1 - c) + 2, down_step, 0)
+    dn_swap = remote(ra.at[far, wide], dn_in, 0, sibling)
+    dn_swap.start()
+    lax.fori_loop(2 * c, 2 * c + 2, down_step, 0)
+    go_on()
+
+    def both(ref, arrived):
+        def body(i, _):
+            rows = pl.ds(pl.multiple_of(c * 4 * half + i * half, half), half)
+            here = pl.ds(pl.multiple_of(i * half, half), half)
+            ref[rows, wide] = (ref[rows, wide].astype(f32) + arrived[here, :].astype(f32)).astype(bf16)
+            return 0
+
+        lax.fori_loop(0, 4, body, 0)
+
+    def group(i):
+        return rows_of(4 * c + i, half)
+
     gg_swap.wait_recv()
-    gg_sum[...] = gg_own[...] + gg_in[...]
+    gg_sum[...] = table[side, :] + gg_in[...]
     dn_swap.wait_recv()
-    for g in range(4):
-        dn_own[g] = (dn_own[g].astype(f32) + dn_in[g].astype(f32)).astype(bf16)
-    dn_out = [remote(dn_own.at[rel[i + 1]], dn_got.at[i], 3 + i, plane[i]) for i in range(3)]
-    gg_out = [remote(gg_sum.at[rel[i + 1]], gg_got.at[i], 6 + i, plane[i]) for i in range(3)]
+    both(ra, dn_in)
+    dn_out = [
+        remote(ra.at[group(rel[i + 1]), wide], dn_got.at[i], 3 + i, plane[i]) for i in range(3)
+    ]
+    gg_out = [
+        remote(gg_sum.at[rows_of(rel[i + 1], half)], gg_got.at[i], 6 + i, plane[i])
+        for i in range(3)
+    ]
     for copy in dn_out + gg_out:
         copy.start()
-    go_on(3)
+    lax.fori_loop(1, 4, grad_step, 0)
+    go_on()
+    lax.fori_loop(2 * (1 - c), 2 * (1 - c) + 2, out_step, 0)
+    mo_swap = remote(xy.at[far], mo_in, 2, sibling)
+    mo_swap.start()
+    lax.fori_loop(2 * c, 2 * c + 2, out_step, 0)
+    in_part, out_part = pl.ds(0, in_cols), pl.ds(0, q_cols)
+    load_in = pltpu.make_async_copy(wa_hbm.at[:, ins], wgu.at[:, in_part], local.at[0])
+    load_out = pltpu.make_async_copy(wa_hbm.at[:, outs], wd, local.at[1])
+    load_out.start()
+    load_in.start()
+    go_on()
     for copy in dn_out:
         copy.wait_recv()
-    loads[4].wait()
+    for copy in dn_out + [dn_swap]:
+        copy.wait_send()
     mo_swap.wait_recv()
-    for g in range(4):
-        mo_own[g] = (mo_own[g].astype(f32) + mo_in[g].astype(f32)).astype(bf16)
-    mo_out = [remote(mo_own.at[rel[i + 1]], mo_got.at[i], 9 + i, plane[i]) for i in range(3)]
-    for copy in mo_out:
-        copy.start()
-    d_two = dn_own[f].astype(f32)
+    both(xy, mo_in)
+    d_two = ra[group(f), wide].astype(f32)
     for i in range(3):
         d_two = d_two + dn_got[i].astype(f32)
     residual = res_ref[...]
@@ -1089,16 +1087,18 @@
     d_norm = inv * scaled - residual * (inv * inv * inv * inside)
     gacc[0] = jnp.zeros(gacc.shape[1:], f32)
     gacc[0, 1:2, :] = jnp.sum(d_two * residual * inv, axis=0, keepdims=True)
-    my_rows = rows_of(c, half)
     d_res = cot_half[...].astype(f32) + d_norm
     dres[...] = d_res
     dattn[my_rows, :] = d_res.astype(bf16)
     da_swap = remote(dattn.at[my_rows], dattn.at[my_rows], 12, sibling)
     da_swap.start()
-    loads[3].wait()
+    mo_out = [remote(xy.at[group(rel[i + 1])], mo_got.at[i], 9 + i, plane[i]) for i in range(3)]
+    for copy in mo_out:
+        copy.start()
+    load_out.wait()
     go_on()
     da_swap.wait_recv()
-    dmixed[...] = dot_f32(dattn[...], wa[:, outs]).astype(bf16)
+    dmixed[...] = dot_f32(dattn[...], wd[...]).astype(bf16)
     go_on()
 
     position = z * count + lax.broadcasted_iota(jnp.int32, (count, HEAD_DIM), 0)
@@ -1122,7 +1122,7 @@
         dproj[:, cols] = turn(d_query, cosine, sine).astype(bf16)
         dkv[:, key_cols] += dot_f32(d_scores, query) * scale
         dkv[:, val_cols] += dot_f32(probs.astype(bf16), d_mix)
-        if g % 2 == 1:
+        if g % 3 == 2:
             go_on()
     dkv_low[...] = dkv[...].reshape(dkv_low.shape).astype(bf16)
     dkv_out = [
@@ -1135,25 +1135,26 @@
         def _(s=s):
             dkv_out[s - 1].start()
 
+    low_rows = pl.ds(4 * shard, shard)
+
     def weight_grad(left, right, cols):
         def body(i, _):
             rows = pl.ds(pl.multiple_of(i * 256, 256), 256)
-            ga[rows, cols] = dot_f32(left[:, rows], right, TN).astype(bf16)
+            xy[rows, cols] = dot_f32(left[:, rows], right, TN).astype(bf16)
             return 0
 
         lax.fori_loop(0, width // 256, body, 0)
 
-    def send_grad(cols, k):
+    def send_grad(cols, into, k):
         third = shard // 3
         copies = []
-        for p in range(1 if cols.size < q_cols else 3):
-            size = shard if cols.size < q_cols else third
+        for p in range(3):
             for i in range(3):
-                rows = pl.ds(pl.multiple_of(rel[i + 1] * shard + p * size, size), size)
+                rows = pl.ds(pl.multiple_of(rel[i + 1] * shard + p * third, third), third)
                 copies.append(
                     remote(
-                        ga.at[rows, cols],
-                        ra.at[i, pl.ds(p * size, size), cols],
+                        xy.at[rows, cols],
+                        ra.at[pl.ds(i * shard + p * third, third), into],
                         k + 3 * p + i,
                         plane[i],
                     )
@@ -1161,12 +1162,30 @@
         pending.extend(copies)
         return copies
 
-    weight_grad(dattn, mixed_ref[...], outs)
-    ga_copies = send_grad(outs, 34)
+    for copy in mo_out + gg_out:
+        copy.wait_recv()
+    moe = xy[group(f), :].astype(f32)
+    gates = gg_sum[rows_of(f, half), :]
+    for i in range(3):
+        moe = moe + mo_got[i].astype(f32)
+        gates = gates + gg_got[i]
+    layer_ref[my_rows, :] = (res_ref[...] + moe).astype(bf16)
+    gate_ref[my_rows, :] = gates
+    lo_swap = remote(layer_ref.at[my_rows], layer_ref.at[my_rows], 27, sibling)
+    gt_swap = remote(gate_ref.at[my_rows], gate_ref.at[my_rows], 28, sibling)
+    lo_swap.start()
+    gt_swap.start()
+    for copy in mo_out + [mo_swap]:
+        copy.wait_send()
+    go_on()
+
+    right_half = pl.ds(q_cols, q_cols)
+    weight_grad(dattn, mixed_ref[...], right_half)
+    ga_copies = send_grad(right_half, outs, 34)
     go_on()
     q_part = pl.ds(0, q_cols)
     weight_grad(xn_ref, dproj[:, q_part], q_part)
-    ga_copies += send_grad(q_part, 43)
+    ga_copies += send_grad(q_part, q_part, 43)
     go_on()
     for s in range(1, 4):
 
@@ -1178,14 +1197,29 @@
     kv_part = pl.ds(q_cols, 2 * HEAD_DIM)
     dproj[:, pl.ds(q_cols, HEAD_DIM)] = turn(dkv[0:count, key_cols], cosine, sine).astype(bf16)
     dproj[:, pl.ds(q_cols + HEAD_DIM, HEAD_DIM)] = dkv[0:count, val_cols].astype(bf16)
-    weight_grad(xn_ref, dproj[:, kv_part], kv_part)
-    ga_copies += send_grad(kv_part, 16)
+    for s in range(4):
+        block = dot_f32(xn_ref[:, pl.ds(s * shard, shard)], dproj[:, kv_part], TN)
+        xy[low_rows, pl.ds(s * 2 * HEAD_DIM, 2 * HEAD_DIM)] = block.astype(bf16)
+    kv_copies = [
+        remote(
+            xy.at[low_rows, rows_of(rel[i + 1], 2 * HEAD_DIM)],
+            ra.at[pl.ds(i * shard, shard), kv_part],
+            16 + i,
+            plane[i],
+        )
+        for i in range(3)
+    ]
+    pending.extend(kv_copies)
+    ga_copies += kv_copies
     go_on()
 
+    load_in.wait()
     for s in range(width // 256):
         rows = pl.ds(s * 256, 256)
-        d1[:, rows] = dot_f32(dproj[my_rows, :], wa[rows, ins], NT)
-        d1_low[:, rows] = dot_f32(dproj[rows_of(1 - c, half), :], wa[rows, ins], NT).astype(bf16)
+        d1[:, rows] = dot_f32(dproj[my_rows, :], wgu[rows, in_part], NT)
+        d1_low[:, rows] = dot_f32(
+            dproj[rows_of(1 - c, half), :], wgu[rows, in_part], NT
+        ).astype(bf16)
     d1_swap = remote(d1_low, d1_in, 25, sibling)
     d1_swap.start()
     go_on()
@@ -1202,21 +1236,6 @@
     tg_swap.start()
     go_on()
 
-    for copy in mo_out + gg_out:
-        copy.wait_recv()
-    moe = mo_own[f].astype(f32)
-    gates = gg_sum[f]
-    for i in range(3):
-        moe = moe + mo_got[i].astype(f32)
-        gates = gates + gg_got[i]
-    layer_ref[my_rows, :] = (res_ref[...] + moe).astype(bf16)
-    gate_ref[my_rows, :] = gates
-    lo_swap = remote(layer_ref.at[my_rows], layer_ref.at[my_rows], 27, sibling)
-    gt_swap = remote(gate_ref.at[my_rows], gate_ref.at[my_rows], 28, sibling)
-    lo_swap.start()
-    gt_swap.start()
-    go_on()
-
     stages = [sibling, at(fx), at(fy), partner, at(ctx=lax.rem(z + 2, 4))]
     gain_copies = [remote(gacc.at[i], gin.at[i], 29 + i, stages[i]) for i in range(5)]
     for i in range(5):
@@ -1241,10 +1260,18 @@
     def attn_sum(i, _):
         size = shard // 8
         here = pl.ds(pl.multiple_of(i * size, size), size)
-        total = ga[pl.ds(pl.multiple_of(f * shard + i * size, size), size), :].astype(f32)
-        for r in range(3):
-            total = total + ra[r, here, :].astype(f32)
-        ra[0, here, :] = total.astype(bf16)
+        rows = pl.ds(pl.multiple_of(f * shard + i * size, size), size)
+        low = pl.ds(pl.multiple_of(4 * shard + i * size, size), size)
+        for cols, mine in (
+            (q_part, xy[rows, q_part]),
+            (kv_part, xy[low, rows_of(f, 2 * HEAD_DIM)]),
+            (outs, xy[rows, right_half]),
+        ):
+            total = mine.astype(f32)
+            for r in range(3):
+                other = pl.ds(pl.multiple_of(r * shard + i * size, size), size)
+                total = total + ra[other, cols].astype(f32)
+            ra[here, cols] = total.astype(bf16)
         return 0
 
     lax.fori_loop(0, 8, attn_sum, 0)
@@ -1253,6 +1280,9 @@
     store = pltpu.make_async_copy(a1, attn_hbm, local.at[0])
     store.start()
 
+    for k in ready:
+        final(k).start()
+
     store.wait()
     for k in range(n_all):
 
@@ -1267,7 +1297,7 @@
             back(k).wait_send()
 
     for k in range(n_expert):
-        if k % 4 == 0:
+        if chunks[k][1] == 0:
             final(k).wait()
         else:
             final(k).wait_send()
@@ -1280,26 +1310,29 @@
 
     for copy in [tg_swap, lo_swap, gt_swap]:
         copy.wait_recv()
-    swaps = [dn_swap, gg_swap, mo_swap, da_swap, d1_swap, tg_swap, lo_swap, gt_swap]
-    for copy in swaps + dn_out + gg_out + mo_out + ga_copies + gain_copies:
+    swaps = [gg_swap, da_swap, d1_swap, tg_swap, lo_swap, gt_swap]
+    for copy in swaps + gg_out + ga_copies + gain_copies:
         copy.wait_send()
 
 
-def rear(tok, cot, res, xn, q, kv, mixed, gain_one, gain_two, ge, dn, mo, gg, wa):
+def rear(res, xn, q, kv, mixed, gain_one, gain_two, tok, cot, x, dy, weights, gate_table, wa):
     count, width = tok.shape
     half = count // 2
+    tokens = 8 * half
     columns = wa.shape[1]
     shard = width // 4
-    mats, _, hidden = ge.shape
+    own, _, _, hidden = weights.shape
+    mats = 3 * own
     q_cols = q.shape[1]
     vmem, hbm = pl.BlockSpec(memory_space=pltpu.VMEM), pl.BlockSpec(memory_space=pl.ANY)
     bf16, f32 = jnp.bfloat16, jnp.float32
     shape = jax.ShapeDtypeStruct
     dma = pltpu.SemaphoreType.DMA
-    n_all = 4 * mats + 8
+    chunks, attn_rows = ctx_chunks(mats, shard)
+    n_expert, n_all = len(chunks), len(chunks) + len(attn_rows)
     return pl.pallas_call(
         rear_kernel,
-        in_specs=[vmem] * 8 + [hbm] * 7,
+        in_specs=[vmem] * 8 + [hbm] * 5 + [vmem, hbm],
         out_specs=[vmem] * 4 + [hbm] * 2,
         out_shape=[
             shape((count, width), bf16),
@@ -1310,19 +1343,20 @@
             shape((4, mats, shard, hidden), bf16),
         ],
         scratch_shapes=[
+            pltpu.VMEM((2 * tokens, width), bf16),
+            pltpu.VMEM((width, 2 * own * hidden), bf16),
+            pltpu.VMEM((width, own * hidden), bf16),
+            pltpu.VMEM((tokens, width), bf16),
+            pltpu.VMEM((tokens, own * hidden), bf16),
+            pltpu.VMEM((tokens, 128), f32),
             pltpu.VMEM((mats, width, hidden), bf16),
             pltpu.VMEM((mats, width, hidden), bf16),
-            pltpu.VMEM((mats, width, hidden), bf16),
-            pltpu.VMEM((width, columns), bf16),
-            pltpu.VMEM((4, half, width), bf16),
-            pltpu.VMEM((4, half, width), bf16),
+            pltpu.VMEM((4 * half, width), bf16),
             pltpu.VMEM((3, half, width), bf16),
-            pltpu.VMEM((4, half, width), bf16),
-            pltpu.VMEM((4, half, width), bf16),
+            pltpu.VMEM((4 * half, width), bf16),
             pltpu.VMEM((3, half, width), bf16),
-            pltpu.VMEM((4, half, 128), f32),
-            pltpu.VMEM((4, half, 128), f32),
-            pltpu.VMEM((4, half, 128), f32),
+            pltpu.VMEM((4 * half, 128), f32),
+            pltpu.VMEM((4 * half, 128), f32),
             pltpu.VMEM((3, half, 128), f32),
             pltpu.VMEM((half, width), f32),
             pltpu.VMEM((count, width), bf16),
@@ -1334,9 +1368,7 @@
             pltpu.VMEM((half, width), f32),
             pltpu.VMEM((half, width), bf16),
             pltpu.VMEM((half, width), bf16),
-            pltpu.VMEM((width, columns), bf16),
-            pltpu.VMEM((3, shard, columns), bf16),
-            pltpu.VMEM((shard, columns), bf16),
+            pltpu.VMEM((3 * shard, columns), bf16),
             pltpu.VMEM((shard, columns), bf16),
             pltpu.VMEM((5, 8, width), f32),
             pltpu.VMEM((5, 8, width), f32),
@@ -1344,20 +1376,37 @@
             pltpu.VMEM((half, width), bf16),
             dma((52,)),
             dma((52,)),
-            dma((7,)),
+            dma((10,)),
             dma((n_all,)),
             dma((n_all,)),
             dma((n_all,)),
             dma((n_all,)),
             dma((n_all,)),
-            dma((4 * mats,)),
-            dma((4 * mats,)),
+            dma((n_expert,)),
+            dma((n_expert,)),
+            pltpu.SemaphoreType.REGULAR,
         ],
         compiler_params=pltpu.CompilerParams(
-            collective_id=1, has_side_effects=True, vmem_limit_bytes=62 * MIB
+            collective_id=1, has_side_effects=True, vmem_limit_bytes=63 * MIB
         ),
         name="rear",
-    )(res, xn, q, kv, mixed, gain_one, gain_two, frequencies(), tok, cot, ge, dn, mo, gg, wa)
+    )(
+        res,
+        xn,
+        q,
+        kv,
+        mixed,
+        gain_one,
+        gain_two,
+        frequencies(),
+        tok,
+        cot,
+        x,
+        dy,
+        weights,
+        gate_table,
+        wa,
+    )
 
 
 def body_fast(
@@ -1391,12 +1440,7 @@
         jnp.transpose(expert_weights, (0, 2, 1, 3)),
         cot,
     )
-    grads, d_normed, moe, gate_parts = moe_layer(
-        x.reshape(8 * half, model_width), dy.reshape(8 * half, model_width), whole_expert, gate_table
-    )
     layer_out, tokens_grad, gains, gate_rows, attn_grad, finals = rear(
-        tok,
-        cot,
         residual,
         normed,
         queries,
@@ -1404,20 +1448,23 @@
         mixed,
         gain_one,
         gain_two,
-        grads,
-        d_normed.reshape(2, 4, half, model_width),
-        moe.reshape(2, 4, half, model_width),
-        gate_parts.reshape(2, 4, half, 128),
+        tok,
+        cot,
+        x.reshape(8 * half, model_width),
+        dy.reshape(8 * half, model_width),
+        whole_expert,
+        gate_table,
         whole_attn,
     )
     picked = route_rows[:, :, None] == jnp.arange(EXPERTS, dtype=jnp.int32)
     gate_grad = jnp.sum(jnp.where(picked, gate_rows[:, None, :EXPERTS], 0.0), axis=-1)
     finals = finals.reshape(EXPERTS, 3, shard, hidden)
-    expert_grad = jnp.transpose(join_experts(finals, expert_order(f).T), (0, 2, 1, 3))
+    expert_grad, attn_lines = join_experts(finals, attn_grad, expert_order(f).T)
+    expert_grad = jnp.transpose(expert_grad, (0, 2, 1, 3))
     return (
         layer_out.reshape(sequence_count, block_len, model_width),
         tokens_grad.reshape(sequence_count, block_len, model_width),
-        attn_grad.astype(jnp.float32)[:, None, :],
+        attn_lines.reshape(shard, 1, attention_params.shape[2]),
         expert_grad,
         gains[0],
         gains[1],

time: 421 us -> 391 us (0.929)
  local copies, waits for them, and re-layouts: 23.1 us -> 5.93 us
  Pallas kernels: 395 us -> 383 us
    pallas_call x2 -> x1, Pallas kernels: 261 us -> 242 us  [rear(): pl.pallas_call(rear_kernel, in_specs=[vmem] * 8 + [hbm] * 5 + [vmem, hbm]...]
    unnamed x45 -> x10, local copies, waits for them, and re-layouts: 20.1 us -> 1.78 us
where the time goes in v6:
time: 391 us
  Pallas kernels  383 us (98%)
  local copies, waits for them, and re-layouts  5.93 us (2%)
    pallas_call x1, Pallas kernels, rear(): pl.pallas_call(rear_kernel, in_specs=[vmem] * 8 + [hbm] * 5 + [vmem, hbm]...  242 us
    pallas_call x1, Pallas kernels, front(): pl.pallas_call(front_kernel, in_specs=[vmem] * 7 + [hbm] * 3, out_specs=[...  131 us
    pallas_call x1, Pallas kernels, join_experts(): pl.pallas_call(join_kernel, grid=(rows // step,), in_specs=[pl.BlockSpec(...  10.6 us

profile of v6, /device:TPU:0, one launch (start us, length us, event | category | flops | bytes accessed | tf_op | source)
XLA Modules:
  0.0 390.8 jit_solution(12247398875283538772)
XLA Ops:
  0.6 1.3 broadcast_in_dim.22.gain_one_ref
  1.9 1.3 broadcast_in_dim.23.gain_two_ref
  3.2 130.7 %front.1 = (bf16[256,1536]{1,0:T(8,128)(2,1)}, bf16[256,768]{1,0:T(8,128)(2,1)}, bf16[4,256,256]{2,1,0:T(8,128)(2,1)}, bf16[256,768]{1,0:T(8,128)(2,1)}, f32[128...) custom-call(bf16[256,1536]{1,0:T(8,128)(2,1)} %bitcast.23, ...), custom_call_target="tpu_custom_call" | custom-call | tf_op jit(solution)/shard_map/front/pallas_call | solution.py:701
  133.9 241.6 %rear.1 = (bf16[256,1536]{1,0:T(8,128)(2,1)}, bf16[256,1536]{1,0:T(8,128)(2,1)}, f32[8,1536]{1,0:T(8,128)}, f32[256,128]{1,0:T(8,128)}, bf16[384,1792]{1,0:T(8,128)(2,1)}, /*index=5*/bf16[4,6,384,384]{3,2,1,0:T(8,128)(2,1)}) custom-call(f32[128,1536]{1,0:T(8,128)} %get-tuple-element.25.res_ref, bf16[256,1536]{1,0:T(8,128)(2,1)} %get-tuple-element.26.xn_ref, ...), custom_call_target="tpu_custom_call" | custom-call | tf_op jit(solution)/shard_map/rear/pallas_call | solution.py:1333
  375.5 0.0 copy-start.2
  375.5 0.0 copy-start.3
  375.5 0.0 copy-start.1
  375.5 0.0 copy-start
  375.6 0.6 fusion.order_ref
  376.2 10.6 %join_experts.1 = (f32[384,3,8,384]{3,2,1,0:T(8,128)}, f32[5376,128]{1,0:T(8,128)}) custom-call(bf16[128,128]{1,0:T(8,128)(2,1)} %fusion.order_ref, bf16[8,3,384,384]{3,2,1,0:T(8,128)(2,1)} %bitcast.20, bf16[384,1792]{1,0:T(8,128)(2,1)} %get-tuple-element.38.attn_in_ref), custom_call_target="tpu_custom_call" | custom-call | tf_op jit(solution)/shard_map/join_experts/pallas_call | solution.py:349
  386.8 1.5 slice_reduce_fusion
  388.3 0.0 copy-done.2
  388.3 0.1 copy.20
  388.4 0.0 copy-done.3
  388.4 0.6 select_reduce_fusion
  389.0 0.0 copy-done.1
  389.0 0.9 copy.24
  389.9 0.0 copy-done
  389.9 0.9 copy.25
  (1 shorter events, 0.0 us)
Async XLA Ops:
  375.5 12.8 %copy-start.2 = (f32[256,128]{1,0:T(8,128)S(1)}, f32[256,128]{1,0:T(8,128)}, u32[]{:S(2)}) copy-start(f32[256,128]{1,0:T(8,128)} %get-tuple-element.42) | copy-start | bytes 393220
  375.5 12.9 %copy-start.3 = (s32[1,256,4]{1,2,0:T(4,128)S(1)}, s32[1,256,4]{1,2,0:T(4,128)}, u32[]{:S(2)}) copy-start(s32[1,256,4]{1,2,0:T(4,128)} %param.17) | copy-start | bytes 12292
  375.5 13.5 %copy-start.1 = (bf16[256,1536]{1,0:T(8,128)(2,1)S(1)}, bf16[256,1536]{1,0:T(8,128)(2,1)}, u32[]{:S(2)}) copy-start(bf16[256,1536]{1,0:T(8,128)(2,1)} %get-tuple-element.35) | copy-start | bytes 2359300
  375.5 14.4 %copy-start = (bf16[256,1536]{1,0:T(8,128)(2,1)S(1)}, bf16[256,1536]{1,0:T(8,128)(2,1)}, u32[]{:S(2)}) copy-start(bf16[256,1536]{1,0:T(8,128)(2,1)} %get-tuple-element.36) | copy-start | bytes 2359300

commit v7 on v6

--- a/solution.py
+++ b/solution.py
@@ -344,7 +344,7 @@
 def join_experts(grads, attn_grad, order):
     experts, _, rows, width = grads.shape
     columns = attn_grad.shape[1]
-    step = 64
+    step = 128
     lines = step * columns // 128
     return pl.pallas_call(
         join_kernel,
@@ -574,6 +574,11 @@
     out_x.start()
     out_y.start()
     handed = hand_on(0, 0) + hand_on(0, 1)
+    dy_copies = [
+        remote(cot_hbm.at[rows_of(c, half)], dy_hbm.at[c, f], 23 + i, plane[i]) for i in range(2)
+    ]
+    for copy in dy_copies:
+        copy.start()
     split(2)
     own_w = pltpu.make_async_copy(pieces.at[pl.ds(0, 2)], w_hbm.at[:, :, mine, :], local.at[1])
     own_w.start()
@@ -620,11 +625,6 @@
     ]
     for copy in w_copies:
         copy.start()
-    dy_copies = [
-        remote(cot_hbm.at[rows_of(c, half)], dy_hbm.at[c, f], 23 + i, plane[i]) for i in range(3)
-    ]
-    for copy in dy_copies:
-        copy.start()
     for i in range(3):
         handed += hand_on(1, i)
 
@@ -640,6 +640,19 @@
         cols = pl.ds(g * HEAD_DIM, HEAD_DIM)
         probs = block_probs(z, keys, q_ref[:, cols]).astype(jnp.bfloat16)
         mixed_ref[:, cols] = dot_f32(probs, vals, TN).astype(jnp.bfloat16)
+
+    upper, lower = pl.ds(0, half // 2), pl.ds(half // 2, half // 2)
+
+    def pass_on(copies, ref, k):
+        copies[0].wait_recv()
+        up = ref.at[c, fx, upper]
+        passed = [remote(up, up, k, at(fy))]
+        passed[0].start()
+        copies[1].wait_recv()
+        low = ref.at[c, fy, lower]
+        passed.append(remote(low, low, k + 1, at(fx)))
+        passed[1].start()
+        return passed
 
     out_xy.wait_recv()
     out_yx.wait_recv()
@@ -658,21 +671,28 @@
     low_half[...] = (residual * inv * gain_two_ref[...]).astype(jnp.bfloat16)
     own_x = pltpu.make_async_copy(low_half, x_hbm.at[c, f], local.at[5])
     own_x.start()
-    x_copies = [remote(low_half, x_hbm.at[c, f], 27 + i, plane[i]) for i in range(3)]
+    x_copies = [remote(low_half, x_hbm.at[c, f], 27 + i, plane[i]) for i in range(2)]
     for copy in x_copies:
         copy.start()
     sib_x = [remote(low_half, x_hbm.at[c, f], 30, sibling)]
     sib_x[0].start()
 
+    dy_passed = pass_on(dy_copies, dy_hbm, 61)
+    x_passed = pass_on(x_copies, x_hbm, 63)
     sib_dy = []
-    for i in range(3):
-        dy_copies[i].wait_recv()
+    for i in range(2):
         sib_dy.append(remote(dy_hbm.at[c, rel[i]], dy_hbm.at[c, rel[i]], 31 + i, sibling))
+        sib_x.append(remote(x_hbm.at[c, rel[i]], x_hbm.at[c, rel[i]], 34 + i, sibling))
         sib_dy[i].start()
-    for i in range(3):
-        x_copies[i].wait_recv()
-        sib_x.append(remote(x_hbm.at[c, rel[i]], x_hbm.at[c, rel[i]], 34 + i, sibling))
         sib_x[i + 1].start()
+    for copy in dy_passed:
+        copy.wait_recv()
+    sib_dy.append(remote(dy_hbm.at[c, fd], dy_hbm.at[c, fd], 33, sibling))
+    sib_dy[2].start()
+    for copy in x_passed:
+        copy.wait_recv()
+    sib_x.append(remote(x_hbm.at[c, fd], x_hbm.at[c, fd], 36, sibling))
+    sib_x[3].start()
 
     for copy in w_copies + gate_copies + handed + sib_dy + sib_x:
         copy.wait_recv()
@@ -684,7 +704,8 @@
 
     for copy in [in_x, in_y, in_xy, in_yx, out_x, out_y, out_xy, out_yx, swap]:
         copy.wait_send()
-    for copy in w_copies + quarters + handed + gate_copies + dy_copies + x_copies + sib_dy + sib_x:
+    sent = w_copies + quarters + handed + gate_copies + dy_copies + x_copies
+    for copy in sent + dy_passed + x_passed + sib_dy + sib_x:
         copy.wait_send()
     for copy in [own_w, own_x, store_wa] + own_dy:
         copy.wait()
@@ -721,8 +742,8 @@
             pltpu.VMEM((count, width), f32),
             pltpu.VMEM((half, width), f32),
             pltpu.VMEM((half, width), bf16),
-            pltpu.SemaphoreType.DMA((61,)),
-            pltpu.SemaphoreType.DMA((61,)),
+            pltpu.SemaphoreType.DMA((65,)),
+            pltpu.SemaphoreType.DMA((65,)),
             pltpu.SemaphoreType.DMA((7,)),
         ],
         compiler_params=pltpu.CompilerParams(
@@ -964,7 +985,7 @@
 
     pending, ready = [], []
     pace = 2
-    lag_a, lag_b, lag_c, window = 1, 3, 6, 3
+    lag_a, lag_b, lag_c, window = 1, 2, 5, 3
 
     def z_step(i):
         if i < n_all:

time: 391 us -> 378 us (0.967)
  Pallas kernels: 383 us -> 370 us
    pallas_call x1, Pallas kernels: 131 us -> 121 us  [front(): pl.pallas_call(front_kernel, in_specs=[vmem] * 7 + [hbm] * 3, out_specs=[...]
where the time goes in v7:
time: 378 us
  Pallas kernels  370 us (98%)
  local copies, waits for them, and re-layouts  5.93 us (2%)
    pallas_call x1, Pallas kernels, rear(): pl.pallas_call(rear_kernel, in_specs=[vmem] * 8 + [hbm] * 5 + [vmem, hbm]...  240 us
    pallas_call x1, Pallas kernels, front(): pl.pallas_call(front_kernel, in_specs=[vmem] * 7 + [hbm] * 3, out_specs=[...  121 us
    pallas_call x1, Pallas kernels, join_experts(): pl.pallas_call(join_kernel, grid=(rows // step,), in_specs=[pl.BlockSpec(...  9.64 us

profile of v7, /device:TPU:0, one launch (start us, length us, event | category | flops | bytes accessed | tf_op | source)
XLA Modules:
  0.0 378.1 jit_solution(1931548334902456341)
XLA Ops:
  0.6 1.3 broadcast_in_dim.22.gain_one_ref
  1.9 1.3 broadcast_in_dim.23.gain_two_ref
  3.2 120.9 %front.1 = (bf16[256,1536]{1,0:T(8,128)(2,1)}, bf16[256,768]{1,0:T(8,128)(2,1)}, bf16[4,256,256]{2,1,0:T(8,128)(2,1)}, bf16[256,768]{1,0:T(8,128)(2,1)}, f32[128...) custom-call(bf16[256,1536]{1,0:T(8,128)(2,1)} %bitcast.23, ...), custom_call_target="tpu_custom_call" | custom-call | tf_op jit(solution)/shard_map/front/pallas_call | solution.py:722
  124.1 239.7 %rear.1 = (bf16[256,1536]{1,0:T(8,128)(2,1)}, bf16[256,1536]{1,0:T(8,128)(2,1)}, f32[8,1536]{1,0:T(8,128)}, f32[256,128]{1,0:T(8,128)}, bf16[384,1792]{1,0:T(8,128)(2,1)}, /*index=5*/bf16[4,6,384,384]{3,2,1,0:T(8,128)(2,1)}) custom-call(f32[128,1536]{1,0:T(8,128)} %get-tuple-element.25.res_ref, bf16[256,1536]{1,0:T(8,128)(2,1)} %get-tuple-element.26.xn_ref, ...), custom_call_target="tpu_custom_call" | custom-call | tf_op jit(solution)/shard_map/rear/pallas_call | solution.py:1354
  363.8 0.0 copy-start.2
  363.8 0.0 copy-start.3
  363.8 0.0 copy-start.1
  363.8 0.0 copy-start
  363.9 0.6 fusion.order_ref
  364.5 9.6 %join_experts.1 = (f32[384,3,8,384]{3,2,1,0:T(8,128)}, f32[5376,128]{1,0:T(8,128)}) custom-call(bf16[128,128]{1,0:T(8,128)(2,1)} %fusion.order_ref, bf16[8,3,384,384]{3,2,1,0:T(8,128)(2,1)} %bitcast.20, bf16[384,1792]{1,0:T(8,128)(2,1)} %get-tuple-element.38.attn_in_ref), custom_call_target="tpu_custom_call" | custom-call | tf_op jit(solution)/shard_map/join_experts/pallas_call | solution.py:349
  374.1 1.5 slice_reduce_fusion
  375.6 0.0 copy-done.2
  375.6 0.1 copy.20
  375.7 0.0 copy-done.3
  375.7 0.6 select_reduce_fusion
  376.3 0.0 copy-done.1
  376.3 0.9 copy.24
  377.2 0.0 copy-done
  377.2 0.9 copy.25
  (1 shorter events, 0.0 us)
Async XLA Ops:
  363.8 11.8 %copy-start.2 = (f32[256,128]{1,0:T(8,128)S(1)}, f32[256,128]{1,0:T(8,128)}, u32[]{:S(2)}) copy-start(f32[256,128]{1,0:T(8,128)} %get-tuple-element.42) | copy-start | bytes 393220
  363.8 11.9 %copy-start.3 = (s32[1,256,4]{1,2,0:T(4,128)S(1)}, s32[1,256,4]{1,2,0:T(4,128)}, u32[]{:S(2)}) copy-start(s32[1,256,4]{1,2,0:T(4,128)} %param.17) | copy-start | bytes 12292
  363.8 12.5 %copy-start.1 = (bf16[256,1536]{1,0:T(8,128)(2,1)S(1)}, bf16[256,1536]{1,0:T(8,128)(2,1)}, u32[]{:S(2)}) copy-start(bf16[256,1536]{1,0:T(8,128)(2,1)} %get-tuple-element.35) | copy-start | bytes 2359300
  363.8 13.4 %copy-start = (bf16[256,1536]{1,0:T(8,128)(2,1)S(1)}, bf16[256,1536]{1,0:T(8,128)(2,1)}, u32[]{:S(2)}) copy-start(bf16[256,1536]{1,0:T(8,128)(2,1)} %get-tuple-element.36) | copy-start | bytes 2359300

commit v8 on v7

--- a/solution.py
+++ b/solution.py
@@ -414,8 +414,7 @@
 
 def front_kernel(
     tok_ref,
-    gain_one_ref,
-    gain_two_ref,
+    gain_ref,
     freq_ref,
     routes_ref,
     gates_ref,
@@ -551,7 +550,7 @@
 
     tok = tok_ref[...].astype(jnp.float32)
     inv = lax.rsqrt(jnp.mean(tok * tok, axis=-1, keepdims=True) + eps)
-    xn_ref[...] = (tok * inv * gain_one_ref[...]).astype(jnp.bfloat16)
+    xn_ref[...] = (tok * inv * gain_ref[0:1, :]).astype(jnp.bfloat16)
     position = z * count + lax.broadcasted_iota(jnp.int32, (count, HEAD_DIM), 0)
     angle = position.astype(jnp.float32) * freq_ref[...]
     cosine = jnp.cos(angle)
@@ -573,7 +572,7 @@
         copy.start()
     out_x.start()
     out_y.start()
-    handed = hand_on(0, 0) + hand_on(0, 1)
+    handed = hand_on(0, 0)
     dy_copies = [
         remote(cot_hbm.at[rows_of(c, half)], dy_hbm.at[c, f], 23 + i, plane[i]) for i in range(2)
     ]
@@ -611,7 +610,7 @@
         def _(s=s):
             kv_ref[s] = jnp.zeros(kv_ref.shape[1:], jnp.bfloat16)
 
-    handed += hand_on(0, 2)
+    handed += hand_on(0, 1) + hand_on(0, 2)
     out_x.wait_recv()
     out_xy = remote(wa.at[top, outs], wa.at[top, outs], 12, at(fy))
     out_xy.start()
@@ -668,7 +667,7 @@
     residual = tok_ref[my_rows, :].astype(jnp.float32) + (part[my_rows, :] + part_in[...])
     res_ref[...] = residual
     inv = lax.rsqrt(jnp.mean(residual * residual, axis=-1, keepdims=True) + eps)
-    low_half[...] = (residual * inv * gain_two_ref[...]).astype(jnp.bfloat16)
+    low_half[...] = (residual * inv * gain_ref[1:2, :]).astype(jnp.bfloat16)
     own_x = pltpu.make_async_copy(low_half, x_hbm.at[c, f], local.at[5])
     own_x.start()
     x_copies = [remote(low_half, x_hbm.at[c, f], 27 + i, plane[i]) for i in range(2)]
@@ -711,7 +710,7 @@
         copy.wait()
 
 
-def front(tok, gain_one, gain_two, routes, gates, order, attn_own, weights, cot):
+def front(tok, gains, routes, gates, order, attn_own, weights, cot):
     count, width = tok.shape
     half = count // 2
     shard, columns = attn_own.shape
@@ -721,7 +720,7 @@
     shape = jax.ShapeDtypeStruct
     return pl.pallas_call(
         front_kernel,
-        in_specs=[vmem] * 7 + [hbm] * 3,
+        in_specs=[vmem] * 6 + [hbm] * 3,
         out_specs=[vmem] * 6 + [hbm] * 4,
         out_shape=[
             shape((count, width), bf16),
@@ -750,7 +749,7 @@
             collective_id=0, has_side_effects=True, vmem_limit_bytes=60 * MIB
         ),
         name="front",
-    )(tok, gain_one, gain_two, frequencies(), routes, gates, order, attn_own, weights, cot)
+    )(tok, gains, frequencies(), routes, gates, order, attn_own, weights, cot)
 
 
 def ctx_chunks(mats, shard):
@@ -766,8 +765,7 @@
     q_ref,
     kv_ref,
     mixed_ref,
-    gain_one_ref,
-    gain_two_ref,
+    gain_ref,
     freq_ref,
     tok_hbm,
     cot_hbm,
@@ -885,7 +883,7 @@
         rows = wl_ref[b % 4, :, pl.ds((b // 4) * half, half)]
         rows = jnp.concatenate([rows, jnp.zeros((128 - EXPERTS, half), f32)], axis=0)
         table[pl.ds(b * half, half), :] = rows.T
-    for copy in loads:
+    for copy in loads[:5]:
         copy.wait()
 
     lanes = lax.broadcasted_iota(jnp.int32, (tile, 128), 1)
@@ -893,6 +891,12 @@
     def act_step(i, _):
         rows = pl.ds(pl.multiple_of(i * tile, tile), tile)
         acts = dot_f32(xy[rows, :], wgu[...])
+
+        @pl.when(i == 0)
+        def _():
+            for copy in loads[5:]:
+                copy.wait()
+
         plain = dot_f32(xy[pl.ds(pl.multiple_of(tokens + i * tile, tile), tile), :], wd[...])
         scales = table[rows, :]
         sums = jnp.zeros((tile, 128), f32)
@@ -1103,7 +1107,7 @@
         d_two = d_two + dn_got[i].astype(f32)
     residual = res_ref[...]
     inv = lax.rsqrt(jnp.mean(residual * residual, axis=-1, keepdims=True) + eps)
-    scaled = d_two * gain_two_ref[...]
+    scaled = d_two * gain_ref[1:2, :]
     inside = jnp.mean(scaled * residual, axis=-1, keepdims=True)
     d_norm = inv * scaled - residual * (inv * inv * inv * inside)
     gacc[0] = jnp.zeros(gacc.shape[1:], f32)
@@ -1248,7 +1252,7 @@
     d_one = d1[...] + d1_in[...].astype(f32)
     tok = tok_half[...].astype(f32)
     inv = lax.rsqrt(jnp.mean(tok * tok, axis=-1, keepdims=True) + eps)
-    scaled = d_one * gain_one_ref[...]
+    scaled = d_one * gain_ref[0:1, :]
     inside = jnp.mean(scaled * tok, axis=-1, keepdims=True)
     d_norm = inv * scaled - tok * (inv * inv * inv * inside)
     gacc[0, 0:1, :] = jnp.sum(d_one * tok * inv, axis=0, keepdims=True)
@@ -1336,7 +1340,7 @@
         copy.wait_send()
 
 
-def rear(res, xn, q, kv, mixed, gain_one, gain_two, tok, cot, x, dy, weights, gate_table, wa):
+def rear(res, xn, q, kv, mixed, gains, tok, cot, x, dy, weights, gate_table, wa):
     count, width = tok.shape
     half = count // 2
     tokens = 8 * half
@@ -1353,7 +1357,7 @@
     n_expert, n_all = len(chunks), len(chunks) + len(attn_rows)
     return pl.pallas_call(
         rear_kernel,
-        in_specs=[vmem] * 8 + [hbm] * 5 + [vmem, hbm],
+        in_specs=[vmem] * 7 + [hbm] * 5 + [vmem, hbm],
         out_specs=[vmem] * 4 + [hbm] * 2,
         out_shape=[
             shape((count, width), bf16),
@@ -1417,8 +1421,7 @@
         q,
         kv,
         mixed,
-        gain_one,
-        gain_two,
+        gains,
         frequencies(),
         tok,
         cot,
@@ -1448,12 +1451,11 @@
     shard, hidden = attention_params.shape[0], expert_weights.shape[3]
     tok = tokens.reshape(count, model_width)
     cot = cotangent.reshape(count, model_width)
-    gain_one, gain_two = attn_norm[None, :], ffn_norm[None, :]
+    norm_gains = jnp.stack([attn_norm, ffn_norm])
     route_rows = routes.reshape(count, TOP)
     normed, queries, kv, mixed, residual, gate_table, whole_attn, whole_expert, x, dy = front(
         tok,
-        gain_one,
-        gain_two,
+        norm_gains,
         route_rows.T,
         gate_values.reshape(count, TOP).T,
         slot_order.reshape(1, count),
@@ -1467,8 +1469,7 @@
         queries,
         kv,
         mixed,
-        gain_one,
-        gain_two,
+        norm_gains,
         tok,
         cot,
         x.reshape(8 * half, model_width),

time: 378 us -> 378 us (level)
  no operation moved by 1% of the time
where the time goes in v8:
time: 378 us
  Pallas kernels  371 us (98%)
  local copies, waits for them, and re-layouts  4.75 us (1%)
    pallas_call x1, Pallas kernels, rear(): pl.pallas_call(rear_kernel, in_specs=[vmem] * 7 + [hbm] * 5 + [vmem, hbm]...  240 us
    pallas_call x1, Pallas kernels, front(): pl.pallas_call(front_kernel, in_specs=[vmem] * 6 + [hbm] * 3, out_specs=[...  121 us
    pallas_call x1, Pallas kernels, join_experts(): pl.pallas_call(join_kernel, grid=(rows // step,), in_specs=[pl.BlockSpec(...  9.64 us

profile of v8, /device:TPU:0, one launch (start us, length us, event | category | flops | bytes accessed | tf_op | source)
XLA Modules:
  0.0 378.1 jit_solution(3050777542778457106)
XLA Ops:
  0.6 0.7 stack.10
  1.3 0.7 stack.9
  2.0 0.6 pad_maximum_fusion.gain_ref
  2.6 120.9 %front.1 = (bf16[256,1536]{1,0:T(8,128)(2,1)}, bf16[256,768]{1,0:T(8,128)(2,1)}, bf16[4,256,256]{2,1,0:T(8,128)(2,1)}, bf16[256,768]{1,0:T(8,128)(2,1)}, f32[128...) custom-call(bf16[256,1536]{1,0:T(8,128)(2,1)} %bitcast.23, ...), custom_call_target="tpu_custom_call" | custom-call | tf_op jit(solution)/shard_map/front/pallas_call | solution.py:721
  123.5 240.2 %rear.1 = (bf16[256,1536]{1,0:T(8,128)(2,1)}, bf16[256,1536]{1,0:T(8,128)(2,1)}, f32[8,1536]{1,0:T(8,128)}, f32[256,128]{1,0:T(8,128)}, bf16[384,1792]{1,0:T(8,128)(2,1)}, /*index=5*/bf16[4,6,384,384]{3,2,1,0:T(8,128)(2,1)}) custom-call(f32[128,1536]{1,0:T(8,128)} %get-tuple-element.25.res_ref, bf16[256,1536]{1,0:T(8,128)(2,1)} %get-tuple-element.26.xn_ref, ...), custom_call_target="tpu_custom_call" | custom-call | tf_op jit(solution)/shard_map/rear/pallas_call | solution.py:1358
  363.8 0.0 copy-start.2
  363.8 0.0 copy-start.3
  363.8 0.0 copy-start.1
  363.8 0.0 copy-start
  363.8 0.6 fusion.order_ref
  364.5 9.6 %join_experts.1 = (f32[384,3,8,384]{3,2,1,0:T(8,128)}, f32[5376,128]{1,0:T(8,128)}) custom-call(bf16[128,128]{1,0:T(8,128)(2,1)} %fusion.order_ref, bf16[8,3,384,384]{3,2,1,0:T(8,128)(2,1)} %bitcast.20, bf16[384,1792]{1,0:T(8,128)(2,1)} %get-tuple-element.38.attn_in_ref), custom_call_target="tpu_custom_call" | custom-call | tf_op jit(solution)/shard_map/join_experts/pallas_call | solution.py:349
  374.1 1.5 slice_reduce_fusion
  375.6 0.0 copy-done.2
  375.6 0.1 copy.20
  375.7 0.0 copy-done.3
  375.7 0.6 select_reduce_fusion
  376.3 0.0 copy-done.1
  376.3 0.9 copy.24
  377.2 0.0 copy-done
  377.2 0.9 copy.25
  (1 shorter events, 0.0 us)
Async XLA Ops:
  363.8 11.8 %copy-start.2 = (f32[256,128]{1,0:T(8,128)S(1)}, f32[256,128]{1,0:T(8,128)}, u32[]{:S(2)}) copy-start(f32[256,128]{1,0:T(8,128)} %get-tuple-element.42) | copy-start | bytes 393220
  363.8 11.9 %copy-start.3 = (s32[1,256,4]{1,2,0:T(4,128)S(1)}, s32[1,256,4]{1,2,0:T(4,128)}, u32[]{:S(2)}) copy-start(s32[1,256,4]{1,2,0:T(4,128)} %param.17) | copy-start | bytes 12292
  363.8 12.5 %copy-start.1 = (bf16[256,1536]{1,0:T(8,128)(2,1)S(1)}, bf16[256,1536]{1,0:T(8,128)(2,1)}, u32[]{:S(2)}) copy-start(bf16[256,1536]{1,0:T(8,128)(2,1)} %get-tuple-element.35) | copy-start | bytes 2359300
  363.8 13.4 %copy-start = (bf16[256,1536]{1,0:T(8,128)(2,1)S(1)}, bf16[256,1536]{1,0:T(8,128)(2,1)}, u32[]{:S(2)}) copy-start(bf16[256,1536]{1,0:T(8,128)(2,1)} %get-tuple-element.36) | copy-start | bytes 2359300

commit v9 on v8

--- a/solution.py
+++ b/solution.py
@@ -572,7 +572,7 @@
         copy.start()
     out_x.start()
     out_y.start()
-    handed = hand_on(0, 0)
+    handed = hand_on(0, 0) + hand_on(0, 1)
     dy_copies = [
         remote(cot_hbm.at[rows_of(c, half)], dy_hbm.at[c, f], 23 + i, plane[i]) for i in range(2)
     ]
@@ -610,7 +610,7 @@
         def _(s=s):
             kv_ref[s] = jnp.zeros(kv_ref.shape[1:], jnp.bfloat16)
 
-    handed += hand_on(0, 1) + hand_on(0, 2)
+    handed += hand_on(0, 2)
     out_x.wait_recv()
     out_xy = remote(wa.at[top, outs], wa.at[top, outs], 12, at(fy))
     out_xy.start()
@@ -883,7 +883,7 @@
         rows = wl_ref[b % 4, :, pl.ds((b // 4) * half, half)]
         rows = jnp.concatenate([rows, jnp.zeros((128 - EXPERTS, half), f32)], axis=0)
         table[pl.ds(b * half, half), :] = rows.T
-    for copy in loads[:5]:
+    for copy in loads:
         copy.wait()
 
     lanes = lax.broadcasted_iota(jnp.int32, (tile, 128), 1)
@@ -891,12 +891,6 @@
     def act_step(i, _):
         rows = pl.ds(pl.multiple_of(i * tile, tile), tile)
         acts = dot_f32(xy[rows, :], wgu[...])
-
-        @pl.when(i == 0)
-        def _():
-            for copy in loads[5:]:
-                copy.wait()
-
         plain = dot_f32(xy[pl.ds(pl.multiple_of(tokens + i * tile, tile), tile), :], wd[...])
         scales = table[rows, :]
         sums = jnp.zeros((tile, 128), f32)

time: 378 us -> 378 us (level)
  no operation moved by 1% of the time
where the time goes in v9:
time: 378 us; the launch traced here: 377 us
  Pallas kernels  370 us (98%)
  local copies, waits for them, and re-layouts  4.75 us (1%)
    pallas_call x1, Pallas kernels, rear(): pl.pallas_call(rear_kernel, in_specs=[vmem] * 7 + [hbm] * 5 + [vmem, hbm]...  240 us
    pallas_call x1, Pallas kernels, front(): pl.pallas_call(front_kernel, in_specs=[vmem] * 6 + [hbm] * 3, out_specs=[...  121 us
    pallas_call x1, Pallas kernels, join_experts(): pl.pallas_call(join_kernel, grid=(rows // step,), in_specs=[pl.BlockSpec(...  9.64 us

profile of v9, /device:TPU:0, one launch (start us, length us, event | category | flops | bytes accessed | tf_op | source)
XLA Modules:
  0.0 377.5 jit_solution(5021335934693874617)
XLA Ops:
  0.6 0.7 stack.10
  1.3 0.7 stack.9
  2.0 0.6 pad_maximum_fusion.gain_ref
  2.6 120.9 %front.1 = (bf16[256,1536]{1,0:T(8,128)(2,1)}, bf16[256,768]{1,0:T(8,128)(2,1)}, bf16[4,256,256]{2,1,0:T(8,128)(2,1)}, bf16[256,768]{1,0:T(8,128)(2,1)}, f32[128...) custom-call(bf16[256,1536]{1,0:T(8,128)(2,1)} %bitcast.23, ...), custom_call_target="tpu_custom_call" | custom-call | tf_op jit(solution)/shard_map/front/pallas_call | solution.py:721
  123.5 239.7 %rear.1 = (bf16[256,1536]{1,0:T(8,128)(2,1)}, bf16[256,1536]{1,0:T(8,128)(2,1)}, f32[8,1536]{1,0:T(8,128)}, f32[256,128]{1,0:T(8,128)}, bf16[384,1792]{1,0:T(8,128)(2,1)}, /*index=5*/bf16[4,6,384,384]{3,2,1,0:T(8,128)(2,1)}) custom-call(f32[128,1536]{1,0:T(8,128)} %get-tuple-element.25.res_ref, bf16[256,1536]{1,0:T(8,128)(2,1)} %get-tuple-element.26.xn_ref, ...), custom_call_target="tpu_custom_call" | custom-call | tf_op jit(solution)/shard_map/rear/pallas_call | solution.py:1352
  363.2 0.0 copy-start.2
  363.2 0.0 copy-start.3
  363.2 0.0 copy-start.1
  363.2 0.0 copy-start
  363.2 0.6 fusion.order_ref
  363.9 9.6 %join_experts.1 = (f32[384,3,8,384]{3,2,1,0:T(8,128)}, f32[5376,128]{1,0:T(8,128)}) custom-call(bf16[128,128]{1,0:T(8,128)(2,1)} %fusion.order_ref, bf16[8,3,384,384]{3,2,1,0:T(8,128)(2,1)} %bitcast.20, bf16[384,1792]{1,0:T(8,128)(2,1)} %get-tuple-element.38.attn_in_ref), custom_call_target="tpu_custom_call" | custom-call | tf_op jit(solution)/shard_map/join_experts/pallas_call | solution.py:349
  373.5 1.5 slice_reduce_fusion
  375.0 0.0 copy-done.2
  375.0 0.1 copy.20
  375.1 0.0 copy-done.3
  375.1 0.6 select_reduce_fusion
  375.7 0.0 copy-done.1
  375.7 0.9 copy.24
  376.6 0.0 copy-done
  376.6 0.9 copy.25
  (1 shorter events, 0.0 us)
Async XLA Ops:
  363.2 11.8 %copy-start.2 = (f32[256,128]{1,0:T(8,128)S(1)}, f32[256,128]{1,0:T(8,128)}, u32[]{:S(2)}) copy-start(f32[256,128]{1,0:T(8,128)} %get-tuple-element.42) | copy-start | bytes 393220
  363.2 11.9 %copy-start.3 = (s32[1,256,4]{1,2,0:T(4,128)S(1)}, s32[1,256,4]{1,2,0:T(4,128)}, u32[]{:S(2)}) copy-start(s32[1,256,4]{1,2,0:T(4,128)} %param.17) | copy-start | bytes 12292
  363.2 12.5 %copy-start.1 = (bf16[256,1536]{1,0:T(8,128)(2,1)S(1)}, bf16[256,1536]{1,0:T(8,128)(2,1)}, u32[]{:S(2)}) copy-start(bf16[256,1536]{1,0:T(8,128)(2,1)} %get-tuple-element.35) | copy-start | bytes 2359300
  363.2 13.4 %copy-start = (bf16[256,1536]{1,0:T(8,128)(2,1)S(1)}, bf16[256,1536]{1,0:T(8,128)(2,1)}, u32[]{:S(2)}) copy-start(bf16[256,1536]{1,0:T(8,128)(2,1)} %get-tuple-element.36) | copy-start | bytes 2359300
